TPU v7x, 32 devices: a whole 2x2x4 slice. The times are simulated.
32 devices in a mesh: dom: 8 (over z, y), grp: 4 (over x, core).
Axes of the slice: x: 2, y: 2, z: 4, core: 2. Of those that a mesh axis runs over, the one named last changes fastest.
Arguments:
- a_strips: bfloat16 [1024, 64, 448], P(('dom', 'grp')), may hold values from -0.25 to 0.25
- p_strips: bfloat16 [1024, 64, 256], P(('dom', 'grp')), may hold values from -1.1953125 to 1.1953125
- nbr_local: int32 [1024, 7], P(('dom', 'grp')), may hold values from 0 to 79, as said below
- ap_slot: int32 [1024, 7, 4], P(('dom', 'grp')), may hold values from 0 to 7, as said below
- tile_slot: int32 [1024, 4, 8], P(('dom', 'grp')), may hold values from 0 to 71, as said below
- send_rows: int32 [32, 8, 6], P(('dom', 'grp')), may hold values from 0 to 31
- owner_map: int32 [32, 72], P(('dom', 'grp')), may hold values from 0 to 127
Outputs:
- coarse_tiles: float32 [64, 262144], P(None, ('dom', 'grp'))
Inputs may be any that keep to these rules, and one draw needn't show every extreme that they name: `nbr_local`: column 0 is the element itself. A value below 32 is an element of the same device; the value 32 + p * 6 + g stands for the row that neighbour p sends to this device in slot g, and every such ghost value appears on every device. `ap_slot`: each row's 7 * 4 entries name every value from 0 to 7. `tile_slot`: on every device each of the 72 partial tiles is named by some entry.
All inputs are finite; a program needn't handle non-finite values.
Results may differ from a plain program's by a relative error of at most 0.0029.
Values may be sent and summed in bfloat16 or wider, within the bound.
No kernel may reach another device: no remote copies, remote signals or barrier semaphores. Data moves between devices by JAX's collectives and lax.ppermute only.
A program may use at most 192 MiB of HBM per device.

v0:
```python
import math

import jax
import jax.numpy as jnp
from jax import lax
from jax.sharding import PartitionSpec as P

KB = 64
KC = 64
NB = 7
PN = 4
QN = 8
OWN = 128


def padded_2(x, sides, width):
    for axis, dim in sides:
        devices, length = (lax.axis_size(axis), x.shape[dim])
        up = [(i, (i + 1) % devices) for i in range(devices)]
        down = [(j, i) for i, j in up]
        last = lax.slice_in_dim(x, length - width, length, axis=dim)
        leading = lax.slice_in_dim(x, 0, width, axis=dim)
        before = lax.ppermute(last, axis, up)
        after = lax.ppermute(leading, axis, down)
        x = jnp.concatenate([before, x, after], axis=dim)
    return x


def local_tiles(a_strips, p_strips, nbr_local, ap_slot, tile_slot, extended, tiles_total):
    rows_here = a_strips.shape[0]
    block_len = math.gcd(rows_here, 32)
    blocks = rows_here // block_len
    tile_ids = jnp.arange(tiles_total, dtype=jnp.int32)

    def regroup(source_array):
        return source_array.reshape((blocks, block_len) + source_array.shape[1:])

    def accumulate(partial_value, inputs):
        a_block, p_block, nbr_block, slot_block, tile_block = inputs
        a_tiles = a_block.reshape(block_len, KB, NB, KB)
        gathered = extended[nbr_block]
        product = jnp.einsum(
            "eijm,ejmn->ejin", a_tiles, gathered, preferred_element_type=jnp.float32
        )
        product = product.reshape(block_len, NB, KB, PN, KC)
        selector = (slot_block[..., None] == jnp.arange(QN, dtype=jnp.int32)).astype(jnp.float32)
        applied = jnp.einsum(
            "ejikc,ejkq->eiqc", product, selector, precision=lax.Precision.HIGHEST
        ).astype(jnp.bfloat16)
        own_tiles = p_block.reshape(block_len, KB, PN, KC)
        contrib = jnp.einsum(
            "emkc,emqd->ekqcd", own_tiles, applied, preferred_element_type=jnp.float32
        )
        placement = (tile_block.reshape(-1)[:, None] == tile_ids[None, :]).astype(jnp.float32)
        added = jnp.einsum(
            "nt,nf->tf", placement, contrib.reshape(-1, KC * KC), precision=lax.Precision.HIGHEST
        )
        return (partial_value + added, None)

    initial = jnp.zeros((tiles_total, KC * KC), jnp.float32)
    inputs = (
        regroup(a_strips),
        regroup(p_strips),
        regroup(nbr_local),
        regroup(ap_slot),
        regroup(tile_slot),
    )
    return lax.scan(accumulate, initial, inputs)[0]


def body(a_strips, p_strips, nbr_local, ap_slot, tile_slot, send_rows, owner_map):
    strip_width = p_strips.shape[2]
    ghost_count = send_rows.shape[2]
    outgoing = p_strips[send_rows.reshape(-1)].reshape(8, ghost_count, KB, strip_width)
    middle = jnp.zeros_like(outgoing[:1])
    cells = jnp.concatenate([outgoing[:4], middle, outgoing[4:]], 0).reshape(
        3, 3, ghost_count, KB, strip_width
    )
    padded = padded_2(cells, (("dom", 0), ("grp", 1)), 1)
    picked = padded[0::2, 0::2].reshape(9, ghost_count, KB, strip_width)
    arrived = jnp.concatenate([picked[:4], picked[5:]], 0)
    extended = jnp.concatenate([p_strips, arrived.reshape(8 * ghost_count, KB, strip_width)], 0)
    tiles_total = owner_map.shape[1]
    slot_count = tiles_total // 9
    partial_value = local_tiles(
        a_strips, p_strips, nbr_local, ap_slot, tile_slot, extended, tiles_total
    )
    parcels = partial_value.reshape(3, 3, slot_count, KC, KC)
    tile_pad = padded_2(parcels, (("dom", 0), ("grp", 1)), 1)
    returned = tile_pad[0::2, 0::2].reshape(tiles_total, KC * KC)
    owner_ids = jnp.arange(OWN, dtype=jnp.int32)
    ownership = (owner_map.reshape(-1)[:, None] == owner_ids[None, :]).astype(jnp.float32)
    owned_tiles = jnp.einsum("tm,tf->mf", ownership, returned, precision=lax.Precision.HIGHEST)
    return owned_tiles.reshape(OWN, KC, KC).transpose(1, 0, 2).reshape(KC, OWN * KC)


def solution(mesh):
    placed = (
        P(("dom", "grp"), None, None),
        P(("dom", "grp"), None, None),
        P(("dom", "grp"), None),
        P(("dom", "grp"), None, None),
        P(("dom", "grp"), None, None),
        P(("dom", "grp"), None, None),
        P(("dom", "grp"), None),
    )
    return jax.shard_map(
        body, mesh=mesh, in_specs=placed, out_specs=P(None, ("dom", "grp")), check_vma=False
    )
```

profile of v0, /device:TPU:1, one launch (start us, length us, event | category | flops | bytes accessed | tf_op | source)
XLA Modules:
  0.0 317.1 jit_solution(6842731636387785229)
XLA Ops:
  1.7 1.9 gather_fusion
  3.7 2.1 collective-permute-start
  5.9 3.1 collective-permute-start.1
  9.4 21.1 %collective-permute-done = bf16[1,3,6,64,256]{4,3,2,1,0:T(8,128)(2,1)S(1)} collective-permute-done((bf16[1,3,6,64,256]{4,3,2,1,0:T(8,128)(2,1)S(1)}, bf16[1,3,6,64,256]{4,3,2,1,0:T(8,128)(2,1)S(1)}, u32[]{:S(2)}, u32[]{:S(2)}) %collective-permute-start) | collective-permute-done | bytes 589856 | tf_op jit(solution)/shard_map/ppermute | solution.py:23
  30.5 1.9 collective-permute-done.1
  33.2 1.5 pad_maximum_fusion.7
  34.7 3.0 collective-permute-start.2
  37.7 1.8 reshape.108
  39.5 6.4 %reshape.106 = bf16[32,64,7,64]{3,2,1,0:T(8,128)(2,1)} reshape(bf16[32,64,448]{2,1,0:T(8,128)(2,1)} %param.7) | data formatting | bytes 3670016 | tf_op jit(solution)/shard_map/while/body/eval_jaxpr/reshape | solution.py:40
  46.5 12.2 %collective-permute-done.2 = bf16[5,1,6,64,256]{4,3,2,1,0:T(8,128)(2,1)} collective-permute-done((bf16[5,1,6,64,256]{4,3,2,1,0:T(8,128)(2,1)}, bf16[5,1,6,64,256]{4,3,2,1,0:T(8,128)(2,1)}, u32[]{:S(2)}, u32[]{:S(2)}) %collective-permute-start.2) | collective-permute-done | bytes 983072 | tf_op jit(solution)/shard_map/ppermute | solution.py:23
  58.7 1.5 collective-permute-done.3
  60.2 2.7 pad_maximum_fusion.1
  64.6 8.3 %gather_fusion.1 = bf16[224,64,256]{2,1,0:T(8,128)(2,1)} fusion(bf16[80,64,256]{2,1,0:T(8,128)(2,1)S(1)} %pad_maximum_fusion.2, s32[1024]{0:T(1024)S(1)} %get-tuple-element.44), kind=kCustom, calls=%fused_computation.1 | custom fusion | bytes 14680960 | tf_op jit(solution)/shard_map/while/body/eval_jaxpr/gather | solution.py:41
  72.9 11.6 %convolution_bitcast_fusion.1 = f32[32,7,64,256]{3,2,1,0:T(8,128)} fusion(bf16[32,7,64,256]{3,2,1,0:T(8,128)(2,1)} %bitcast.62, bf16[32,64,7,64]{3,2,1,0:T(8,128)(2,1)} %reshape.106), kind=kOutput, calls=%fused_computation.3 | convolution fusion | flops 469762048 | bytes 23855104 | tf_op jit(solution)/shard_map/while/body/eval_jaxpr/eijm,ejmn->ejin/dot_general | solution.py:42
  84.6 25.3 %reshape.107 = f32[32,7,64,4,64]{4,3,2,1,0:T(4,128)} reshape(f32[32,7,64,256]{3,2,1,0:T(8,128)} %convolution_bitcast_fusion.1) | data formatting | bytes 29360128 | tf_op jit(solution)/shard_map/while/body/eval_jaxpr/reshape | solution.py:45
  109.9 26.6 %convolution_bitcast_fusion.2 = bf16[32,8,64,64,1]{3,1,4,2,0:T(8,128)(2,1)} fusion(f32[32,7,64,4,64]{4,3,2,1,0:T(4,128)} %reshape.107, pred[32,7,4,8,1]{3,2,4,1,0:T(4,128)(4,1)S(1)} %fusion.25), kind=kOutput, calls=%fused_computation.9 | convolution fusion | flops 352321536 | bytes 16784384 | tf_op jit(solution)/shard_map/while/body/eval_jaxpr/ejikc,ejkq->eiqc/dot_general | solution.py:47
  136.5 7.0 %copy.24 = bf16[32,8,64,64,1]{2,3,1,0,4:T(8,128)(2,1)} copy(bf16[32,8,64,64,1]{3,1,4,2,0:T(8,128)(2,1)} %convolution_bitcast_fusion.2) | data formatting | bytes 4194304 | tf_op jit(solution)/shard_map/while/body/eval_jaxpr/ejikc,ejkq->eiqc/dot_general | solution.py:47
  143.4 15.3 %convolution_bitcast_fusion = f32[32,4,8,64,64]{3,4,1,2,0:T(8,128)} fusion(bf16[32,8,64,64,1]{2,3,1,0,4:T(8,128)(2,1)} %copy.24, bf16[32,64,4,64,1]{3,2,1,0,4:T(4,128)(2,1)S(1)} %bitcast.63), kind=kOutput, calls=%fused_computation.2 | convolution fusion | flops 536870912 | bytes 19922944 | tf_op jit(solution)/shard_map/while/body/eval_jaxpr/emkc,emqd->ekqcd/dot_general | solution.py:51
  158.7 33.5 %copy.19 = f32[32,4,8,64,64]{4,3,2,1,0:T(8,128)} copy(f32[32,4,8,64,64]{3,4,1,2,0:T(8,128)} %convolution_bitcast_fusion) | data formatting | bytes 33554432 | tf_op jit(solution)/shard_map/while/body/eval_jaxpr/emkc,emqd->ekqcd/transpose | solution.py:51
  192.2 27.9 %reshape.109 = f32[1024,4096]{1,0:T(8,128)} reshape(f32[32,4,8,64,64]{4,3,2,1,0:T(8,128)} %copy.19) | data formatting | bytes 33554432 | tf_op jit(solution)/shard_map/while/body/eval_jaxpr/reshape | solution.py:56
  220.1 10.4 %fusion.4 = f32[72,4096]{1,0:T(8,128)S(1)} fusion(f32[1024,4096]{1,0:T(8,128)} %reshape.109, s32[1024]{0:T(1024)S(1)} %eq.61), kind=kOutput, calls=%fused_computation.19 | convolution fusion | flops 3623952384 | bytes 17960960 | tf_op jit(solution)/shard_map/while/body/eval_jaxpr/nt,nf->tf/dot_general | solution.py:55
  233.0 4.2 %collective-permute-start.5 = (f32[1,3,8,64,64]{4,3,2,1,0:T(8,128)}, f32[1,3,8,64,64]{4,3,2,1,0:T(8,128)}, u32[]{:S(2)}, u32[]{:S(2)}) collective-permute-start(f32[1,3,8,64,64]{4,3,2,1,0:T(8,128)} %slice.82), channel_id=1, source_target_pairs={{4,0},{8,4},{12,8},{16,12},{20,16},{24,20},{28,24},{0,28},{5,1},{9... | collective-permute-start | bytes 1179656 | tf_op jit(solution)/shard_map/ppermute | solution.py:24
  238.1 28.0 %collective-permute-done.4 = f32[1,3,8,64,64]{4,3,2,1,0:T(8,128)} collective-permute-done((f32[1,3,8,64,64]{4,3,2,1,0:T(8,128)}, f32[1,3,8,64,64]{4,3,2,1,0:T(8,128)}, u32[]{:S(2)}, u32[]{:S(2)}) %collective-permute-start.4) | collective-permute-done | bytes 393248 | tf_op jit(solution)/shard_map/ppermute | solution.py:23
  267.5 2.8 collective-permute-done.5
  271.8 1.7 collective-permute-start.6
  273.5 27.8 %collective-permute-done.6 = f32[5,1,8,64,64]{4,3,2,1,0:T(8,128)S(1)} collective-permute-done((f32[5,1,8,64,64]{4,3,2,1,0:T(8,128)S(1)}, f32[5,1,8,64,64]{4,3,2,1,0:T(8,128)S(1)}, u32[]{:S(2)}, u32[]{:S(2)}) %collective-permute-start.6) | collective-permute-done | bytes 655392 | tf_op jit(solution)/shard_map/ppermute | solution.py:23
  301.3 1.5 collective-permute-done.7
  302.8 1.4 pad_maximum_fusion
  305.1 1.8 copy.20
  306.9 2.7 convolution_bitcast_fusion.3
  309.6 2.7 copy.21
  312.4 4.8 %reshape.112 = f32[64,8192]{1,0:T(8,128)} reshape(f32[64,128,64]{2,1,0:T(8,128)} %copy.21) | data formatting | bytes 4194304 | tf_op jit(solution)/shard_map/reshape | solution.py:94
  (48 shorter events, 12.5 us)
Async XLA Ops:
  3.7 26.8 %collective-permute-start = (bf16[1,3,6,64,256]{4,3,2,1,0:T(8,128)(2,1)S(1)}, bf16[1,3,6,64,256]{4,3,2,1,0:T(8,128)(2,1)S(1)}, u32[]{:S(2)}, u32[]{:S(2)}) collective-permute-start(bf16[1,3,6,64,256]{4,3,2,1,0:T(8,128)(2,1)S(1)} %bitcast.72), channel_id=1, source_target_pairs={{0,4},{4,8},{8,12},{12,16},{16,20},{20,24},{24,28},{28,0},{1,5},{5... | collective-permute-start | bytes 1769480 | tf_op jit(solution)/shard_map/ppermute | solution.py:23
  5.9 26.5 %collective-permute-start.1 = (bf16[1,3,6,64,256]{4,3,2,1,0:T(8,128)(2,1)S(1)}, bf16[1,3,6,64,256]{4,3,2,1,0:T(8,128)(2,1)S(1)}, u32[]{:S(2)}, u32[]{:S(2)}) collective-permute-start(bf16[1,3,6,64,256]{4,3,2,1,0:T(8,128)(2,1)S(1)} %bitcast.71), channel_id=1, source_target_pairs={{4,0},{8,4},{12,8},{16,12},{20,16},{24,20},{28,24},{0,28},{5,1},{9... | collective-permute-start | bytes 1769480 | tf_op jit(solution)/shard_map/ppermute | solution.py:24
  9.1 28.5 %copy-start.1 = (bf16[32,64,256]{2,1,0:T(8,128)(2,1)S(1)}, bf16[32,64,256]{2,1,0:T(8,128)(2,1)}, u32[]{:S(2)}) copy-start(bf16[32,64,256]{2,1,0:T(8,128)(2,1)} %param.8) | copy-start | bytes 3145732
  32.4 0.8 copy-start.3
  34.7 24.0 %collective-permute-start.2 = (bf16[5,1,6,64,256]{4,3,2,1,0:T(8,128)(2,1)}, bf16[5,1,6,64,256]{4,3,2,1,0:T(8,128)(2,1)}, u32[]{:S(2)}, u32[]{:S(2)}) collective-permute-start(bf16[5,1,6,64,256]{4,3,2,1,0:T(8,128)(2,1)} %get-tuple-element.23), channel_id=1, source_target_pairs={{0,1},{1,2},{2,3},{3,0},{4,5},{5,6},{6,7},{7,4},{8,9},{9,10},{10,1... | collective-permute-start | bytes 2949128 | tf_op jit(solution)/shard_map/ppermute | solution.py:23
  37.7 22.6 %collective-permute-start.3 = (bf16[5,1,6,64,256]{4,3,2,1,0:T(8,128)(2,1)}, bf16[5,1,6,64,256]{4,3,2,1,0:T(8,128)(2,1)}, u32[]{:S(2)}, u32[]{:S(2)}) collective-permute-start(bf16[5,1,6,64,256]{4,3,2,1,0:T(8,128)(2,1)} %get-tuple-element.24), channel_id=1, source_target_pairs={{1,0},{2,1},{3,2},{0,3},{5,4},{6,5},{7,6},{4,7},{9,8},{10,9},{11,1... | collective-permute-start | bytes 2949128 | tf_op jit(solution)/shard_map/ppermute | solution.py:24
  39.4 6.4 %copy-start.6 = (s32[32,7,4]{0,2,1:T(4,128)S(1)}, s32[32,7,4]{0,2,1:T(4,128)}, u32[]{:S(2)}) copy-start(s32[32,7,4]{0,2,1:T(4,128)} %param.10) | copy-start | bytes 10756
  39.5 6.5 %copy-start.5 = (s32[32,4,8]{0,2,1:T(8,128)S(1)}, s32[32,4,8]{0,2,1:T(8,128)}, u32[]{:S(2)}) copy-start(s32[32,4,8]{0,2,1:T(8,128)} %param.11) | copy-start | bytes 12292
  39.5 20.8 %copy-start.4 = (bf16[1,3,6,64,256]{4,3,2,1,0:T(8,128)(2,1)S(1)}, bf16[1,3,6,64,256]{4,3,2,1,0:T(8,128)(2,1)}, u32[]{:S(2)}) copy-start(bf16[1,3,6,64,256]{4,3,2,1,0:T(8,128)(2,1)} %copy-done.3) | copy-start | bytes 1769476
  63.1 1.2 copy-start.2
  136.5 7.0 %copy-start = (bf16[32,64,4,64]{3,2,1,0:T(4,128)(2,1)S(1)}, bf16[32,64,4,64]{3,2,1,0:T(4,128)(2,1)}, u32[]{:S(2)}) copy-start(bf16[32,64,4,64]{3,2,1,0:T(4,128)(2,1)} %reshape.108) | copy-start | bytes 3145732
  231.8 34.4 %collective-permute-start.4 = (f32[1,3,8,64,64]{4,3,2,1,0:T(8,128)}, f32[1,3,8,64,64]{4,3,2,1,0:T(8,128)}, u32[]{:S(2)}, u32[]{:S(2)}) collective-permute-start(f32[1,3,8,64,64]{4,3,2,1,0:T(8,128)} %slice.80), channel_id=1, source_target_pairs={{0,4},{4,8},{8,12},{12,16},{16,20},{20,24},{24,28},{28,0},{1,5},{5... | collective-permute-start | bytes 1179656 | tf_op jit(solution)/shard_map/ppermute | solution.py:23
  233.0 37.3 %collective-permute-start.5 = (f32[1,3,8,64,64]{4,3,2,1,0:T(8,128)}, f32[1,3,8,64,64]{4,3,2,1,0:T(8,128)}, u32[]{:S(2)}, u32[]{:S(2)}) collective-permute-start(f32[1,3,8,64,64]{4,3,2,1,0:T(8,128)} %slice.82), channel_id=1, source_target_pairs={{4,0},{8,4},{12,8},{16,12},{20,16},{24,20},{28,24},{0,28},{5,1},{9... | collective-permute-start | bytes 1179656 | tf_op jit(solution)/shard_map/ppermute | solution.py:24
  271.8 29.5 %collective-permute-start.6 = (f32[5,1,8,64,64]{4,3,2,1,0:T(8,128)S(1)}, f32[5,1,8,64,64]{4,3,2,1,0:T(8,128)S(1)}, u32[]{:S(2)}, u32[]{:S(2)}) collective-permute-start(f32[5,1,8,64,64]{4,3,2,1,0:T(8,128)S(1)} %get-tuple-element.21), channel_id=1, source_target_pairs={{0,1},{1,2},{2,3},{3,0},{4,5},{5,6},{6,7},{7,4},{8,9},{9,10},{10,1... | collective-permute-start | bytes 1966088 | tf_op jit(solution)/shard_map/ppermute | solution.py:23
  273.5 29.3 %collective-permute-start.7 = (f32[5,1,8,64,64]{4,3,2,1,0:T(8,128)S(1)}, f32[5,1,8,64,64]{4,3,2,1,0:T(8,128)S(1)}, u32[]{:S(2)}, u32[]{:S(2)}) collective-permute-start(f32[5,1,8,64,64]{4,3,2,1,0:T(8,128)S(1)} %get-tuple-element.22), channel_id=1, source_target_pairs={{1,0},{2,1},{3,2},{0,3},{5,4},{6,5},{7,6},{4,7},{9,8},{10,9},{11,1... | collective-permute-start | bytes 1966088 | tf_op jit(solution)/shard_map/ppermute | solution.py:24
  304.4 2.5 copy-start.7
where the time goes:
time: 319 us; the launch traced here: 317 us
  local copies, waits for them, and re-layouts  132 us (41%)
  waiting for transfers between devices  96.8 us (30%)
  matrix products  66.6 us (21%)
  starting transfers between devices  14.1 us (4%)
  other arithmetic  7.18 us (2%)
    ppermute x4, waiting for transfers between devices, padded_2(): before = lax.ppermute(last, axis, up)  89.2 us
    transpose x1, local copies, waits for them, and re-layouts, accumulate(): jnp.einsum('emkc,emqd->ekqcd', own_tiles, applied, preferred_element_type...  33.5 us
    reshape x1, local copies, waits for them, and re-layouts, accumulate(): contrib.reshape(-1, KC * KC)  27.9 us
    dot_general x1, matrix products, accumulate(): jnp.einsum('ejikc,ejkq->eiqc', product, selector, precision=lax.Precision...  26.6 us
    reshape x1, local copies, waits for them, and re-layouts, accumulate(): product = product.reshape(block_len, NB, KB, PN, KC)  25.3 us
    dot_general x1, matrix products, accumulate(): jnp.einsum('emkc,emqd->ekqcd', own_tiles, applied, preferred_element_type...  15.3 us
    dot_general x1, matrix products, accumulate(): jnp.einsum('eijm,ejmn->ejin', a_tiles, gathered, preferred_element_type=j...  11.6 us
    dot_general x1, matrix products, accumulate(): jnp.einsum('nt,nf->tf', placement, contrib.reshape(-1, KC * KC), precisio...  10.4 us
  transfers between devices with their start and end apart: 8, of which 8 were waited for; matrix products, arithmetic and copies ran while one was open for 4% of the time, Pallas kernels for 0%

commit v1 on v0

v1 whole, which is shorter than its diff:
```python
import functools

import jax
import jax.numpy as jnp
from jax import lax
from jax.experimental import pallas as pl
from jax.experimental.pallas import tpu as pltpu
from jax.sharding import PartitionSpec as P

OWN = 128
OFFSETS = ((-1, -1), (-1, 0), (-1, 1), (0, -1), (0, 1), (1, -1), (1, 0), (1, 1))
GROUP = 4
SMEM = pl.BlockSpec(memory_space=pltpu.SMEM)
VMEM = pl.BlockSpec(memory_space=pltpu.VMEM)
ANY = pl.BlockSpec(memory_space=pl.ANY)
LIMIT = 48 * 1024 * 1024


def shifted(x, a, b):
    domains, groups = lax.axis_size("dom"), lax.axis_size("grp")
    pairs = [
        (i * groups + j, ((i + a) % domains) * groups + (j + b) % groups)
        for i in range(domains)
        for j in range(groups)
    ]
    return lax.ppermute(x, ("dom", "grp"), pairs)


def pack_kernel(send_ref, p_ref, *rest):
    outs, sems = rest[:-1], rest[-1]
    copies = [
        pltpu.make_async_copy(p_ref.at[send_ref[0, p, g]], out.at[g], sems.at[p, g])
        for p, out in enumerate(outs)
        for g in range(out.shape[0])
    ]
    for copy in copies:
        copy.start()
    for copy in copies:
        copy.wait()


def pack(send_rows, p_strips):
    _, neighbours, ghosts = send_rows.shape
    return pl.pallas_call(
        pack_kernel,
        out_shape=[jax.ShapeDtypeStruct((ghosts,) + p_strips.shape[1:], p_strips.dtype)] * neighbours,
        in_specs=[SMEM, ANY],
        out_specs=[ANY] * neighbours,
        scratch_shapes=[pltpu.SemaphoreType.DMA((neighbours, ghosts))],
        name="pack",
    )(send_rows, p_strips)


def local_kernel(blocks, pieces, slots, nbr_ref, ap_ref, a_ref, p_ref, sums_ref, ga_ref, pt_ref, info_ref):
    elements, kb, _ = a_ref.shape
    kc = p_ref.shape[2] // pieces
    stride = slots + 1
    left = lax.broadcasted_iota(jnp.int32, (kb, 2 * kc), 1) < kc

    def element(e, count):
        sums_ref[pl.ds(e * stride, stride)] = jnp.zeros((stride, kb, 2 * kc), jnp.float32)
        for j in range(blocks):
            n = nbr_ref[e * blocks + j]
            ghost = n >= elements
            a = a_ref[e, :, j * kb : (j + 1) * kb]
            product = jnp.dot(
                a, p_ref[jnp.where(ghost, 0, n)], preferred_element_type=jnp.float32
            )
            for k in range(pieces):
                slot = ap_ref[(e * blocks + j) * pieces + k]
                row = e * stride + jnp.where(ghost, slots, slot)
                piece = product[:, (k // 2) * 2 * kc : (k // 2 + 1) * 2 * kc]
                sums_ref[row] += jnp.where(left if k % 2 == 0 else ~left, piece, 0.0)
                if j > 0:
                    info_ref[count * (pieces + 1) + k] = e * stride + slot
            if j > 0:
                info_ref[count * (pieces + 1) + pieces] = n - elements
                ga_ref[count] = a
                count = count + ghost.astype(jnp.int32)
        pt = p_ref[e].astype(jnp.float32).T.reshape(pieces, 2, kc // 2, kb)
        pt_ref[e, :, :kb] = pt[:, 0].reshape(pieces * kc // 2, kb).astype(jnp.bfloat16)
        pt_ref[e, :, kb:] = pt[:, 1].reshape(pieces * kc // 2, kb).astype(jnp.bfloat16)
        return count

    count = lax.fori_loop(0, elements, element, jnp.int32(0))
    for u in range(GROUP):
        for k in range(pieces):
            info_ref[(count + u) * (pieces + 1) + k] = slots
        info_ref[(count + u) * (pieces + 1) + pieces] = 0
    info_ref[info_ref.shape[0] - 1] = count


def local_part(a_strips, p_strips, nbr_local, ap_slot, slots):
    elements, kb, _ = a_strips.shape
    blocks, pieces = ap_slot.shape[1:]
    kc = p_strips.shape[2] // pieces
    capacity = elements * (blocks - 1) + GROUP
    return pl.pallas_call(
        functools.partial(local_kernel, blocks, pieces, slots),
        out_shape=[
            pltpu.VMEM((elements * (slots + 1), kb, 2 * kc), jnp.float32),
            pltpu.VMEM((capacity, kb, kb), jnp.bfloat16),
            pltpu.VMEM((elements, pieces * kc // 2, 2 * kb), jnp.bfloat16),
            jax.ShapeDtypeStruct((capacity * (pieces + 1) + 1,), jnp.int32),
        ],
        in_specs=[SMEM, SMEM, VMEM, VMEM],
        out_specs=[VMEM, VMEM, VMEM, SMEM],
        compiler_params=pltpu.CompilerParams(vmem_limit_bytes=LIMIT),
        name="local_part",
    )(nbr_local.reshape(-1), ap_slot.reshape(-1), a_strips, p_strips)


def finish_kernel(pieces, slots, cells, info_ref, tile_ref, sums_ref, ga_ref, pt_ref, *rest):
    arrived = rest[: cells - 1]
    sums_out = rest[cells - 1]
    sent = rest[cells : 2 * cells]
    ghost_ref, tiles_ref, sems = rest[2 * cells :]
    del sums_ref
    ghosts = arrived[0].shape[0]
    elements, _, kb2 = pt_ref.shape
    kb = kb2 // 2
    kc2 = sums_out.shape[2]
    half = kc2 // 4
    stride = slots + 1
    copies = [
        pltpu.make_async_copy(ref, ghost_ref.at[pl.ds(p * ghosts, ghosts)], sems.at[p])
        for p, ref in enumerate(arrived)
    ]
    for copy in copies:
        copy.start()
    tiles_ref[...] = jnp.zeros_like(tiles_ref)
    left = lax.broadcasted_iota(jnp.int32, (kb, kc2), 1) < kc2 // 2
    for copy in copies:
        copy.wait()
    count = info_ref[info_ref.shape[0] - 1]

    def ghost_group(i, carry):
        for u in range(GROUP):
            at = i * GROUP + u
            product = jnp.dot(
                ga_ref[at],
                ghost_ref[info_ref[at * (pieces + 1) + pieces]],
                preferred_element_type=jnp.float32,
            )
            for k in range(pieces):
                piece = product[:, (k // 2) * kc2 : (k // 2 + 1) * kc2]
                sums_out[info_ref[at * (pieces + 1) + k]] += jnp.where(
                    left if k % 2 == 0 else ~left, piece, 0.0
                )
        return carry

    lax.fori_loop(0, (count + GROUP - 1) // GROUP, ghost_group, 0)
    zero = jnp.zeros((kb, kc2), jnp.bfloat16)

    def element(e, carry):
        pt = pt_ref[e]
        for pair in range(slots // 2):
            columns = []
            for q in (2 * pair, 2 * pair + 1):
                x = sums_out[e * stride + q]
                y = (x + pltpu.roll(x, kc2 // 2, 1)).astype(jnp.bfloat16)
                columns.append(
                    jnp.concatenate([jnp.where(left, y, zero), jnp.where(left, zero, y)], axis=0)
                )
            terms = jnp.dot(
                pt, jnp.concatenate(columns, axis=1), preferred_element_type=jnp.float32
            )
            for k in range(pieces):
                for u in range(2):
                    t = tile_ref[(e * pieces + k) * slots + 2 * pair + u]
                    tiles_ref[t] += terms[k * half : (k + 1) * half, u * kc2 : (u + 1) * kc2]
        return carry

    lax.fori_loop(0, elements, element, 0)
    for cell, out in enumerate(sent):
        count_of = out.shape[0]
        out[...] = tiles_ref[pl.ds(cell * count_of, count_of)].astype(out.dtype)


def finish(info, tile_slot, sums, ga, pt, arrived, tiles_total):
    pieces, slots = tile_slot.shape[1:]
    cells = len(arrived) + 1
    half, kc2 = sums.shape[2] // 4, sums.shape[2]
    capacity = tiles_total // cells
    results = pl.pallas_call(
        functools.partial(finish_kernel, pieces, slots, cells),
        out_shape=[pltpu.VMEM(sums.shape, sums.dtype)]
        + [
            jax.ShapeDtypeStruct(
                (capacity, half, kc2), jnp.float32 if cell == cells // 2 else jnp.bfloat16
            )
            for cell in range(cells)
        ],
        in_specs=[SMEM, SMEM, VMEM, VMEM, VMEM] + [ANY] * (cells - 1),
        out_specs=[VMEM] * (cells + 1),
        scratch_shapes=[
            pltpu.VMEM(((cells - 1) * arrived[0].shape[0],) + arrived[0].shape[1:], jnp.bfloat16),
            pltpu.VMEM((tiles_total, half, kc2), jnp.float32),
            pltpu.SemaphoreType.DMA((cells - 1,)),
        ],
        input_output_aliases={2: 0},
        compiler_params=pltpu.CompilerParams(vmem_limit_bytes=LIMIT),
        name="finish",
    )(info, tile_slot.reshape(-1), sums, ga, pt, *arrived)
    return results[1:]


def owner_kernel(owner_ref, *rest):
    parcels, out_ref, tiles_ref = rest[:-2], rest[-2], rest[-1]
    tiles_ref[...] = jnp.zeros_like(tiles_ref)
    owned, half, kc2 = tiles_ref.shape
    for c, parcel in enumerate(parcels):
        capacity = parcel.shape[0]
        for g in range(capacity):
            tiles_ref[owner_ref[c * capacity + g]] += parcel[g].astype(jnp.float32)
    left = lax.broadcasted_iota(jnp.int32, (half, kc2), 1) < kc2 // 2
    for i in range(owned // 2):
        first, second = tiles_ref[2 * i], tiles_ref[2 * i + 1]
        columns = pl.ds(i * kc2, kc2)
        out_ref[:half, columns] = jnp.where(left, first, pltpu.roll(second, kc2 // 2, 1))
        out_ref[half:, columns] = jnp.where(left, pltpu.roll(first, kc2 // 2, 1), second)


def owner_sums(owner_map, parcels):
    _, half, kc2 = parcels[0].shape
    return pl.pallas_call(
        owner_kernel,
        out_shape=jax.ShapeDtypeStruct((2 * half, OWN * kc2 // 2), jnp.float32),
        in_specs=[SMEM] + [VMEM] * len(parcels),
        out_specs=VMEM,
        scratch_shapes=[pltpu.VMEM((OWN, half, kc2), jnp.float32)],
        compiler_params=pltpu.CompilerParams(vmem_limit_bytes=LIMIT),
        name="owner_sums",
    )(owner_map.reshape(-1), *parcels)


def body(a_strips, p_strips, nbr_local, ap_slot, tile_slot, send_rows, owner_map):
    outgoing = pack(send_rows, p_strips)
    arrived = [shifted(outgoing[7 - p], -a, -b) for p, (a, b) in enumerate(OFFSETS)]
    sums, ga, pt, info = local_part(a_strips, p_strips, nbr_local, ap_slot, tile_slot.shape[2])
    tiles = finish(info, tile_slot, sums, ga, pt, arrived, owner_map.shape[1])
    middle = len(tiles) // 2
    returned = [
        tiles[middle]
        if c == middle
        else shifted(tiles[len(tiles) - 1 - c], -(c // 3 - 1), -(c % 3 - 1))
        for c in range(len(tiles))
    ]
    return owner_sums(owner_map, returned)


def solution(mesh):
    placed = (
        P(("dom", "grp"), None, None),
        P(("dom", "grp"), None, None),
        P(("dom", "grp"), None),
        P(("dom", "grp"), None, None),
        P(("dom", "grp"), None, None),
        P(("dom", "grp"), None, None),
        P(("dom", "grp"), None),
    )
    return jax.shard_map(
        body, mesh=mesh, in_specs=placed, out_specs=P(None, ("dom", "grp")), check_vma=False
    )
```

time: 319 us -> 140 us (0.44)
  local copies, waits for them, and re-layouts: 132 us -> 10.2 us
  Pallas kernels: 0 us -> 85.6 us
  waiting for transfers between devices: 96.8 us -> 20.8 us
  matrix products: 66.6 us -> 0 us
  starting transfers between devices: 14.1 us -> 22.6 us
  other arithmetic: 7.18 us -> 0 us
    pallas_call x0 -> x4, Pallas kernels: none -> 85.6 us  [the longest x1 49.9 us: pack(): pl.pallas_call(pack_kernel, out_shape=[jax.ShapeDtypeStruct((ghosts,) + p...]
    ppermute x8 -> x16, waiting for transfers between devices: 96.8 us -> 20.8 us  [shifted(): return lax.ppermute(x, ('dom', 'grp'), pairs)]
    reshape x9 -> x3, local copies, waits for them, and re-layouts: 69.6 us -> 2.1 us  [the longest x1 0.71 us: finish(): tile_slot.reshape(-1)]
    dot_general x5 -> x0, matrix products: 66.6 us -> none  [the longest x1 26.6 us: accumulate(): jnp.einsum('ejikc,ejkq->eiqc', product, selector, precision=lax.Precision...]
    transpose x2 -> x0, local copies, waits for them, and re-layouts: 36.2 us -> none  [the longest x1 33.5 us: accumulate(): jnp.einsum('emkc,emqd->ekqcd', own_tiles, applied, preferred_element_type...]
    gather x2 -> x0, local copies, waits for them, and re-layouts: 10.2 us -> none  [the longest x1 8.35 us: accumulate(): gathered = extended[nbr_block]]
    ppermute x8 -> x16, starting transfers between devices: 14.1 us -> 22.6 us  [shifted(): return lax.ppermute(x, ('dom', 'grp'), pairs)]
    dot_general x1 -> x0, local copies, waits for them, and re-layouts: 6.95 us -> none  [accumulate(): jnp.einsum('ejikc,ejkq->eiqc', product, selector, precision=lax.Precision...]
  transfers between devices with their start and end apart: 8 -> 16, of which waited for: 8 -> 8; matrix products, arithmetic and copies ran while one was open for 4% -> 3% of each run, Pallas kernels for 0% -> 10%
where the time goes in v1:
time: 140 us; the launch traced here: 139 us
  Pallas kernels  85.6 us (61%)
  starting transfers between devices  22.6 us (16%)
  waiting for transfers between devices  20.8 us (15%)
  local copies, waits for them, and re-layouts  10.2 us (7%)
    pallas_call x1, Pallas kernels, pack(): pl.pallas_call(pack_kernel, out_shape=[jax.ShapeDtypeStruct((ghosts,) + p...  49.9 us
    ppermute x16, starting transfers between devices, shifted(): return lax.ppermute(x, ('dom', 'grp'), pairs)  22.6 us
    ppermute x16, waiting for transfers between devices, shifted(): return lax.ppermute(x, ('dom', 'grp'), pairs)  20.8 us
    pallas_call x1, Pallas kernels, finish(): pl.pallas_call(functools.partial(finish_kernel, pieces, slots, cells), ou...  19.1 us
    pallas_call x1, Pallas kernels, local_part(): pl.pallas_call(functools.partial(local_kernel, blocks, pieces, slots), ou...  13.7 us
    unnamed x28, local copies, waits for them, and re-layouts  8.15 us
    pallas_call x1, Pallas kernels, owner_sums(): pl.pallas_call(owner_kernel, out_shape=jax.ShapeDtypeStruct((2 * half, OW...  2.87 us
  transfers between devices with their start and end apart: 16, of which 8 were waited for; matrix products, arithmetic and copies ran while one was open for 3% of the time, Pallas kernels for 10%

profile of v1, /device:TPU:1, one launch (start us, length us, event | category | flops | bytes accessed | tf_op | source)
XLA Modules:
  0.0 139.5 jit_solution(1988325217425755120)
XLA Ops:
  0.0 1.3 copy.13.send_ref
  1.3 49.9 %pack.1 = (bf16[6,64,256]{2,1,0:T(8,128)(2,1)}, bf16[6,64,256]{2,1,0:T(8,128)(2,1)}, bf16[6,64,256]{2,1,0:T(8,128)(2,1)}, bf16[6,64,256]{2,1,0:T(8,128)(2,1)}, b...) custom-call(s32[1,8,6]{2,1,0:T(8,128)} %copy.13.send_ref, ...), custom_call_target="tpu_custom_call" | custom-call | tf_op jit(solution)/shard_map/pack/pallas_call | solution.py:44
  51.3 3.6 %collective-permute-start = (bf16[6,64,256]{2,1,0:T(8,128)(2,1)}, bf16[6,64,256]{2,1,0:T(8,128)(2,1)S(1)}, u32[]{:S(2)}, u32[]{:S(2)}) collective-permute-start(bf16[6,64,256]{2,1,0:T(8,128)(2,1)} %get-tuple-element.30), channel_id=1, source_target_pairs={{0,5},{1,6},{2,7},{3,4},{4,9},{5,10},{6,11},{7,8},{8,13},{9,14},{1... | collective-permute-start | bytes 589832 | tf_op jit(solution)/shard_map/ppermute | solution.py:26
  54.9 1.2 collective-permute-start.1
  56.4 2.4 %collective-permute-start.3 = (bf16[6,64,256]{2,1,0:T(8,128)(2,1)}, bf16[6,64,256]{2,1,0:T(8,128)(2,1)S(1)}, u32[]{:S(2)}, u32[]{:S(2)}) collective-permute-start(bf16[6,64,256]{2,1,0:T(8,128)(2,1)} %get-tuple-element.33), channel_id=1, source_target_pairs={{0,1},{1,2},{2,3},{3,0},{4,5},{5,6},{6,7},{7,4},{8,9},{9,10},{10,1... | collective-permute-start | bytes 589832 | tf_op jit(solution)/shard_map/ppermute | solution.py:26
  58.8 3.8 %collective-permute-done.rest_0_ = bf16[6,64,256]{2,1,0:T(8,128)(2,1)S(1)} collective-permute-done((bf16[6,64,256]{2,1,0:T(8,128)(2,1)}, bf16[6,64,256]{2,1,0:T(8,128)(2,1)S(1)}, u32[]{:S(2)}, u32[]{:S(2)}) %collective-permute-start) | collective-permute-done | bytes 196640 | tf_op jit(solution)/shard_map/ppermute | solution.py:26
  62.7 2.0 %collective-permute-start.5 = (bf16[6,64,256]{2,1,0:T(8,128)(2,1)}, bf16[6,64,256]{2,1,0:T(8,128)(2,1)S(1)}, u32[]{:S(2)}, u32[]{:S(2)}) collective-permute-start(bf16[6,64,256]{2,1,0:T(8,128)(2,1)} %get-tuple-element.35), channel_id=1, source_target_pairs={{0,29},{1,30},{2,31},{3,28},{4,1},{5,2},{6,3},{7,0},{8,5},{9,6},{1... | collective-permute-start | bytes 589832 | tf_op jit(solution)/shard_map/ppermute | solution.py:26
  64.6 3.7 %collective-permute-done.1.rest_1_ = bf16[6,64,256]{2,1,0:T(8,128)(2,1)S(1)} collective-permute-done((bf16[6,64,256]{2,1,0:T(8,128)(2,1)}, bf16[6,64,256]{2,1,0:T(8,128)(2,1)S(1)}, u32[]{:S(2)}, u32[]{:S(2)}) %collective-permute-start.1) | collective-permute-done | bytes 196640 | tf_op jit(solution)/shard_map/ppermute | solution.py:26
  68.3 0.9 collective-permute-start.6
  69.2 4.1 %collective-permute-done.2.rest_2_ = bf16[6,64,256]{2,1,0:T(8,128)(2,1)S(1)} collective-permute-done((bf16[6,64,256]{2,1,0:T(8,128)(2,1)}, bf16[6,64,256]{2,1,0:T(8,128)(2,1)S(1)}, u32[]{:S(2)}, u32[]{:S(2)}) %collective-permute-start.2) | collective-permute-done | bytes 196640 | tf_op jit(solution)/shard_map/ppermute | solution.py:26
  73.3 5.9 %collective-permute-start.7 = (bf16[6,64,256]{2,1,0:T(8,128)(2,1)}, bf16[6,64,256]{2,1,0:T(8,128)(2,1)S(1)}, u32[]{:S(2)}, u32[]{:S(2)}) collective-permute-start(bf16[6,64,256]{2,1,0:T(8,128)(2,1)} %get-tuple-element.37), channel_id=1, source_target_pairs={{0,31},{1,28},{2,29},{3,30},{4,3},{5,0},{6,1},{7,2},{8,7},{9,4},{1... | collective-permute-start | bytes 589832 | tf_op jit(solution)/shard_map/ppermute | solution.py:26
  79.2 0.8 copy.10
  79.9 0.7 reshape.13.nbr_ref
  80.6 0.8 copy.12
  81.4 0.7 reshape.15.tile_ref
  82.2 0.8 copy.11
  83.0 0.7 reshape.14.ap_ref
  83.7 13.7 %local_part.1 = (f32[288,64,128]{2,1,0:T(8,128)S(1)}, bf16[196,64,64]{2,1,0:T(8,128)(2,1)S(1)}, bf16[32,128,128]{2,1,0:T(8,128)(2,1)S(1)}, s32[981]{0:T(1024)}) custom-call(s32[224]{0:T(256)} %reshape.13.nbr_ref, s32[896]{0:T(1024)} %reshape.14.ap_ref, bf16[32,64,448]{2,1,0:T(8,128)(2,1)} %a_ref.1, bf16[32,64,256]{2,1,0:T(8,128)(2,1)} %p_ref.3), custom_call_target="tpu_custom_call" | custom-call | tf_op jit(solution)/shard_map/local_part/pallas_call | solution.py:98
  97.4 1.6 %copy-done = bf16[196,64,64]{2,1,0:T(8,128)(2,1)} copy-done((bf16[196,64,64]{2,1,0:T(8,128)(2,1)}, bf16[196,64,64]{2,1,0:T(8,128)(2,1)S(1)}, u32[]{:S(2)}) %copy-start) | copy-done | bytes 1605656
  99.0 1.0 copy-done.1
  101.0 19.1 %finish.1 = (f32[288,64,128]{2,1,0:T(8,128)S(1)}, bf16[8,32,128]{2,1,0:T(8,128)(2,1)}, bf16[8,32,128]{2,1,0:T(8,128)(2,1)}, bf16[8,32,128]{2,1,0:T(8,128)(2,1)},...) custom-call(s32[981]{0:T(1024)} %get-tuple-element.26.info_ref, ...), custom_call_target="tpu_custom_call", output_to_operand_aliasing={{0}: (2, {})} | custom-call | tf_op jit(solution)/shard_map/finish/pallas_call | solution.py:185
  120.2 0.9 collective-permute-start.9
  121.1 2.3 %collective-permute-start.11 = (bf16[8,32,128]{2,1,0:T(8,128)(2,1)}, bf16[8,32,128]{2,1,0:T(8,128)(2,1)S(1)}, u32[]{:S(2)}, u32[]{:S(2)}) collective-permute-start(bf16[8,32,128]{2,1,0:T(8,128)(2,1)} %get-tuple-element.41), channel_id=1, source_target_pairs={{0,1},{1,2},{2,3},{3,0},{4,5},{5,6},{6,7},{7,4},{8,9},{9,10},{10,1... | collective-permute-start | bytes 196616 | tf_op jit(solution)/shard_map/ppermute | solution.py:26
  123.3 3.8 %collective-permute-done.8.rest_0_ = bf16[8,32,128]{2,1,0:T(8,128)(2,1)S(1)} collective-permute-done((bf16[8,32,128]{2,1,0:T(8,128)(2,1)}, bf16[8,32,128]{2,1,0:T(8,128)(2,1)S(1)}, u32[]{:S(2)}, u32[]{:S(2)}) %collective-permute-start.8) | collective-permute-done | bytes 65568 | tf_op jit(solution)/shard_map/ppermute | solution.py:26
  127.2 2.1 %collective-permute-start.13 = (bf16[8,32,128]{2,1,0:T(8,128)(2,1)}, bf16[8,32,128]{2,1,0:T(8,128)(2,1)S(1)}, u32[]{:S(2)}, u32[]{:S(2)}) collective-permute-start(bf16[8,32,128]{2,1,0:T(8,128)(2,1)} %get-tuple-element.44), channel_id=1, source_target_pairs={{0,29},{1,30},{2,31},{3,28},{4,1},{5,2},{6,3},{7,0},{8,5},{9,6},{1... | collective-permute-start | bytes 196616 | tf_op jit(solution)/shard_map/ppermute | solution.py:26
  129.2 0.6 collective-permute-start.14
  129.9 1.0 collective-permute-done.10.rest_2_
  131.3 1.0 collective-permute-done.13.rest_6_
  132.3 1.5 %collective-permute-done.14.rest_7_ = bf16[8,32,128]{2,1,0:T(8,128)(2,1)S(1)} collective-permute-done((bf16[8,32,128]{2,1,0:T(8,128)(2,1)}, bf16[8,32,128]{2,1,0:T(8,128)(2,1)S(1)}, u32[]{:S(2)}, u32[]{:S(2)}) %collective-permute-start.14) | collective-permute-done | bytes 65568 | tf_op jit(solution)/shard_map/ppermute | solution.py:26
  133.9 1.8 %collective-permute-done.15.rest_8_ = bf16[8,32,128]{2,1,0:T(8,128)(2,1)S(1)} collective-permute-done((bf16[8,32,128]{2,1,0:T(8,128)(2,1)}, bf16[8,32,128]{2,1,0:T(8,128)(2,1)S(1)}, u32[]{:S(2)}, u32[]{:S(2)}) %collective-permute-start.15) | collective-permute-done | bytes 65568 | tf_op jit(solution)/shard_map/ppermute | solution.py:26
  135.7 0.9 copy-done.2
  136.6 2.9 %owner_sums.1 = f32[64,8192]{1,0:T(8,128)} custom-call(s32[72]{0:T(128)S(1)} %bitcast.1, bf16[8,32,128]{2,1,0:T(8,128)(2,1)S(1)} %collective-permute-done.8.rest_0_, bf16[8,32,128]{2,1,0:T(8,128)(2,1)S(1)} %collective-permute-done.9.rest_1_, bf16[8,32,128]{2,1,0:T(8,128)(2,1)S(1)} %collective-permute-done.10.rest_2_, ...), custom_call_target="tpu_custom_call" | custom-call | tf_op jit(solution)/shard_map/owner_sums/pallas_call | solution.py:226
  (35 shorter events, 1.7 us)
Async XLA Ops:
  51.3 11.4 %collective-permute-start = (bf16[6,64,256]{2,1,0:T(8,128)(2,1)}, bf16[6,64,256]{2,1,0:T(8,128)(2,1)S(1)}, u32[]{:S(2)}, u32[]{:S(2)}) collective-permute-start(bf16[6,64,256]{2,1,0:T(8,128)(2,1)} %get-tuple-element.30), channel_id=1, source_target_pairs={{0,5},{1,6},{2,7},{3,4},{4,9},{5,10},{6,11},{7,8},{8,13},{9,14},{1... | collective-permute-start | bytes 589832 | tf_op jit(solution)/shard_map/ppermute | solution.py:26
  54.9 13.5 %collective-permute-start.1 = (bf16[6,64,256]{2,1,0:T(8,128)(2,1)}, bf16[6,64,256]{2,1,0:T(8,128)(2,1)S(1)}, u32[]{:S(2)}, u32[]{:S(2)}) collective-permute-start(bf16[6,64,256]{2,1,0:T(8,128)(2,1)} %get-tuple-element.31), channel_id=1, source_target_pairs={{0,4},{1,5},{2,6},{3,7},{4,8},{5,9},{6,10},{7,11},{8,12},{9,13},{1... | collective-permute-start | bytes 589832 | tf_op jit(solution)/shard_map/ppermute | solution.py:26
  56.1 17.2 %collective-permute-start.2 = (bf16[6,64,256]{2,1,0:T(8,128)(2,1)}, bf16[6,64,256]{2,1,0:T(8,128)(2,1)S(1)}, u32[]{:S(2)}, u32[]{:S(2)}) collective-permute-start(bf16[6,64,256]{2,1,0:T(8,128)(2,1)} %get-tuple-element.32), channel_id=1, source_target_pairs={{0,7},{1,4},{2,5},{3,6},{4,11},{5,8},{6,9},{7,10},{8,15},{9,12},{1... | collective-permute-start | bytes 589832 | tf_op jit(solution)/shard_map/ppermute | solution.py:26
  56.4 43.6 %collective-permute-start.3 = (bf16[6,64,256]{2,1,0:T(8,128)(2,1)}, bf16[6,64,256]{2,1,0:T(8,128)(2,1)S(1)}, u32[]{:S(2)}, u32[]{:S(2)}) collective-permute-start(bf16[6,64,256]{2,1,0:T(8,128)(2,1)} %get-tuple-element.33), channel_id=1, source_target_pairs={{0,1},{1,2},{2,3},{3,0},{4,5},{5,6},{6,7},{7,4},{8,9},{9,10},{10,1... | collective-permute-start | bytes 589832 | tf_op jit(solution)/shard_map/ppermute | solution.py:26
  58.8 41.2 %collective-permute-start.4 = (bf16[6,64,256]{2,1,0:T(8,128)(2,1)}, bf16[6,64,256]{2,1,0:T(8,128)(2,1)S(1)}, u32[]{:S(2)}, u32[]{:S(2)}) collective-permute-start(bf16[6,64,256]{2,1,0:T(8,128)(2,1)} %get-tuple-element.34), channel_id=1, source_target_pairs={{0,3},{1,0},{2,1},{3,2},{4,7},{5,4},{6,5},{7,6},{8,11},{9,8},{10,9... | collective-permute-start | bytes 589832 | tf_op jit(solution)/shard_map/ppermute | solution.py:26
  62.7 37.4 %copy-start.4 = (bf16[6,64,256]{2,1,0:T(8,128)(2,1)}, bf16[6,64,256]{2,1,0:T(8,128)(2,1)S(1)}, u32[]{:S(2)}) copy-start(bf16[6,64,256]{2,1,0:T(8,128)(2,1)S(1)} %collective-permute-done.rest_0_) | copy-start | bytes 589828
  62.7 37.3 %collective-permute-start.5 = (bf16[6,64,256]{2,1,0:T(8,128)(2,1)}, bf16[6,64,256]{2,1,0:T(8,128)(2,1)S(1)}, u32[]{:S(2)}, u32[]{:S(2)}) collective-permute-start(bf16[6,64,256]{2,1,0:T(8,128)(2,1)} %get-tuple-element.35), channel_id=1, source_target_pairs={{0,29},{1,30},{2,31},{3,28},{4,1},{5,2},{6,3},{7,0},{8,5},{9,6},{1... | collective-permute-start | bytes 589832 | tf_op jit(solution)/shard_map/ppermute | solution.py:26
  68.3 31.7 %copy-start.5 = (bf16[6,64,256]{2,1,0:T(8,128)(2,1)}, bf16[6,64,256]{2,1,0:T(8,128)(2,1)S(1)}, u32[]{:S(2)}) copy-start(bf16[6,64,256]{2,1,0:T(8,128)(2,1)S(1)} %collective-permute-done.1.rest_1_) | copy-start | bytes 589828
  68.3 31.7 %collective-permute-start.6 = (bf16[6,64,256]{2,1,0:T(8,128)(2,1)}, bf16[6,64,256]{2,1,0:T(8,128)(2,1)S(1)}, u32[]{:S(2)}, u32[]{:S(2)}) collective-permute-start(bf16[6,64,256]{2,1,0:T(8,128)(2,1)} %get-tuple-element.36), channel_id=1, source_target_pairs={{0,28},{1,29},{2,30},{3,31},{4,0},{5,1},{6,2},{7,3},{8,4},{9,5},{1... | collective-permute-start | bytes 589832 | tf_op jit(solution)/shard_map/ppermute | solution.py:26
  73.3 26.8 %copy-start.6 = (bf16[6,64,256]{2,1,0:T(8,128)(2,1)}, bf16[6,64,256]{2,1,0:T(8,128)(2,1)S(1)}, u32[]{:S(2)}) copy-start(bf16[6,64,256]{2,1,0:T(8,128)(2,1)S(1)} %collective-permute-done.2.rest_2_) | copy-start | bytes 589828
  73.3 26.8 %collective-permute-start.7 = (bf16[6,64,256]{2,1,0:T(8,128)(2,1)}, bf16[6,64,256]{2,1,0:T(8,128)(2,1)S(1)}, u32[]{:S(2)}, u32[]{:S(2)}) collective-permute-start(bf16[6,64,256]{2,1,0:T(8,128)(2,1)} %get-tuple-element.37), channel_id=1, source_target_pairs={{0,31},{1,28},{2,29},{3,30},{4,3},{5,0},{6,1},{7,2},{8,7},{9,4},{1... | collective-permute-start | bytes 589832 | tf_op jit(solution)/shard_map/ppermute | solution.py:26
  97.4 1.7 %copy-start = (bf16[196,64,64]{2,1,0:T(8,128)(2,1)}, bf16[196,64,64]{2,1,0:T(8,128)(2,1)S(1)}, u32[]{:S(2)}) copy-start(bf16[196,64,64]{2,1,0:T(8,128)(2,1)S(1)} %get-tuple-element.28.ga_ref) | copy-start | bytes 4816900
  99.0 1.0 copy-start.1
  100.0 0.7 copy-start.7
  100.0 0.7 copy-start.8
  100.0 0.8 copy-start.9
  100.0 0.8 copy-start.10
  100.1 0.9 copy-start.11
  101.0 34.7 %copy-start.3 = (s32[1,72]{1,0:T(1,128)S(1)}, s32[1,72]{1,0:T(1,128)}, u32[]{:S(2)}) copy-start(s32[1,72]{1,0:T(1,128)} %param.13) | copy-start | bytes 868
  120.1 7.0 %collective-permute-start.8 = (bf16[8,32,128]{2,1,0:T(8,128)(2,1)}, bf16[8,32,128]{2,1,0:T(8,128)(2,1)S(1)}, u32[]{:S(2)}, u32[]{:S(2)}) collective-permute-start(bf16[8,32,128]{2,1,0:T(8,128)(2,1)} %get-tuple-element.38), channel_id=1, source_target_pairs={{0,5},{1,6},{2,7},{3,4},{4,9},{5,10},{6,11},{7,8},{8,13},{9,14},{1... | collective-permute-start | bytes 196616 | tf_op jit(solution)/shard_map/ppermute | solution.py:26
  120.2 9.1 %collective-permute-start.9 = (bf16[8,32,128]{2,1,0:T(8,128)(2,1)}, bf16[8,32,128]{2,1,0:T(8,128)(2,1)S(1)}, u32[]{:S(2)}, u32[]{:S(2)}) collective-permute-start(bf16[8,32,128]{2,1,0:T(8,128)(2,1)} %get-tuple-element.39), channel_id=1, source_target_pairs={{0,4},{1,5},{2,6},{3,7},{4,8},{5,9},{6,10},{7,11},{8,12},{9,13},{1... | collective-permute-start | bytes 196616 | tf_op jit(solution)/shard_map/ppermute | solution.py:26
  121.1 9.8 %collective-permute-start.10 = (bf16[8,32,128]{2,1,0:T(8,128)(2,1)}, bf16[8,32,128]{2,1,0:T(8,128)(2,1)S(1)}, u32[]{:S(2)}, u32[]{:S(2)}) collective-permute-start(bf16[8,32,128]{2,1,0:T(8,128)(2,1)} %get-tuple-element.40), channel_id=1, source_target_pairs={{0,7},{1,4},{2,5},{3,6},{4,11},{5,8},{6,9},{7,10},{8,15},{9,12},{1... | collective-permute-start | bytes 196616 | tf_op jit(solution)/shard_map/ppermute | solution.py:26
  121.1 10.3 %collective-permute-start.11 = (bf16[8,32,128]{2,1,0:T(8,128)(2,1)}, bf16[8,32,128]{2,1,0:T(8,128)(2,1)S(1)}, u32[]{:S(2)}, u32[]{:S(2)}) collective-permute-start(bf16[8,32,128]{2,1,0:T(8,128)(2,1)} %get-tuple-element.41), channel_id=1, source_target_pairs={{0,1},{1,2},{2,3},{3,0},{4,5},{5,6},{6,7},{7,4},{8,9},{9,10},{10,1... | collective-permute-start | bytes 196616 | tf_op jit(solution)/shard_map/ppermute | solution.py:26
  123.3 8.0 %collective-permute-start.12 = (bf16[8,32,128]{2,1,0:T(8,128)(2,1)}, bf16[8,32,128]{2,1,0:T(8,128)(2,1)S(1)}, u32[]{:S(2)}, u32[]{:S(2)}) collective-permute-start(bf16[8,32,128]{2,1,0:T(8,128)(2,1)} %get-tuple-element.43), channel_id=1, source_target_pairs={{0,3},{1,0},{2,1},{3,2},{4,7},{5,4},{6,5},{7,6},{8,11},{9,8},{10,9... | collective-permute-start | bytes 196616 | tf_op jit(solution)/shard_map/ppermute | solution.py:26
  127.2 5.2 %collective-permute-start.13 = (bf16[8,32,128]{2,1,0:T(8,128)(2,1)}, bf16[8,32,128]{2,1,0:T(8,128)(2,1)S(1)}, u32[]{:S(2)}, u32[]{:S(2)}) collective-permute-start(bf16[8,32,128]{2,1,0:T(8,128)(2,1)} %get-tuple-element.44), channel_id=1, source_target_pairs={{0,29},{1,30},{2,31},{3,28},{4,1},{5,2},{6,3},{7,0},{8,5},{9,6},{1... | collective-permute-start | bytes 196616 | tf_op jit(solution)/shard_map/ppermute | solution.py:26
  129.2 4.6 %collective-permute-start.14 = (bf16[8,32,128]{2,1,0:T(8,128)(2,1)}, bf16[8,32,128]{2,1,0:T(8,128)(2,1)S(1)}, u32[]{:S(2)}, u32[]{:S(2)}) collective-permute-start(bf16[8,32,128]{2,1,0:T(8,128)(2,1)} %get-tuple-element.45), channel_id=1, source_target_pairs={{0,28},{1,29},{2,30},{3,31},{4,0},{5,1},{6,2},{7,3},{8,4},{9,5},{1... | collective-permute-start | bytes 196616 | tf_op jit(solution)/shard_map/ppermute | solution.py:26
  130.9 4.8 %collective-permute-start.15 = (bf16[8,32,128]{2,1,0:T(8,128)(2,1)}, bf16[8,32,128]{2,1,0:T(8,128)(2,1)S(1)}, u32[]{:S(2)}, u32[]{:S(2)}) collective-permute-start(bf16[8,32,128]{2,1,0:T(8,128)(2,1)} %get-tuple-element.46), channel_id=1, source_target_pairs={{0,31},{1,28},{2,29},{3,30},{4,3},{5,0},{6,1},{7,2},{8,7},{9,4},{1... | collective-permute-start | bytes 196616 | tf_op jit(solution)/shard_map/ppermute | solution.py:26
  135.7 0.9 copy-start.2

commit v2 on v1

--- a/solution.py
+++ b/solution.py
@@ -10,10 +10,15 @@
 OWN = 128
 OFFSETS = ((-1, -1), (-1, 0), (-1, 1), (0, -1), (0, 1), (1, -1), (1, 0), (1, 1))
 GROUP = 4
+NACC = 4
 SMEM = pl.BlockSpec(memory_space=pltpu.SMEM)
 VMEM = pl.BlockSpec(memory_space=pltpu.VMEM)
 ANY = pl.BlockSpec(memory_space=pl.ANY)
 LIMIT = 48 * 1024 * 1024
+
+
+def resident(x):
+    return pltpu.with_memory_space_constraint(x, pltpu.VMEM)
 
 
 def shifted(x, a, b):
@@ -26,29 +31,22 @@
     return lax.ppermute(x, ("dom", "grp"), pairs)
 
 
-def pack_kernel(send_ref, p_ref, *rest):
-    outs, sems = rest[:-1], rest[-1]
-    copies = [
-        pltpu.make_async_copy(p_ref.at[send_ref[0, p, g]], out.at[g], sems.at[p, g])
-        for p, out in enumerate(outs)
-        for g in range(out.shape[0])
-    ]
-    for copy in copies:
-        copy.start()
-    for copy in copies:
-        copy.wait()
+def pack_kernel(send_ref, p_ref, *outs):
+    for p, out in enumerate(outs):
+        for g in range(out.shape[0]):
+            out[g] = p_ref[send_ref[0, p, g]]
 
 
 def pack(send_rows, p_strips):
     _, neighbours, ghosts = send_rows.shape
     return pl.pallas_call(
         pack_kernel,
-        out_shape=[jax.ShapeDtypeStruct((ghosts,) + p_strips.shape[1:], p_strips.dtype)] * neighbours,
-        in_specs=[SMEM, ANY],
-        out_specs=[ANY] * neighbours,
-        scratch_shapes=[pltpu.SemaphoreType.DMA((neighbours, ghosts))],
+        out_shape=[pltpu.VMEM((ghosts,) + p_strips.shape[1:], p_strips.dtype)] * neighbours,
+        in_specs=[SMEM, VMEM],
+        out_specs=[VMEM] * neighbours,
+        compiler_params=pltpu.CompilerParams(vmem_limit_bytes=LIMIT),
         name="pack",
-    )(send_rows, p_strips)
+    )(send_rows, resident(p_strips))
 
 
 def local_kernel(blocks, pieces, slots, nbr_ref, ap_ref, a_ref, p_ref, sums_ref, ga_ref, pt_ref, info_ref):
@@ -114,7 +112,7 @@
     arrived = rest[: cells - 1]
     sums_out = rest[cells - 1]
     sent = rest[cells : 2 * cells]
-    ghost_ref, tiles_ref, sems = rest[2 * cells :]
+    ghost_ref, *accs = rest[2 * cells :]
     del sums_ref
     ghosts = arrived[0].shape[0]
     elements, _, kb2 = pt_ref.shape
@@ -122,16 +120,11 @@
     kc2 = sums_out.shape[2]
     half = kc2 // 4
     stride = slots + 1
-    copies = [
-        pltpu.make_async_copy(ref, ghost_ref.at[pl.ds(p * ghosts, ghosts)], sems.at[p])
-        for p, ref in enumerate(arrived)
-    ]
-    for copy in copies:
-        copy.start()
-    tiles_ref[...] = jnp.zeros_like(tiles_ref)
+    for p, ref in enumerate(arrived):
+        ghost_ref[pl.ds(p * ghosts, ghosts)] = ref[...]
+    for acc in accs:
+        acc[...] = jnp.zeros_like(acc)
     left = lax.broadcasted_iota(jnp.int32, (kb, kc2), 1) < kc2 // 2
-    for copy in copies:
-        copy.wait()
     count = info_ref[info_ref.shape[0] - 1]
 
     def ghost_group(i, carry):
@@ -152,7 +145,7 @@
     lax.fori_loop(0, (count + GROUP - 1) // GROUP, ghost_group, 0)
     zero = jnp.zeros((kb, kc2), jnp.bfloat16)
 
-    def element(e, carry):
+    def one(e):
         pt = pt_ref[e]
         for pair in range(slots // 2):
             columns = []
@@ -168,13 +161,18 @@
             for k in range(pieces):
                 for u in range(2):
                     t = tile_ref[(e * pieces + k) * slots + 2 * pair + u]
-                    tiles_ref[t] += terms[k * half : (k + 1) * half, u * kc2 : (u + 1) * kc2]
+                    accs[(k * 2 + u) % len(accs)][t] += terms[k * half : (k + 1) * half, u * kc2 : (u + 1) * kc2]
+
+    def element(i, carry):
+        for u in range(4):
+            one(i * 4 + u)
         return carry
 
-    lax.fori_loop(0, elements, element, 0)
+    lax.fori_loop(0, elements // 4, element, 0)
     for cell, out in enumerate(sent):
         count_of = out.shape[0]
-        out[...] = tiles_ref[pl.ds(cell * count_of, count_of)].astype(out.dtype)
+        rows = pl.ds(cell * count_of, count_of)
+        out[...] = functools.reduce(jnp.add, [acc[rows] for acc in accs]).astype(out.dtype)
 
 
 def finish(info, tile_slot, sums, ga, pt, arrived, tiles_total):
@@ -186,22 +184,19 @@
         functools.partial(finish_kernel, pieces, slots, cells),
         out_shape=[pltpu.VMEM(sums.shape, sums.dtype)]
         + [
-            jax.ShapeDtypeStruct(
-                (capacity, half, kc2), jnp.float32 if cell == cells // 2 else jnp.bfloat16
-            )
+            pltpu.VMEM((capacity, half, kc2), jnp.float32 if cell == cells // 2 else jnp.bfloat16)
             for cell in range(cells)
         ],
-        in_specs=[SMEM, SMEM, VMEM, VMEM, VMEM] + [ANY] * (cells - 1),
+        in_specs=[SMEM, SMEM] + [VMEM] * (cells + 2),
         out_specs=[VMEM] * (cells + 1),
         scratch_shapes=[
             pltpu.VMEM(((cells - 1) * arrived[0].shape[0],) + arrived[0].shape[1:], jnp.bfloat16),
-            pltpu.VMEM((tiles_total, half, kc2), jnp.float32),
-            pltpu.SemaphoreType.DMA((cells - 1,)),
-        ],
+        ]
+        + [pltpu.VMEM((tiles_total, half, kc2), jnp.float32)] * NACC,
         input_output_aliases={2: 0},
         compiler_params=pltpu.CompilerParams(vmem_limit_bytes=LIMIT),
         name="finish",
-    )(info, tile_slot.reshape(-1), sums, ga, pt, *arrived)
+    )(info, tile_slot.reshape(-1), sums, resident(ga), resident(pt), *map(resident, arrived))
     return results[1:]
 
 
@@ -231,7 +226,7 @@
         scratch_shapes=[pltpu.VMEM((OWN, half, kc2), jnp.float32)],
         compiler_params=pltpu.CompilerParams(vmem_limit_bytes=LIMIT),
         name="owner_sums",
-    )(owner_map.reshape(-1), *parcels)
+    )(owner_map.reshape(-1), *map(resident, parcels))
 
 
 def body(a_strips, p_strips, nbr_local, ap_slot, tile_slot, send_rows, owner_map):

time: 140 us -> 75.4 us (0.54)
  Pallas kernels: 85.6 us -> 25.6 us
  local copies, waits for them, and re-layouts: 10.2 us -> 6.45 us
    pallas_call x1, Pallas kernels: 49.9 us -> 0.7 us  [pack(): pl.pallas_call(pack_kernel, out_shape=[pltpu.VMEM((ghosts,) + p_strips.sh...]
    pallas_call x1, Pallas kernels: 19.1 us -> 8.3 us  [finish(): pl.pallas_call(functools.partial(finish_kernel, pieces, slots, cells), ou...]
    unnamed x28 -> x8, local copies, waits for them, and re-layouts: 8.15 us -> 4.4 us
  transfers between devices with their start and end apart: 16 -> 16, of which waited for: 8 -> 8; matrix products, arithmetic and copies ran while one was open for 3% -> 6% of each run, Pallas kernels for 10% -> 18%
where the time goes in v2:
time: 75.4 us; the launch traced here: 75 us
  Pallas kernels  25.6 us (34%)
  starting transfers between devices  23.2 us (31%)
  waiting for transfers between devices  19.7 us (26%)
  local copies, waits for them, and re-layouts  6.45 us (9%)
    ppermute x16, starting transfers between devices, shifted(): return lax.ppermute(x, ('dom', 'grp'), pairs)  23.2 us
    ppermute x16, waiting for transfers between devices, shifted(): return lax.ppermute(x, ('dom', 'grp'), pairs)  19.7 us
    pallas_call x1, Pallas kernels, local_part(): pl.pallas_call(functools.partial(local_kernel, blocks, pieces, slots), ou...  13.7 us
    pallas_call x1, Pallas kernels, finish(): pl.pallas_call(functools.partial(finish_kernel, pieces, slots, cells), ou...  8.3 us
    unnamed x8, local copies, waits for them, and re-layouts  4.4 us
    pallas_call x1, Pallas kernels, owner_sums(): pl.pallas_call(owner_kernel, out_shape=jax.ShapeDtypeStruct((2 * half, OW...  2.87 us
  transfers between devices with their start and end apart: 16, of which 8 were waited for; matrix products, arithmetic and copies ran while one was open for 6% of the time, Pallas kernels for 18%

profile of v2, /device:TPU:1, one launch (start us, length us, event | category | flops | bytes accessed | tf_op | source)
XLA Modules:
  0.0 75.0 jit_solution(17641349830594659721)
XLA Ops:
  0.0 0.8 %copy.13.send_ref = s32[1,8,6]{2,1,0:T(8,128)S(1)} copy(s32[1,8,6]{1,0,2:T(1,128)} %param.12) | data formatting | bytes 384 | tf_op args[5]
  0.8 1.2 %copy-done = bf16[32,64,256]{2,1,0:T(8,128)(2,1)S(1)} copy-done((bf16[32,64,256]{2,1,0:T(8,128)(2,1)S(1)}, bf16[32,64,256]{2,1,0:T(8,128)(2,1)}, u32[]{:S(2)}) %copy-start) | copy-done | bytes 1048600
  2.0 0.7 pack.1
  2.7 3.6 %collective-permute-start = (bf16[6,64,256]{2,1,0:T(8,128)(2,1)S(1)}, bf16[6,64,256]{2,1,0:T(8,128)(2,1)S(1)}, u32[]{:S(2)}, u32[]{:S(2)}) collective-permute-start(bf16[6,64,256]{2,1,0:T(8,128)(2,1)S(1)} %get-tuple-element.30), channel_id=1, source_target_pairs={{0,5},{1,6},{2,7},{3,4},{4,9},{5,10},{6,11},{7,8},{8,13},{9,14},{1... | collective-permute-start | bytes 589832 | tf_op jit(solution)/shard_map/ppermute | solution.py:31
  6.3 1.2 %collective-permute-start.1 = (bf16[6,64,256]{2,1,0:T(8,128)(2,1)S(1)}, bf16[6,64,256]{2,1,0:T(8,128)(2,1)S(1)}, u32[]{:S(2)}, u32[]{:S(2)}) collective-permute-start(bf16[6,64,256]{2,1,0:T(8,128)(2,1)S(1)} %get-tuple-element.31), channel_id=1, source_target_pairs={{0,4},{1,5},{2,6},{3,7},{4,8},{5,9},{6,10},{7,11},{8,12},{9,13},{1... | collective-permute-start | bytes 589832 | tf_op jit(solution)/shard_map/ppermute | solution.py:31
  7.5 0.3 collective-permute-start.2
  7.9 2.4 %collective-permute-start.3 = (bf16[6,64,256]{2,1,0:T(8,128)(2,1)S(1)}, bf16[6,64,256]{2,1,0:T(8,128)(2,1)S(1)}, u32[]{:S(2)}, u32[]{:S(2)}) collective-permute-start(bf16[6,64,256]{2,1,0:T(8,128)(2,1)S(1)} %get-tuple-element.33), channel_id=1, source_target_pairs={{0,1},{1,2},{2,3},{3,0},{4,5},{5,6},{6,7},{7,4},{8,9},{9,10},{10,1... | collective-permute-start | bytes 589832 | tf_op jit(solution)/shard_map/ppermute | solution.py:31
  10.3 3.6 %collective-permute-done.rest_0_ = bf16[6,64,256]{2,1,0:T(8,128)(2,1)S(1)} collective-permute-done((bf16[6,64,256]{2,1,0:T(8,128)(2,1)S(1)}, bf16[6,64,256]{2,1,0:T(8,128)(2,1)S(1)}, u32[]{:S(2)}, u32[]{:S(2)}) %collective-permute-start) | collective-permute-done | bytes 196640 | tf_op jit(solution)/shard_map/ppermute | solution.py:31
  13.9 2.0 %collective-permute-start.5 = (bf16[6,64,256]{2,1,0:T(8,128)(2,1)S(1)}, bf16[6,64,256]{2,1,0:T(8,128)(2,1)S(1)}, u32[]{:S(2)}, u32[]{:S(2)}) collective-permute-start(bf16[6,64,256]{2,1,0:T(8,128)(2,1)S(1)} %get-tuple-element.35), channel_id=1, source_target_pairs={{0,29},{1,30},{2,31},{3,28},{4,1},{5,2},{6,3},{7,0},{8,5},{9,6},{1... | collective-permute-start | bytes 589832 | tf_op jit(solution)/shard_map/ppermute | solution.py:31
  15.9 3.6 %collective-permute-done.1.rest_1_ = bf16[6,64,256]{2,1,0:T(8,128)(2,1)S(1)} collective-permute-done((bf16[6,64,256]{2,1,0:T(8,128)(2,1)S(1)}, bf16[6,64,256]{2,1,0:T(8,128)(2,1)S(1)}, u32[]{:S(2)}, u32[]{:S(2)}) %collective-permute-start.1) | collective-permute-done | bytes 196640 | tf_op jit(solution)/shard_map/ppermute | solution.py:31
  19.4 1.0 %collective-permute-start.6 = (bf16[6,64,256]{2,1,0:T(8,128)(2,1)S(1)}, bf16[6,64,256]{2,1,0:T(8,128)(2,1)S(1)}, u32[]{:S(2)}, u32[]{:S(2)}) collective-permute-start(bf16[6,64,256]{2,1,0:T(8,128)(2,1)S(1)} %get-tuple-element.36), channel_id=1, source_target_pairs={{0,28},{1,29},{2,30},{3,31},{4,0},{5,1},{6,2},{7,3},{8,4},{9,5},{1... | collective-permute-start | bytes 589832 | tf_op jit(solution)/shard_map/ppermute | solution.py:31
  20.5 4.1 %collective-permute-done.2.rest_2_ = bf16[6,64,256]{2,1,0:T(8,128)(2,1)S(1)} collective-permute-done((bf16[6,64,256]{2,1,0:T(8,128)(2,1)S(1)}, bf16[6,64,256]{2,1,0:T(8,128)(2,1)S(1)}, u32[]{:S(2)}, u32[]{:S(2)}) %collective-permute-start.2) | collective-permute-done | bytes 196640 | tf_op jit(solution)/shard_map/ppermute | solution.py:31
  24.5 5.9 %collective-permute-start.7 = (bf16[6,64,256]{2,1,0:T(8,128)(2,1)S(1)}, bf16[6,64,256]{2,1,0:T(8,128)(2,1)S(1)}, u32[]{:S(2)}, u32[]{:S(2)}) collective-permute-start(bf16[6,64,256]{2,1,0:T(8,128)(2,1)S(1)} %get-tuple-element.37), channel_id=1, source_target_pairs={{0,31},{1,28},{2,29},{3,30},{4,3},{5,0},{6,1},{7,2},{8,7},{9,4},{1... | collective-permute-start | bytes 589832 | tf_op jit(solution)/shard_map/ppermute | solution.py:31
  30.4 0.8 %copy.10 = s32[32,7]{1,0:T(8,128)S(1)} copy(s32[32,7]{0,1:T(8,128)} %param.9) | data formatting | bytes 1792 | tf_op args[2]
  31.1 0.7 reshape.13.nbr_ref
  31.8 0.8 %copy.12 = s32[32,4,8]{2,1,0:T(4,128)S(1)} copy(s32[32,4,8]{0,2,1:T(8,128)} %param.11) | data formatting | bytes 8192 | tf_op args[4]
  32.6 0.7 reshape.15.tile_ref
  33.3 0.8 %copy.11 = s32[32,7,4]{2,1,0:T(8,128)S(1)} copy(s32[32,7,4]{0,2,1:T(4,128)} %param.10) | data formatting | bytes 7168 | tf_op args[3]
  34.2 0.7 reshape.14.ap_ref
  34.9 13.7 %local_part.1 = (f32[288,64,128]{2,1,0:T(8,128)S(1)}, bf16[196,64,64]{2,1,0:T(8,128)(2,1)S(1)}, bf16[32,128,128]{2,1,0:T(8,128)(2,1)S(1)}, s32[981]{0:T(1024)}) custom-call(s32[224]{0:T(256)} %reshape.13.nbr_ref, s32[896]{0:T(1024)} %reshape.14.ap_ref, bf16[32,64,448]{2,1,0:T(8,128)(2,1)} %a_ref.1, bf16[32,64,256]{2,1,0:T(8,128)(2,1)} %p_ref.3), custom_call_target="tpu_custom_call" | custom-call | tf_op jit(solution)/shard_map/local_part/pallas_call | solution.py:96
  48.6 8.3 %finish.1 = (f32[288,64,128]{2,1,0:T(8,128)S(1)}, bf16[8,32,128]{2,1,0:T(8,128)(2,1)S(1)}, bf16[8,32,128]{2,1,0:T(8,128)(2,1)S(1)}, bf16[8,32,128]{2,1,0:T(8,128...) custom-call(s32[981]{0:T(1024)} %get-tuple-element.26.info_ref, ...), custom_call_target="tpu_custom_call", output_to_operand_aliasing={{0}: (2, {})} | custom-call | tf_op jit(solution)/shard_map/finish/pallas_call | solution.py:183
  57.0 0.9 %collective-permute-start.9 = (bf16[8,32,128]{2,1,0:T(8,128)(2,1)S(1)}, bf16[8,32,128]{2,1,0:T(8,128)(2,1)S(1)}, u32[]{:S(2)}, u32[]{:S(2)}) collective-permute-start(bf16[8,32,128]{2,1,0:T(8,128)(2,1)S(1)} %get-tuple-element.39), channel_id=1, source_target_pairs={{0,4},{1,5},{2,6},{3,7},{4,8},{5,9},{6,10},{7,11},{8,12},{9,13},{1... | collective-permute-start | bytes 196616 | tf_op jit(solution)/shard_map/ppermute | solution.py:31
  57.8 2.3 %collective-permute-start.11 = (bf16[8,32,128]{2,1,0:T(8,128)(2,1)S(1)}, bf16[8,32,128]{2,1,0:T(8,128)(2,1)S(1)}, u32[]{:S(2)}, u32[]{:S(2)}) collective-permute-start(bf16[8,32,128]{2,1,0:T(8,128)(2,1)S(1)} %get-tuple-element.41), channel_id=1, source_target_pairs={{0,1},{1,2},{2,3},{3,0},{4,5},{5,6},{6,7},{7,4},{8,9},{9,10},{10,1... | collective-permute-start | bytes 196616 | tf_op jit(solution)/shard_map/ppermute | solution.py:31
  60.1 3.6 %collective-permute-done.8.rest_0_ = bf16[8,32,128]{2,1,0:T(8,128)(2,1)S(1)} collective-permute-done((bf16[8,32,128]{2,1,0:T(8,128)(2,1)S(1)}, bf16[8,32,128]{2,1,0:T(8,128)(2,1)S(1)}, u32[]{:S(2)}, u32[]{:S(2)}) %collective-permute-start.8) | collective-permute-done | bytes 65568 | tf_op jit(solution)/shard_map/ppermute | solution.py:31
  63.8 2.3 %collective-permute-start.13 = (bf16[8,32,128]{2,1,0:T(8,128)(2,1)S(1)}, bf16[8,32,128]{2,1,0:T(8,128)(2,1)S(1)}, u32[]{:S(2)}, u32[]{:S(2)}) collective-permute-start(bf16[8,32,128]{2,1,0:T(8,128)(2,1)S(1)} %get-tuple-element.44), channel_id=1, source_target_pairs={{0,29},{1,30},{2,31},{3,28},{4,1},{5,2},{6,3},{7,0},{8,5},{9,6},{1... | collective-permute-start | bytes 196616 | tf_op jit(solution)/shard_map/ppermute | solution.py:31
  66.0 0.7 collective-permute-start.14
  66.7 0.8 %collective-permute-done.10.rest_2_ = bf16[8,32,128]{2,1,0:T(8,128)(2,1)S(1)} collective-permute-done((bf16[8,32,128]{2,1,0:T(8,128)(2,1)S(1)}, bf16[8,32,128]{2,1,0:T(8,128)(2,1)S(1)}, u32[]{:S(2)}, u32[]{:S(2)}) %collective-permute-start.10) | collective-permute-done | bytes 65568 | tf_op jit(solution)/shard_map/ppermute | solution.py:31
  67.5 0.7 collective-permute-start.15
  68.2 0.9 %collective-permute-done.13.rest_6_ = bf16[8,32,128]{2,1,0:T(8,128)(2,1)S(1)} collective-permute-done((bf16[8,32,128]{2,1,0:T(8,128)(2,1)S(1)}, bf16[8,32,128]{2,1,0:T(8,128)(2,1)S(1)}, u32[]{:S(2)}, u32[]{:S(2)}) %collective-permute-start.13) | collective-permute-done | bytes 65568 | tf_op jit(solution)/shard_map/ppermute | solution.py:31
  69.1 1.2 %collective-permute-done.14.rest_7_ = bf16[8,32,128]{2,1,0:T(8,128)(2,1)S(1)} collective-permute-done((bf16[8,32,128]{2,1,0:T(8,128)(2,1)S(1)}, bf16[8,32,128]{2,1,0:T(8,128)(2,1)S(1)}, u32[]{:S(2)}, u32[]{:S(2)}) %collective-permute-start.14) | collective-permute-done | bytes 65568 | tf_op jit(solution)/shard_map/ppermute | solution.py:31
  70.3 1.8 %collective-permute-done.15.rest_8_ = bf16[8,32,128]{2,1,0:T(8,128)(2,1)S(1)} collective-permute-done((bf16[8,32,128]{2,1,0:T(8,128)(2,1)S(1)}, bf16[8,32,128]{2,1,0:T(8,128)(2,1)S(1)}, u32[]{:S(2)}, u32[]{:S(2)}) %collective-permute-start.15) | collective-permute-done | bytes 65568 | tf_op jit(solution)/shard_map/ppermute | solution.py:31
  72.1 2.9 %owner_sums.1 = f32[64,8192]{1,0:T(8,128)} custom-call(s32[72]{0:T(128)S(1)} %bitcast.1, bf16[8,32,128]{2,1,0:T(8,128)(2,1)S(1)} %collective-permute-done.8.rest_0_, bf16[8,32,128]{2,1,0:T(8,128)(2,1)S(1)} %collective-permute-done.9.rest_1_, bf16[8,32,128]{2,1,0:T(8,128)(2,1)S(1)} %collective-permute-done.10.rest_2_, ...), custom_call_target="tpu_custom_call" | custom-call | tf_op jit(solution)/shard_map/owner_sums/pallas_call | solution.py:221
  (15 shorter events, 0.1 us)
Async XLA Ops:
  0.8 1.2 %copy-start = (bf16[32,64,256]{2,1,0:T(8,128)(2,1)S(1)}, bf16[32,64,256]{2,1,0:T(8,128)(2,1)}, u32[]{:S(2)}) copy-start(bf16[32,64,256]{2,1,0:T(8,128)(2,1)} %p_ref.3) | copy-start | bytes 3145732
  2.7 11.2 %collective-permute-start = (bf16[6,64,256]{2,1,0:T(8,128)(2,1)S(1)}, bf16[6,64,256]{2,1,0:T(8,128)(2,1)S(1)}, u32[]{:S(2)}, u32[]{:S(2)}) collective-permute-start(bf16[6,64,256]{2,1,0:T(8,128)(2,1)S(1)} %get-tuple-element.30), channel_id=1, source_target_pairs={{0,5},{1,6},{2,7},{3,4},{4,9},{5,10},{6,11},{7,8},{8,13},{9,14},{1... | collective-permute-start | bytes 589832 | tf_op jit(solution)/shard_map/ppermute | solution.py:31
  6.3 13.1 %collective-permute-start.1 = (bf16[6,64,256]{2,1,0:T(8,128)(2,1)S(1)}, bf16[6,64,256]{2,1,0:T(8,128)(2,1)S(1)}, u32[]{:S(2)}, u32[]{:S(2)}) collective-permute-start(bf16[6,64,256]{2,1,0:T(8,128)(2,1)S(1)} %get-tuple-element.31), channel_id=1, source_target_pairs={{0,4},{1,5},{2,6},{3,7},{4,8},{5,9},{6,10},{7,11},{8,12},{9,13},{1... | collective-permute-start | bytes 589832 | tf_op jit(solution)/shard_map/ppermute | solution.py:31
  7.5 17.0 %collective-permute-start.2 = (bf16[6,64,256]{2,1,0:T(8,128)(2,1)S(1)}, bf16[6,64,256]{2,1,0:T(8,128)(2,1)S(1)}, u32[]{:S(2)}, u32[]{:S(2)}) collective-permute-start(bf16[6,64,256]{2,1,0:T(8,128)(2,1)S(1)} %get-tuple-element.32), channel_id=1, source_target_pairs={{0,7},{1,4},{2,5},{3,6},{4,11},{5,8},{6,9},{7,10},{8,15},{9,12},{1... | collective-permute-start | bytes 589832 | tf_op jit(solution)/shard_map/ppermute | solution.py:31
  7.9 40.7 %collective-permute-start.3 = (bf16[6,64,256]{2,1,0:T(8,128)(2,1)S(1)}, bf16[6,64,256]{2,1,0:T(8,128)(2,1)S(1)}, u32[]{:S(2)}, u32[]{:S(2)}) collective-permute-start(bf16[6,64,256]{2,1,0:T(8,128)(2,1)S(1)} %get-tuple-element.33), channel_id=1, source_target_pairs={{0,1},{1,2},{2,3},{3,0},{4,5},{5,6},{6,7},{7,4},{8,9},{9,10},{10,1... | collective-permute-start | bytes 589832 | tf_op jit(solution)/shard_map/ppermute | solution.py:31
  10.2 38.3 %collective-permute-start.4 = (bf16[6,64,256]{2,1,0:T(8,128)(2,1)S(1)}, bf16[6,64,256]{2,1,0:T(8,128)(2,1)S(1)}, u32[]{:S(2)}, u32[]{:S(2)}) collective-permute-start(bf16[6,64,256]{2,1,0:T(8,128)(2,1)S(1)} %get-tuple-element.34), channel_id=1, source_target_pairs={{0,3},{1,0},{2,1},{3,2},{4,7},{5,4},{6,5},{7,6},{8,11},{9,8},{10,9... | collective-permute-start | bytes 589832 | tf_op jit(solution)/shard_map/ppermute | solution.py:31
  13.9 34.7 %collective-permute-start.5 = (bf16[6,64,256]{2,1,0:T(8,128)(2,1)S(1)}, bf16[6,64,256]{2,1,0:T(8,128)(2,1)S(1)}, u32[]{:S(2)}, u32[]{:S(2)}) collective-permute-start(bf16[6,64,256]{2,1,0:T(8,128)(2,1)S(1)} %get-tuple-element.35), channel_id=1, source_target_pairs={{0,29},{1,30},{2,31},{3,28},{4,1},{5,2},{6,3},{7,0},{8,5},{9,6},{1... | collective-permute-start | bytes 589832 | tf_op jit(solution)/shard_map/ppermute | solution.py:31
  19.4 29.1 %collective-permute-start.6 = (bf16[6,64,256]{2,1,0:T(8,128)(2,1)S(1)}, bf16[6,64,256]{2,1,0:T(8,128)(2,1)S(1)}, u32[]{:S(2)}, u32[]{:S(2)}) collective-permute-start(bf16[6,64,256]{2,1,0:T(8,128)(2,1)S(1)} %get-tuple-element.36), channel_id=1, source_target_pairs={{0,28},{1,29},{2,30},{3,31},{4,0},{5,1},{6,2},{7,3},{8,4},{9,5},{1... | collective-permute-start | bytes 589832 | tf_op jit(solution)/shard_map/ppermute | solution.py:31
  24.5 24.1 %collective-permute-start.7 = (bf16[6,64,256]{2,1,0:T(8,128)(2,1)S(1)}, bf16[6,64,256]{2,1,0:T(8,128)(2,1)S(1)}, u32[]{:S(2)}, u32[]{:S(2)}) collective-permute-start(bf16[6,64,256]{2,1,0:T(8,128)(2,1)S(1)} %get-tuple-element.37), channel_id=1, source_target_pairs={{0,31},{1,28},{2,29},{3,30},{4,3},{5,0},{6,1},{7,2},{8,7},{9,4},{1... | collective-permute-start | bytes 589832 | tf_op jit(solution)/shard_map/ppermute | solution.py:31
  48.6 23.5 %copy-start.1 = (s32[1,72]{1,0:T(1,128)S(1)}, s32[1,72]{1,0:T(1,128)}, u32[]{:S(2)}) copy-start(s32[1,72]{1,0:T(1,128)} %param.13) | copy-start | bytes 868
  56.9 6.8 %collective-permute-start.8 = (bf16[8,32,128]{2,1,0:T(8,128)(2,1)S(1)}, bf16[8,32,128]{2,1,0:T(8,128)(2,1)S(1)}, u32[]{:S(2)}, u32[]{:S(2)}) collective-permute-start(bf16[8,32,128]{2,1,0:T(8,128)(2,1)S(1)} %get-tuple-element.38), channel_id=1, source_target_pairs={{0,5},{1,6},{2,7},{3,4},{4,9},{5,10},{6,11},{7,8},{8,13},{9,14},{1... | collective-permute-start | bytes 196616 | tf_op jit(solution)/shard_map/ppermute | solution.py:31
  57.0 9.0 %collective-permute-start.9 = (bf16[8,32,128]{2,1,0:T(8,128)(2,1)S(1)}, bf16[8,32,128]{2,1,0:T(8,128)(2,1)S(1)}, u32[]{:S(2)}, u32[]{:S(2)}) collective-permute-start(bf16[8,32,128]{2,1,0:T(8,128)(2,1)S(1)} %get-tuple-element.39), channel_id=1, source_target_pairs={{0,4},{1,5},{2,6},{3,7},{4,8},{5,9},{6,10},{7,11},{8,12},{9,13},{1... | collective-permute-start | bytes 196616 | tf_op jit(solution)/shard_map/ppermute | solution.py:31
  57.8 9.7 %collective-permute-start.10 = (bf16[8,32,128]{2,1,0:T(8,128)(2,1)S(1)}, bf16[8,32,128]{2,1,0:T(8,128)(2,1)S(1)}, u32[]{:S(2)}, u32[]{:S(2)}) collective-permute-start(bf16[8,32,128]{2,1,0:T(8,128)(2,1)S(1)} %get-tuple-element.40), channel_id=1, source_target_pairs={{0,7},{1,4},{2,5},{3,6},{4,11},{5,8},{6,9},{7,10},{8,15},{9,12},{1... | collective-permute-start | bytes 196616 | tf_op jit(solution)/shard_map/ppermute | solution.py:31
  57.8 10.3 %collective-permute-start.11 = (bf16[8,32,128]{2,1,0:T(8,128)(2,1)S(1)}, bf16[8,32,128]{2,1,0:T(8,128)(2,1)S(1)}, u32[]{:S(2)}, u32[]{:S(2)}) collective-permute-start(bf16[8,32,128]{2,1,0:T(8,128)(2,1)S(1)} %get-tuple-element.41), channel_id=1, source_target_pairs={{0,1},{1,2},{2,3},{3,0},{4,5},{5,6},{6,7},{7,4},{8,9},{9,10},{10,1... | collective-permute-start | bytes 196616 | tf_op jit(solution)/shard_map/ppermute | solution.py:31
  60.1 8.1 %collective-permute-start.12 = (bf16[8,32,128]{2,1,0:T(8,128)(2,1)S(1)}, bf16[8,32,128]{2,1,0:T(8,128)(2,1)S(1)}, u32[]{:S(2)}, u32[]{:S(2)}) collective-permute-start(bf16[8,32,128]{2,1,0:T(8,128)(2,1)S(1)} %get-tuple-element.43), channel_id=1, source_target_pairs={{0,3},{1,0},{2,1},{3,2},{4,7},{5,4},{6,5},{7,6},{8,11},{9,8},{10,9... | collective-permute-start | bytes 196616 | tf_op jit(solution)/shard_map/ppermute | solution.py:31
  63.8 5.3 %collective-permute-start.13 = (bf16[8,32,128]{2,1,0:T(8,128)(2,1)S(1)}, bf16[8,32,128]{2,1,0:T(8,128)(2,1)S(1)}, u32[]{:S(2)}, u32[]{:S(2)}) collective-permute-start(bf16[8,32,128]{2,1,0:T(8,128)(2,1)S(1)} %get-tuple-element.44), channel_id=1, source_target_pairs={{0,29},{1,30},{2,31},{3,28},{4,1},{5,2},{6,3},{7,0},{8,5},{9,6},{1... | collective-permute-start | bytes 196616 | tf_op jit(solution)/shard_map/ppermute | solution.py:31
  66.0 4.3 %collective-permute-start.14 = (bf16[8,32,128]{2,1,0:T(8,128)(2,1)S(1)}, bf16[8,32,128]{2,1,0:T(8,128)(2,1)S(1)}, u32[]{:S(2)}, u32[]{:S(2)}) collective-permute-start(bf16[8,32,128]{2,1,0:T(8,128)(2,1)S(1)} %get-tuple-element.45), channel_id=1, source_target_pairs={{0,28},{1,29},{2,30},{3,31},{4,0},{5,1},{6,2},{7,3},{8,4},{9,5},{1... | collective-permute-start | bytes 196616 | tf_op jit(solution)/shard_map/ppermute | solution.py:31
  67.5 4.6 %collective-permute-start.15 = (bf16[8,32,128]{2,1,0:T(8,128)(2,1)S(1)}, bf16[8,32,128]{2,1,0:T(8,128)(2,1)S(1)}, u32[]{:S(2)}, u32[]{:S(2)}) collective-permute-start(bf16[8,32,128]{2,1,0:T(8,128)(2,1)S(1)} %get-tuple-element.46), channel_id=1, source_target_pairs={{0,31},{1,28},{2,29},{3,30},{4,3},{5,0},{6,1},{7,2},{8,7},{9,4},{1... | collective-permute-start | bytes 196616 | tf_op jit(solution)/shard_map/ppermute | solution.py:31

commit v3 on v1

v3 whole, which is shorter than its diff:
```python
import functools

import jax
import jax.numpy as jnp
from jax import lax
from jax.experimental import pallas as pl
from jax.experimental.pallas import tpu as pltpu
from jax.sharding import PartitionSpec as P

OWN = 128
GROUP = 4
STEP = 4
SUMS = 4
SMEM = pl.BlockSpec(memory_space=pltpu.SMEM)
VMEM = pl.BlockSpec(memory_space=pltpu.VMEM)
ANY = pl.BlockSpec(memory_space=pl.ANY)
PARAMS = pltpu.CompilerParams(vmem_limit_bytes=12 * 1024 * 1024)


def moved(x, a, along):
    domains, groups = lax.axis_size("dom"), lax.axis_size("grp")

    def target(j):
        if along == "pair":
            return j ^ 1
        if along == "far":
            return (j - 1 + 2 * (j % 2)) % groups
        return j

    pairs = [
        (i * groups + j, (i + a) % domains * groups + target(j))
        for i in range(domains)
        for j in range(groups)
    ]
    return lax.ppermute(x, ("dom", "grp"), pairs)


def resident(x):
    return pltpu.with_memory_space_constraint(x, pltpu.VMEM)


def exchange(parts):
    pair, up_far, down_far, far, up, down = parts
    size = up.shape[0]
    pair = moved(pair, 0, "pair")
    up = moved(jnp.concatenate([up, pair[size : 2 * size]]), 1, "own")
    down = moved(jnp.concatenate([down, pair[2 * size :]]), -1, "own")
    return pair, moved(up_far, 1, "far"), moved(down_far, -1, "far"), moved(far, 0, "far"), up, down


def pair_offset():
    return 1 - 2 * (lax.axis_index("grp") % 2)


def sent_cells(offset):
    return (
        (4 + offset, 7 + offset, 1 + offset),
        (7 - offset,),
        (1 - offset,),
        (4 - offset,),
        (7,),
        (1,),
    )


def arrived_cells(offset):
    return ((4 + offset,), (1 - offset,), (7 - offset,), (4 - offset,), (1, 1 + offset), (7, 7 + offset))


EARLY, LATE = (0, 1, 2, 3), (4, 5)


def neighbour_of(cell):
    return cell - jnp.where(cell > 4, 1, 0)


def pack_kernel(send_ref, p_ref, *rest):
    outs, sems = rest[:-1], rest[-1]
    ghosts = send_ref.shape[0]
    copies = []
    for out, cells in zip(outs, sent_cells(pair_offset())):
        for at, cell in enumerate(cells):
            p = neighbour_of(cell)
            for g in range(ghosts):
                copies.append(
                    pltpu.make_async_copy(
                        p_ref.at[send_ref[g, 0, p]], out.at[at * ghosts + g], sems.at[len(copies)]
                    )
                )
    for copy in copies:
        copy.start()
    for copy in copies:
        copy.wait()


def pack(send_rows, p_strips):
    ghosts = send_rows.shape[2]
    return pl.pallas_call(
        pack_kernel,
        out_shape=[
            pltpu.VMEM((len(cells) * ghosts,) + p_strips.shape[1:], p_strips.dtype)
            for cells in sent_cells(1)
        ],
        in_specs=[SMEM, ANY],
        out_specs=[VMEM] * 6,
        scratch_shapes=[pltpu.SemaphoreType.DMA((8 * ghosts,))],
        compiler_params=PARAMS,
        name="pack",
    )(send_rows.transpose(2, 0, 1), p_strips)


def local_kernel(ghosts, slots, nbr_ref, ap_ref, a_ref, p_ref, *rest):
    even_ref, odd_ref, ga_ref, pt_ref, info_ref, order_ref, late_ref = rest
    blocks, pieces, elements = ap_ref.shape
    kb = a_ref.shape[1]
    kc = p_ref.shape[2] // pieces
    stride = slots + 1
    capacity = ga_ref.shape[0] // 2
    offset = pair_offset()
    for cell in (0, 1, 2, 3, 5, 6, 7, 8):
        late = jnp.int32(cell // 3 != 1)
        if cell % 3 != 1:
            late = late * (cell % 3 - 1 == offset).astype(jnp.int32)
        for g in range(ghosts):
            late_ref[(cell - (cell > 4)) * ghosts + g] = late

    def element(e, carry):
        early_count, late_count, early_elements, late_elements = carry
        for ref in (even_ref, odd_ref):
            ref[pl.ds(e * stride, stride)] = jnp.zeros((stride,) + ref.shape[1:], jnp.float32)
        waits = jnp.int32(0)
        for j in range(blocks):
            n = nbr_ref[j, e]
            ghost = n >= elements
            a = a_ref[e, :, j * kb : (j + 1) * kb]
            product = jnp.dot(
                a, p_ref[jnp.where(ghost, 0, n)], preferred_element_type=jnp.float32
            )
            for k in range(pieces):
                row = e * stride + jnp.where(ghost, slots, ap_ref[j, k, e])
                piece = product[:, (k // 2) * 2 * kc : (k // 2 + 1) * 2 * kc]
                ref = odd_ref if k % 2 else even_ref
                ref[row] += piece
            if j > 0:
                late = late_ref[jnp.where(ghost, n - elements, 0)]
                at = jnp.where(late == 1, capacity + late_count, early_count)
                for k in range(pieces):
                    info_ref[at * (pieces + 1) + k] = e * stride + ap_ref[j, k, e]
                info_ref[at * (pieces + 1) + pieces] = n - elements
                ga_ref[at] = a
                is_ghost = ghost.astype(jnp.int32)
                late_count += is_ghost * late
                early_count += is_ghost * (1 - late)
                waits = jnp.maximum(waits, is_ghost * late)
        order_ref[jnp.where(waits == 1, elements - 1 - late_elements, early_elements)] = e
        pt = p_ref[e].astype(jnp.float32).T.reshape(pieces, 2, kc // 2, kb)
        pt_ref[e, :, :kb] = pt[:, 0].reshape(pieces * kc // 2, kb).astype(jnp.bfloat16)
        pt_ref[e, :, kb:] = pt[:, 1].reshape(pieces * kc // 2, kb).astype(jnp.bfloat16)
        return early_count, late_count, early_elements + 1 - waits, late_elements + waits

    zero = jnp.int32(0)
    early_count, late_count, early_elements, _ = lax.fori_loop(
        0, elements, element, (zero, zero, zero, zero)
    )
    for start in (early_count, capacity + late_count):
        for u in range(GROUP):
            for k in range(pieces):
                info_ref[(start + u) * (pieces + 1) + k] = slots
            info_ref[(start + u) * (pieces + 1) + pieces] = 0
    order_ref[elements] = early_elements // STEP
    order_ref[elements + 1] = (early_count + GROUP - 1) // GROUP
    order_ref[elements + 2] = (late_count + GROUP - 1) // GROUP


def local_part(a_strips, p_strips, nbr_local, ap_slot, slots, ghosts):
    elements, kb, _ = a_strips.shape
    blocks, pieces = ap_slot.shape[1:]
    kc = p_strips.shape[2] // pieces
    capacity = elements * (blocks - 1) + GROUP
    sums = pltpu.VMEM((elements * (slots + 1), kb, 2 * kc), jnp.float32)
    return pl.pallas_call(
        functools.partial(local_kernel, ghosts, slots),
        out_shape=[
            sums,
            sums,
            pltpu.VMEM((2 * capacity, kb, kb), jnp.bfloat16),
            pltpu.VMEM((elements, pieces * kc // 2, 2 * kb), jnp.bfloat16),
            jax.ShapeDtypeStruct((2 * capacity * (pieces + 1),), jnp.int32),
            jax.ShapeDtypeStruct((elements + 3,), jnp.int32),
        ],
        in_specs=[SMEM, SMEM, VMEM, VMEM],
        out_specs=[VMEM] * 4 + [SMEM] * 2,
        scratch_shapes=[pltpu.SMEM((8 * ghosts,), jnp.int32)],
        compiler_params=PARAMS,
        cost_estimate=pl.CostEstimate(flops=5 * 10**9, bytes_accessed=10**7, transcendentals=0),
        name="local_part",
    )(nbr_local.T, ap_slot.transpose(1, 2, 0), a_strips, p_strips)


def finish_kernel(late, info_ref, order_ref, tile_ref, ga_ref, pt_ref, *rest):
    parts = LATE if late else EARLY
    arrived, rest = rest[: len(parts)], rest[len(parts) :]
    rest = rest[2 + SUMS * late :]
    even_ref, odd_ref, *tiles = rest[: 2 + SUMS]
    sent, ghost_ref = rest[2 + SUMS : -1], rest[-1]
    pieces, slots, elements = tile_ref.shape
    kb, kc2 = even_ref.shape[1:]
    half = kc2 // 4
    stride = slots + 1
    ghosts = ghost_ref.shape[0] // 8
    first = ga_ref.shape[0] // 2 if late else 0
    offset = pair_offset()
    for part, ref in zip(parts, arrived):
        for at, cell in enumerate(arrived_cells(offset)[part]):
            rows = pl.ds(neighbour_of(cell) * ghosts, ghosts)
            ghost_ref[rows] = ref[at * ghosts : (at + 1) * ghosts]
    if not late:
        for ref in tiles:
            ref[...] = jnp.zeros_like(ref)
    left = lax.broadcasted_iota(jnp.int32, (kb, kc2), 1) < kc2 // 2

    def ghost_group(i, carry):
        for u in range(GROUP):
            at = first + i * GROUP + u
            product = jnp.dot(
                ga_ref[at],
                ghost_ref[info_ref[at * (pieces + 1) + pieces]],
                preferred_element_type=jnp.float32,
            )
            for k in range(pieces):
                ref = odd_ref if k % 2 else even_ref
                ref[info_ref[at * (pieces + 1) + k]] += product[
                    :, (k // 2) * kc2 : (k // 2 + 1) * kc2
                ]
        return carry

    lax.fori_loop(0, order_ref[elements + 1 + late], ghost_group, 0)
    zero = jnp.zeros((kb, kc2), jnp.bfloat16)

    def one(e):
        pt = pt_ref[e]
        for pair in range(slots // 2):
            columns = []
            for q in (2 * pair, 2 * pair + 1):
                x = jnp.where(left, even_ref[e * stride + q], odd_ref[e * stride + q])
                y = (x + pltpu.roll(x, kc2 // 2, 1)).astype(jnp.bfloat16)
                columns.append(
                    jnp.concatenate([jnp.where(left, y, zero), jnp.where(left, zero, y)], axis=0)
                )
            terms = jnp.dot(
                pt, jnp.concatenate(columns, axis=1), preferred_element_type=jnp.float32
            )
            for k in range(pieces):
                for u in range(2):
                    ref = tiles[(2 * k + u) % SUMS]
                    ref[tile_ref[k, 2 * pair + u, e]] += terms[
                        k * half : (k + 1) * half, u * kc2 : (u + 1) * kc2
                    ]

    def step(i, carry):
        for u in range(STEP):
            one(order_ref[i * STEP + u])
        return carry

    early_steps = order_ref[elements]
    if not late:
        lax.fori_loop(0, early_steps, step, 0)
        return
    lax.fori_loop(early_steps, elements // STEP, step, 0)
    capacity = sent[-1].shape[0]

    def total(cell):
        rows = pl.ds(cell * capacity, capacity)
        return functools.reduce(jnp.add, [ref[rows] for ref in tiles])

    for out, cells in zip(sent, sent_cells(offset)):
        for at, cell in enumerate(cells):
            out[at * capacity : (at + 1) * capacity] = total(cell).astype(out.dtype)
    sent[-1][...] = total(4)


def finish(late, info, order, tile_slot, ga, pt, arrived, sums, tiles_total):
    parts = LATE if late else EARLY
    kb, kc2 = sums[0].shape[1:]
    half = kc2 // 4
    capacity = tiles_total // 9
    out_shape = [pltpu.VMEM(x.shape, x.dtype) for x in sums[:2]]
    out_shape += [pltpu.VMEM((tiles_total, half, kc2), jnp.float32)] * SUMS
    if late:
        out_shape += [
            pltpu.VMEM((len(cells) * capacity, half, kc2), jnp.bfloat16) for cells in sent_cells(1)
        ]
        out_shape += [pltpu.VMEM((capacity, half, kc2), jnp.float32)]
    ghost = arrived[0].shape[1:]
    inputs = 5 + len(parts)
    return pl.pallas_call(
        functools.partial(finish_kernel, late),
        out_shape=out_shape,
        in_specs=[SMEM] * 3 + [VMEM] * (2 + len(parts) + len(sums)),
        out_specs=[VMEM] * len(out_shape),
        scratch_shapes=[pltpu.VMEM((8 * (arrived[3].shape[0]),) + ghost, jnp.bfloat16)],
        input_output_aliases={inputs + i: i for i in range(len(sums))},
        compiler_params=PARAMS,
        cost_estimate=pl.CostEstimate(flops=2 * 10**9, bytes_accessed=10**6, transcendentals=0),
        name="late_part" if late else "early_part",
    )(
        info,
        order,
        tile_slot.transpose(1, 2, 0),
        resident(ga),
        resident(pt),
        *(resident(arrived[part]) for part in parts),
        *sums,
    )


def owner_kernel(owner_ref, *rest):
    own, parcels, out_ref, tiles_ref = rest[0], rest[1:-2], rest[-2], rest[-1]
    tiles_ref[...] = jnp.zeros_like(tiles_ref)
    owned, half, kc2 = tiles_ref.shape
    capacity = own.shape[0]

    def add(cell, parcel, at):
        for g in range(capacity):
            tiles_ref[owner_ref[0, cell * capacity + g]] += parcel[at * capacity + g].astype(
                jnp.float32
            )

    add(4, own, 0)
    for parcel, cells in zip(parcels, arrived_cells(pair_offset())):
        for at, cell in enumerate(cells):
            add(cell, parcel, at)
    left = lax.broadcasted_iota(jnp.int32, (half, kc2), 1) < kc2 // 2
    for i in range(owned // 2):
        first, second = tiles_ref[2 * i], tiles_ref[2 * i + 1]
        columns = pl.ds(i * kc2, kc2)
        out_ref[:half, columns] = jnp.where(left, first, pltpu.roll(second, kc2 // 2, 1))
        out_ref[half:, columns] = jnp.where(left, pltpu.roll(first, kc2 // 2, 1), second)


def owner_sums(owner_map, own, parcels):
    _, half, kc2 = own.shape
    return pl.pallas_call(
        owner_kernel,
        out_shape=jax.ShapeDtypeStruct((2 * half, OWN * kc2 // 2), jnp.float32),
        in_specs=[SMEM] + [VMEM] * 7,
        out_specs=VMEM,
        scratch_shapes=[pltpu.VMEM((OWN, half, kc2), jnp.float32)],
        compiler_params=PARAMS,
        name="owner_sums",
    )(owner_map, resident(own), *map(resident, parcels))


def body(a_strips, p_strips, nbr_local, ap_slot, tile_slot, send_rows, owner_map):
    tiles_total = owner_map.shape[1]
    arrived = exchange(pack(send_rows, p_strips))
    *sums, ga, pt, info, order = local_part(
        a_strips, p_strips, nbr_local, ap_slot, tile_slot.shape[2], send_rows.shape[2]
    )
    sums = finish(False, info, order, tile_slot, ga, pt, arrived, sums, tiles_total)
    results = finish(True, info, order, tile_slot, ga, pt, arrived, sums, tiles_total)
    *parcels, own = results[2 + SUMS :]
    return owner_sums(owner_map, own, exchange(parcels))


def solution(mesh):
    placed = (
        P(("dom", "grp"), None, None),
        P(("dom", "grp"), None, None),
        P(("dom", "grp"), None),
        P(("dom", "grp"), None, None),
        P(("dom", "grp"), None, None),
        P(("dom", "grp"), None, None),
        P(("dom", "grp"), None),
    )
    return jax.shard_map(
        body, mesh=mesh, in_specs=placed, out_specs=P(None, ("dom", "grp")), check_vma=False
    )
```

time: 140 us -> 62.9 us (0.45)
  Pallas kernels: 85.6 us -> 27.4 us
  waiting for transfers between devices: 20.8 us -> 8.95 us
  local copies, waits for them, and re-layouts: 10.2 us -> 1.97 us
    pallas_call x3 -> x4, Pallas kernels: 82.7 us -> 24.5 us  [the longest x1 11.6 us: local_part(): pl.pallas_call(functools.partial(local_kernel, ghosts, slots), out_shape=...]
    ppermute x16 -> x12, waiting for transfers between devices: 20.8 us -> 8.95 us  [moved(): return lax.ppermute(x, ('dom', 'grp'), pairs)]
    unnamed x28 -> x16, local copies, waits for them, and re-layouts: 8.15 us -> 1.93 us
    reshape x3 -> x0, local copies, waits for them, and re-layouts: 2.1 us -> none  [the longest x1 0.71 us: finish(): tile_slot.reshape(-1)]
    ppermute x16 -> x12, starting transfers between devices: 22.6 us -> 23.5 us  [moved(): return lax.ppermute(x, ('dom', 'grp'), pairs)]
  transfers between devices with their start and end apart: 16 -> 12, of which waited for: 8 -> 5; matrix products, arithmetic and copies ran while one was open for 3% -> 0% of each run, Pallas kernels for 10% -> 25%
where the time goes in v3:
time: 62.9 us; the launch traced here: 62.1 us
  Pallas kernels  27.4 us (44%)
  starting transfers between devices  23.5 us (37%)
  waiting for transfers between devices  8.95 us (14%)
  local copies, waits for them, and re-layouts  1.97 us (3%)
    ppermute x12, starting transfers between devices, moved(): return lax.ppermute(x, ('dom', 'grp'), pairs)  23.5 us
    pallas_call x1, Pallas kernels, local_part(): pl.pallas_call(functools.partial(local_kernel, ghosts, slots), out_shape=...  11.6 us
    pallas_call x2, Pallas kernels, finish(): pl.pallas_call(functools.partial(finish_kernel, late), out_shape=out_shap...  9.34 us
    ppermute x12, waiting for transfers between devices, moved(): return lax.ppermute(x, ('dom', 'grp'), pairs)  8.95 us
    pallas_call x1, Pallas kernels, pack(): pl.pallas_call(pack_kernel, out_shape=[pltpu.VMEM((len(cells) * ghosts,)...  3.56 us
    pallas_call x1, Pallas kernels, owner_sums(): pl.pallas_call(owner_kernel, out_shape=jax.ShapeDtypeStruct((2 * half, OW...  2.89 us
    unnamed x16, local copies, waits for them, and re-layouts  1.93 us
  transfers between devices with their start and end apart: 12, of which 5 were waited for; matrix products, arithmetic and copies ran while one was open for 0% of the time, Pallas kernels for 25%

profile of v3, /device:TPU:1, one launch (start us, length us, event | category | flops | bytes accessed | tf_op | source)
XLA Modules:
  0.0 62.1 jit_solution(12639621993873154940)
XLA Ops:
  0.0 1.2 %copy-done = bf16[32,64,256]{2,1,0:T(8,128)(2,1)S(1)} copy-done((bf16[32,64,256]{2,1,0:T(8,128)(2,1)S(1)}, bf16[32,64,256]{2,1,0:T(8,128)(2,1)}, u32[]{:S(2)}) %copy-start) | copy-done | bytes 1048600
  1.2 0.7 %copy-done.3 = s32[1,8,6]{1,0,2:T(1,128)S(1)} copy-done((s32[1,8,6]{1,0,2:T(1,128)S(1)}, s32[1,8,6]{1,0,2:T(1,128)}, u32[]{:S(2)}) %copy-start.3) | copy-done | bytes 216
  1.9 3.6 %pack.1 = (bf16[18,64,256]{2,1,0:T(8,128)(2,1)S(1)}, bf16[6,64,256]{2,1,0:T(8,128)(2,1)S(1)}, bf16[6,64,256]{2,1,0:T(8,128)(2,1)S(1)}, bf16[6,64,256]{2,1,0:T(8,...) custom-call(s32[6,1,8]{2,1,0:T(1,128)S(1)} %bitcast.6, bf16[32,64,256]{2,1,0:T(8,128)(2,1)S(1)} %copy-done), custom_call_target="tpu_custom_call" | custom-call | tf_op jit(solution)/shard_map/pack/pallas_call | solution.py:98
  5.5 0.1 collective-permute-start
  5.6 3.6 %collective-permute-start.3 = (bf16[6,64,256]{2,1,0:T(8,128)(2,1)S(1)}, bf16[6,64,256]{2,1,0:T(8,128)(2,1)S(1)}, u32[]{:S(2)}, u32[]{:S(2)}) collective-permute-start(bf16[6,64,256]{2,1,0:T(8,128)(2,1)S(1)} %get-tuple-element.37), channel_id=1, source_target_pairs={{0,7},{1,6},{2,5},{3,4},{4,11},{5,10},{6,9},{7,8},{8,15},{9,14},{1... | collective-permute-start | bytes 589832 | tf_op jit(solution)/shard_map/ppermute | solution.py:35
  9.2 3.1 %collective-permute-start.4 = (bf16[6,64,256]{2,1,0:T(8,128)(2,1)S(1)}, bf16[6,64,256]{2,1,0:T(8,128)(2,1)S(1)}, u32[]{:S(2)}, u32[]{:S(2)}) collective-permute-start(bf16[6,64,256]{2,1,0:T(8,128)(2,1)S(1)} %get-tuple-element.38), channel_id=1, source_target_pairs={{0,31},{1,30},{2,29},{3,28},{4,3},{5,2},{6,1},{7,0},{8,7},{9,6},{1... | collective-permute-start | bytes 589832 | tf_op jit(solution)/shard_map/ppermute | solution.py:35
  12.3 1.3 %collective-permute-start.5 = (bf16[6,64,256]{2,1,0:T(8,128)(2,1)S(1)}, bf16[6,64,256]{2,1,0:T(8,128)(2,1)S(1)}, u32[]{:S(2)}, u32[]{:S(2)}) collective-permute-start(bf16[6,64,256]{2,1,0:T(8,128)(2,1)S(1)} %get-tuple-element.39), channel_id=1, source_target_pairs={{0,3},{1,2},{2,1},{3,0},{4,7},{5,6},{6,5},{7,4},{8,11},{9,10},{10,... | collective-permute-start | bytes 589832 | tf_op jit(solution)/shard_map/ppermute | solution.py:35
  13.6 0.0 collective-permute-done.rest_0_
  13.6 0.1 collective-permute-start.1
  13.8 4.2 %collective-permute-start.2 = (bf16[12,64,256]{2,1,0:T(8,128)(2,1)S(1)}, bf16[12,64,256]{2,1,0:T(8,128)(2,1)S(1)}, u32[]{:S(2)}, u32[]{:S(2)}) collective-permute-start(bf16[12,64,256]{2,1,0:T(8,128)(2,1)S(1)} %pad_maximum_fusion.1), channel_id=1, source_target_pairs={{0,28},{1,29},{2,30},{3,31},{4,0},{5,1},{6,2},{7,3},{8,4},{9,5},{1... | collective-permute-start | bytes 1179656 | tf_op jit(solution)/shard_map/ppermute | solution.py:35
  18.0 0.0 copy-start.2
  18.0 11.6 %local_part.1 = (f32[288,64,128]{2,1,0:T(8,128)S(1)}, f32[288,64,128]{2,1,0:T(8,128)S(1)}, bf16[392,64,64]{2,1,0:T(8,128)(2,1)S(1)}, bf16[32,128,128]{2,1,0:T(8,...) custom-call(s32[7,32]{1,0:T(8,128)S(1)} %bitcast.8, s32[7,4,32]{2,1,0:T(4,128)S(1)} %bitcast.7, ...), custom_call_target="tpu_custom_call" | custom-call | flops 5000000000 | bytes 10000000 | tf_op jit(solution)/shard_map/local_part/pallas_call | solution.py:181
  29.6 0.0 collective-permute-done.3.rest_1_
  29.6 0.0 collective-permute-done.4.rest_2_
  29.6 0.0 collective-permute-done.5.rest_3_
  29.7 4.1 %early_part.1 = (f32[288,64,128]{2,1,0:T(8,128)S(1)}, f32[288,64,128]{2,1,0:T(8,128)S(1)}, f32[72,32,128]{2,1,0:T(8,128)S(1)}, f32[72,32,128]{2,1,0:T(8,128)S(1)...) custom-call(s32[1960]{0:T(1024)S(1)} %get-tuple-element.30.info_ref, ...), custom_call_target="tpu_custom_call", output_to_operand_aliasing={{0}: (9, {}), {1}: (10, {})} | custom-call | flops 2000000000 | bytes 1000000 | tf_op jit(solution)/shard_map/early_part/pallas_call | solution.py:296
  33.8 1.1 %collective-permute-done.1.rest_0_ = bf16[12,64,256]{2,1,0:T(8,128)(2,1)S(1)} collective-permute-done((bf16[12,64,256]{2,1,0:T(8,128)(2,1)S(1)}, bf16[12,64,256]{2,1,0:T(8,128)(2,1)S(1)}, u32[]{:S(2)}, u32[]{:S(2)}) %collective-permute-start.1) | collective-permute-done | bytes 393248 | tf_op jit(solution)/shard_map/ppermute | solution.py:35
  34.9 3.4 %collective-permute-done.2.rest_1_ = bf16[12,64,256]{2,1,0:T(8,128)(2,1)S(1)} collective-permute-done((bf16[12,64,256]{2,1,0:T(8,128)(2,1)S(1)}, bf16[12,64,256]{2,1,0:T(8,128)(2,1)S(1)}, u32[]{:S(2)}, u32[]{:S(2)}) %collective-permute-start.2) | collective-permute-done | bytes 393248 | tf_op jit(solution)/shard_map/ppermute | solution.py:35
  38.3 5.2 %late_part.1 = (f32[288,64,128]{2,1,0:T(8,128)S(1)}, f32[288,64,128]{2,1,0:T(8,128)S(1)}, f32[72,32,128]{2,1,0:T(8,128)S(1)}, f32[72,32,128]{2,1,0:T(8,128)S(1)}...) custom-call(s32[1960]{0:T(1024)S(1)} %get-tuple-element.30.info_ref,, ...), custom_call_target="tpu_custom_call", output_to_operand_aliasing={{0}: (7, {}), {1}: (8, {}), {2}: (9, {}), {3}: (10, {}), {4... | custom-call | flops 2000000000 | bytes 1000000 | tf_op jit(solution)/shard_map/late_part/pallas_call | solution.py:296
  43.5 0.5 collective-permute-start.6
  44.1 1.1 %collective-permute-done.6.rest_1_ = bf16[24,32,128]{2,1,0:T(8,128)(2,1)S(1)} collective-permute-done((bf16[24,32,128]{2,1,0:T(8,128)(2,1)S(1)}, bf16[24,32,128]{2,1,0:T(8,128)(2,1)S(1)}, u32[]{:S(2)}, u32[]{:S(2)}) %collective-permute-start.6) | collective-permute-done | bytes 196640 | tf_op jit(solution)/shard_map/ppermute | solution.py:35
  45.2 0.1 collective-permute-start.10
  45.3 4.2 %collective-permute-start.11 = (bf16[16,32,128]{2,1,0:T(8,128)(2,1)S(1)}, bf16[16,32,128]{2,1,0:T(8,128)(2,1)S(1)}, u32[]{:S(2)}, u32[]{:S(2)}) collective-permute-start(bf16[16,32,128]{2,1,0:T(8,128)(2,1)S(1)} %pad_maximum_fusion.3), channel_id=1, source_target_pairs={{0,28},{1,29},{2,30},{3,31},{4,0},{5,1},{6,2},{7,3},{8,4},{9,5},{1... | collective-permute-start | bytes 393224 | tf_op jit(solution)/shard_map/ppermute | solution.py:35
  49.5 0.0 collective-permute-start.7
  49.5 5.3 %collective-permute-start.8 = (bf16[8,32,128]{2,1,0:T(8,128)(2,1)S(1)}, bf16[8,32,128]{2,1,0:T(8,128)(2,1)S(1)}, u32[]{:S(2)}, u32[]{:S(2)}) collective-permute-start(bf16[8,32,128]{2,1,0:T(8,128)(2,1)S(1)} %get-tuple-element.51), channel_id=1, source_target_pairs={{0,31},{1,30},{2,29},{3,28},{4,3},{5,2},{6,1},{7,0},{8,7},{9,6},{1... | collective-permute-start | bytes 196616 | tf_op jit(solution)/shard_map/ppermute | solution.py:35
  54.8 1.1 %collective-permute-start.9 = (bf16[8,32,128]{2,1,0:T(8,128)(2,1)S(1)}, bf16[8,32,128]{2,1,0:T(8,128)(2,1)S(1)}, u32[]{:S(2)}, u32[]{:S(2)}) collective-permute-start(bf16[8,32,128]{2,1,0:T(8,128)(2,1)S(1)} %get-tuple-element.52), channel_id=1, source_target_pairs={{0,3},{1,2},{2,1},{3,0},{4,7},{5,6},{6,5},{7,4},{8,11},{9,10},{10,... | collective-permute-start | bytes 196616 | tf_op jit(solution)/shard_map/ppermute | solution.py:35
  55.9 1.6 %collective-permute-done.7.rest_2_ = bf16[8,32,128]{2,1,0:T(8,128)(2,1)S(1)} collective-permute-done((bf16[8,32,128]{2,1,0:T(8,128)(2,1)S(1)}, bf16[8,32,128]{2,1,0:T(8,128)(2,1)S(1)}, u32[]{:S(2)}, u32[]{:S(2)}) %collective-permute-start.7) | collective-permute-done | bytes 65568 | tf_op jit(solution)/shard_map/ppermute | solution.py:35
  57.5 0.0 collective-permute-done.8.rest_3_
  57.5 1.7 %collective-permute-done.9.rest_4_ = bf16[8,32,128]{2,1,0:T(8,128)(2,1)S(1)} collective-permute-done((bf16[8,32,128]{2,1,0:T(8,128)(2,1)S(1)}, bf16[8,32,128]{2,1,0:T(8,128)(2,1)S(1)}, u32[]{:S(2)}, u32[]{:S(2)}) %collective-permute-start.9) | collective-permute-done | bytes 65568 | tf_op jit(solution)/shard_map/ppermute | solution.py:35
  59.2 0.0 collective-permute-done.10.rest_5_
  59.2 0.0 collective-permute-done.11.rest_6_
  59.2 2.9 %owner_sums.1 = f32[64,8192]{1,0:T(8,128)} custom-call(s32[1,72]{1,0:T(1,128)S(1)} %copy-done.4, f32[8,32,128]{2,1,0:T(8,128)S(1)} %get-tuple-element.48.rest_0_, bf16[24,32,128]{2,1,0:T(8,128)(2,1)S(1)} %collective-permute-done.6.rest_1_, bf16[8,32,128]{2,1,0:T(8,128)(2,1)S(1)} %collective-permute-done.7.rest_2_, ...), custom_call_target="tpu_custom_call" | custom-call | tf_op jit(solution)/shard_map/owner_sums/pallas_call | solution.py:343
  (19 shorter events, 0.2 us)
Async XLA Ops:
  0.0 1.2 %copy-start = (bf16[32,64,256]{2,1,0:T(8,128)(2,1)S(1)}, bf16[32,64,256]{2,1,0:T(8,128)(2,1)}, u32[]{:S(2)}) copy-start(bf16[32,64,256]{2,1,0:T(8,128)(2,1)} %p_ref.3) | copy-start | bytes 3145732
  1.2 0.7 %copy-start.3 = (s32[1,8,6]{1,0,2:T(1,128)S(1)}, s32[1,8,6]{1,0,2:T(1,128)}, u32[]{:S(2)}) copy-start(s32[1,8,6]{1,0,2:T(1,128)} %param.12) | copy-start | bytes 580
  1.9 16.0 %copy-start.1 = (bf16[32,64,256]{2,1,0:T(8,128)(2,1)S(1)}, bf16[32,64,256]{2,1,0:T(8,128)(2,1)}, u32[]{:S(2)}) copy-start(bf16[32,64,256]{2,1,0:T(8,128)(2,1)} %p_ref.3) | copy-start | bytes 3145732
  1.9 16.0 %copy-start.5 = (bf16[32,64,448]{2,1,0:T(8,128)(2,1)S(1)}, bf16[32,64,448]{2,1,0:T(8,128)(2,1)}, u32[]{:S(2)}) copy-start(bf16[32,64,448]{2,1,0:T(8,128)(2,1)} %a_ref.1) | copy-start | bytes 5505028
  1.9 16.0 %copy-start.6 = (s32[32,7,4]{0,2,1:T(4,128)S(1)}, s32[32,7,4]{0,2,1:T(4,128)}, u32[]{:S(2)}) copy-start(s32[32,7,4]{0,2,1:T(4,128)} %param.10) | copy-start | bytes 10756
  1.9 16.0 %copy-start.7 = (s32[32,7]{0,1:T(8,128)S(1)}, s32[32,7]{0,1:T(8,128)}, u32[]{:S(2)}) copy-start(s32[32,7]{0,1:T(8,128)} %param.9) | copy-start | bytes 2692
  5.5 8.1 %collective-permute-start = (bf16[18,64,256]{2,1,0:T(8,128)(2,1)S(1)}, bf16[18,64,256]{2,1,0:T(8,128)(2,1)S(1)}, u32[]{:S(2)}, u32[]{:S(2)}) collective-permute-start(bf16[18,64,256]{2,1,0:T(8,128)(2,1)S(1)} %get-tuple-element.35), channel_id=1, source_target_pairs={{0,1},{1,0},{2,3},{3,2},{4,5},{5,4},{6,7},{7,6},{8,9},{9,8},{10,11... | collective-permute-start | bytes 1769480 | tf_op jit(solution)/shard_map/ppermute | solution.py:35
  5.6 24.0 %collective-permute-start.3 = (bf16[6,64,256]{2,1,0:T(8,128)(2,1)S(1)}, bf16[6,64,256]{2,1,0:T(8,128)(2,1)S(1)}, u32[]{:S(2)}, u32[]{:S(2)}) collective-permute-start(bf16[6,64,256]{2,1,0:T(8,128)(2,1)S(1)} %get-tuple-element.37), channel_id=1, source_target_pairs={{0,7},{1,6},{2,5},{3,4},{4,11},{5,10},{6,9},{7,8},{8,15},{9,14},{1... | collective-permute-start | bytes 589832 | tf_op jit(solution)/shard_map/ppermute | solution.py:35
  9.2 20.5 %collective-permute-start.4 = (bf16[6,64,256]{2,1,0:T(8,128)(2,1)S(1)}, bf16[6,64,256]{2,1,0:T(8,128)(2,1)S(1)}, u32[]{:S(2)}, u32[]{:S(2)}) collective-permute-start(bf16[6,64,256]{2,1,0:T(8,128)(2,1)S(1)} %get-tuple-element.38), channel_id=1, source_target_pairs={{0,31},{1,30},{2,29},{3,28},{4,3},{5,2},{6,1},{7,0},{8,7},{9,6},{1... | collective-permute-start | bytes 589832 | tf_op jit(solution)/shard_map/ppermute | solution.py:35
  12.3 17.3 %collective-permute-start.5 = (bf16[6,64,256]{2,1,0:T(8,128)(2,1)S(1)}, bf16[6,64,256]{2,1,0:T(8,128)(2,1)S(1)}, u32[]{:S(2)}, u32[]{:S(2)}) collective-permute-start(bf16[6,64,256]{2,1,0:T(8,128)(2,1)S(1)} %get-tuple-element.39), channel_id=1, source_target_pairs={{0,3},{1,2},{2,1},{3,0},{4,7},{5,6},{6,5},{7,4},{8,11},{9,10},{10,... | collective-permute-start | bytes 589832 | tf_op jit(solution)/shard_map/ppermute | solution.py:35
  13.6 21.2 %collective-permute-start.1 = (bf16[12,64,256]{2,1,0:T(8,128)(2,1)S(1)}, bf16[12,64,256]{2,1,0:T(8,128)(2,1)S(1)}, u32[]{:S(2)}, u32[]{:S(2)}) collective-permute-start(bf16[12,64,256]{2,1,0:T(8,128)(2,1)S(1)} %pad_maximum_fusion), channel_id=1, source_target_pairs={{0,4},{1,5},{2,6},{3,7},{4,8},{5,9},{6,10},{7,11},{8,12},{9,13},{1... | collective-permute-start | bytes 1179656 | tf_op jit(solution)/shard_map/ppermute | solution.py:35
  13.8 24.6 %collective-permute-start.2 = (bf16[12,64,256]{2,1,0:T(8,128)(2,1)S(1)}, bf16[12,64,256]{2,1,0:T(8,128)(2,1)S(1)}, u32[]{:S(2)}, u32[]{:S(2)}) collective-permute-start(bf16[12,64,256]{2,1,0:T(8,128)(2,1)S(1)} %pad_maximum_fusion.1), channel_id=1, source_target_pairs={{0,28},{1,29},{2,30},{3,31},{4,0},{5,1},{6,2},{7,3},{8,4},{9,5},{1... | collective-permute-start | bytes 1179656 | tf_op jit(solution)/shard_map/ppermute | solution.py:35
  18.0 11.7 %copy-start.2 = (s32[32,4,8]{0,2,1:T(8,128)S(1)}, s32[32,4,8]{0,2,1:T(8,128)}, u32[]{:S(2)}) copy-start(s32[32,4,8]{0,2,1:T(8,128)} %param.11) | copy-start | bytes 12292
  38.3 20.9 %copy-start.4 = (s32[1,72]{1,0:T(1,128)S(1)}, s32[1,72]{1,0:T(1,128)}, u32[]{:S(2)}) copy-start(s32[1,72]{1,0:T(1,128)} %owner_ref.1) | copy-start | bytes 868
  43.5 1.6 %collective-permute-start.6 = (bf16[24,32,128]{2,1,0:T(8,128)(2,1)S(1)}, bf16[24,32,128]{2,1,0:T(8,128)(2,1)S(1)}, u32[]{:S(2)}, u32[]{:S(2)}) collective-permute-start(bf16[24,32,128]{2,1,0:T(8,128)(2,1)S(1)} %get-tuple-element.49), channel_id=1, source_target_pairs={{0,1},{1,0},{2,3},{3,2},{4,5},{5,4},{6,7},{7,6},{8,9},{9,8},{10,11... | collective-permute-start | bytes 589832 | tf_op jit(solution)/shard_map/ppermute | solution.py:35
  45.2 14.1 %collective-permute-start.10 = (bf16[16,32,128]{2,1,0:T(8,128)(2,1)S(1)}, bf16[16,32,128]{2,1,0:T(8,128)(2,1)S(1)}, u32[]{:S(2)}, u32[]{:S(2)}) collective-permute-start(bf16[16,32,128]{2,1,0:T(8,128)(2,1)S(1)} %pad_maximum_fusion.2), channel_id=1, source_target_pairs={{0,4},{1,5},{2,6},{3,7},{4,8},{5,9},{6,10},{7,11},{8,12},{9,13},{1... | collective-permute-start | bytes 393224 | tf_op jit(solution)/shard_map/ppermute | solution.py:35
  45.3 14.0 %collective-permute-start.11 = (bf16[16,32,128]{2,1,0:T(8,128)(2,1)S(1)}, bf16[16,32,128]{2,1,0:T(8,128)(2,1)S(1)}, u32[]{:S(2)}, u32[]{:S(2)}) collective-permute-start(bf16[16,32,128]{2,1,0:T(8,128)(2,1)S(1)} %pad_maximum_fusion.3), channel_id=1, source_target_pairs={{0,28},{1,29},{2,30},{3,31},{4,0},{5,1},{6,2},{7,3},{8,4},{9,5},{1... | collective-permute-start | bytes 393224 | tf_op jit(solution)/shard_map/ppermute | solution.py:35
  49.5 8.0 %collective-permute-start.7 = (bf16[8,32,128]{2,1,0:T(8,128)(2,1)S(1)}, bf16[8,32,128]{2,1,0:T(8,128)(2,1)S(1)}, u32[]{:S(2)}, u32[]{:S(2)}) collective-permute-start(bf16[8,32,128]{2,1,0:T(8,128)(2,1)S(1)} %get-tuple-element.50), channel_id=1, source_target_pairs={{0,7},{1,6},{2,5},{3,4},{4,11},{5,10},{6,9},{7,8},{8,15},{9,14},{1... | collective-permute-start | bytes 196616 | tf_op jit(solution)/shard_map/ppermute | solution.py:35
  49.5 8.0 %collective-permute-start.8 = (bf16[8,32,128]{2,1,0:T(8,128)(2,1)S(1)}, bf16[8,32,128]{2,1,0:T(8,128)(2,1)S(1)}, u32[]{:S(2)}, u32[]{:S(2)}) collective-permute-start(bf16[8,32,128]{2,1,0:T(8,128)(2,1)S(1)} %get-tuple-element.51), channel_id=1, source_target_pairs={{0,31},{1,30},{2,29},{3,28},{4,3},{5,2},{6,1},{7,0},{8,7},{9,6},{1... | collective-permute-start | bytes 196616 | tf_op jit(solution)/shard_map/ppermute | solution.py:35
  54.8 4.4 %collective-permute-start.9 = (bf16[8,32,128]{2,1,0:T(8,128)(2,1)S(1)}, bf16[8,32,128]{2,1,0:T(8,128)(2,1)S(1)}, u32[]{:S(2)}, u32[]{:S(2)}) collective-permute-start(bf16[8,32,128]{2,1,0:T(8,128)(2,1)S(1)} %get-tuple-element.52), channel_id=1, source_target_pairs={{0,3},{1,2},{2,1},{3,0},{4,7},{5,6},{6,5},{7,4},{8,11},{9,10},{10,... | collective-permute-start | bytes 196616 | tf_op jit(solution)/shard_map/ppermute | solution.py:35

commit v4 on v3

--- a/solution.py
+++ b/solution.py
@@ -13,7 +13,7 @@
 SUMS = 4
 SMEM = pl.BlockSpec(memory_space=pltpu.SMEM)
 VMEM = pl.BlockSpec(memory_space=pltpu.VMEM)
-ANY = pl.BlockSpec(memory_space=pl.ANY)
+HBM = pl.BlockSpec(memory_space=pltpu.HBM)
 PARAMS = pltpu.CompilerParams(vmem_limit_bytes=12 * 1024 * 1024)
 
 
@@ -39,13 +39,22 @@
     return pltpu.with_memory_space_constraint(x, pltpu.VMEM)
 
 
-def exchange(parts):
-    pair, up_far, down_far, far, up, down = parts
+def exchange(parts, started=None, beside=None):
+    pair, far, up, down = parts
     size = up.shape[0]
-    pair = moved(pair, 0, "pair")
-    up = moved(jnp.concatenate([up, pair[size : 2 * size]]), 1, "own")
-    down = moved(jnp.concatenate([down, pair[2 * size :]]), -1, "own")
-    return pair, moved(up_far, 1, "far"), moved(down_far, -1, "far"), moved(far, 0, "far"), up, down
+    pair, far = moved(pair, 0, "pair"), moved(far, 0, "far")
+    up, down = jnp.concatenate([up, pair[size : 2 * size]]), jnp.concatenate([down, pair[2 * size :]])
+    if beside is not None:
+        up, down, started = lax.optimization_barrier((up, down, started))
+        result, done = beside(started)
+        far, done = lax.optimization_barrier((far, done))
+        result = *result, done
+    else:
+        result = None
+    up, down = moved(up, 1, "own"), moved(down, -1, "own")
+    up_far = moved(far[size : 2 * size], 1, "own")
+    down_far = moved(far[2 * size :], -1, "own")
+    return result, (pair, far, up, down, up_far, down_far)
 
 
 def pair_offset():
@@ -53,18 +62,11 @@
 
 
 def sent_cells(offset):
-    return (
-        (4 + offset, 7 + offset, 1 + offset),
-        (7 - offset,),
-        (1 - offset,),
-        (4 - offset,),
-        (7,),
-        (1,),
-    )
+    return (4 + offset, 7 + offset, 1 + offset), (4 - offset, 7 - offset, 1 - offset), (7,), (1,)
 
 
 def arrived_cells(offset):
-    return ((4 + offset,), (1 - offset,), (7 - offset,), (4 - offset,), (1, 1 + offset), (7, 7 + offset))
+    return (4 + offset,), (4 - offset,), (1, 1 + offset), (7, 7 + offset), (1 - offset,), (7 - offset,)
 
 
 EARLY, LATE = (0, 1, 2, 3), (4, 5)
@@ -74,39 +76,46 @@
     return cell - jnp.where(cell > 4, 1, 0)
 
 
-def pack_kernel(send_ref, p_ref, *rest):
-    outs, sems = rest[:-1], rest[-1]
+def pack_kernel(send_hbm, p_hbm, *rest):
+    outs, (send_ref, p_ref, sems) = rest[:-3], rest[-3:]
     ghosts = send_ref.shape[0]
-    copies = []
+    copies = [
+        pltpu.make_async_copy(send_hbm, send_ref, sems.at[0]),
+        pltpu.make_async_copy(p_hbm, p_ref, sems.at[1]),
+    ]
+    for copy in copies:
+        copy.start()
+    for copy in copies:
+        copy.wait()
     for out, cells in zip(outs, sent_cells(pair_offset())):
         for at, cell in enumerate(cells):
             p = neighbour_of(cell)
             for g in range(ghosts):
-                copies.append(
-                    pltpu.make_async_copy(
-                        p_ref.at[send_ref[g, 0, p]], out.at[at * ghosts + g], sems.at[len(copies)]
-                    )
-                )
-    for copy in copies:
-        copy.start()
-    for copy in copies:
-        copy.wait()
+                out[at * ghosts + g] = p_ref[send_ref[g, 0, p]]
 
 
 def pack(send_rows, p_strips):
     ghosts = send_rows.shape[2]
+    send = send_rows.transpose(2, 0, 1)
     return pl.pallas_call(
         pack_kernel,
         out_shape=[
             pltpu.VMEM((len(cells) * ghosts,) + p_strips.shape[1:], p_strips.dtype)
             for cells in sent_cells(1)
         ],
-        in_specs=[SMEM, ANY],
-        out_specs=[VMEM] * 6,
-        scratch_shapes=[pltpu.SemaphoreType.DMA((8 * ghosts,))],
+        in_specs=[HBM, HBM],
+        out_specs=[VMEM] * 4,
+        scratch_shapes=[
+            pltpu.SMEM(send.shape, jnp.int32),
+            pltpu.VMEM(p_strips.shape, p_strips.dtype),
+            pltpu.SemaphoreType.DMA((2,)),
+        ],
         compiler_params=PARAMS,
         name="pack",
-    )(send_rows.transpose(2, 0, 1), p_strips)
+    )(
+        pltpu.with_memory_space_constraint(send, pltpu.HBM),
+        pltpu.with_memory_space_constraint(p_strips, pltpu.HBM),
+    )
 
 
 def local_kernel(ghosts, slots, nbr_ref, ap_ref, a_ref, p_ref, *rest):
@@ -118,9 +127,9 @@
     capacity = ga_ref.shape[0] // 2
     offset = pair_offset()
     for cell in (0, 1, 2, 3, 5, 6, 7, 8):
-        late = jnp.int32(cell // 3 != 1)
-        if cell % 3 != 1:
-            late = late * (cell % 3 - 1 == offset).astype(jnp.int32)
+        late = jnp.int32(0)
+        if cell // 3 != 1 and cell % 3 != 1:
+            late = (cell % 3 - 1 == -offset).astype(jnp.int32)
         for g in range(ghosts):
             late_ref[(cell - (cell > 4)) * ghosts + g] = late
 
@@ -298,7 +307,7 @@
         out_shape=out_shape,
         in_specs=[SMEM] * 3 + [VMEM] * (2 + len(parts) + len(sums)),
         out_specs=[VMEM] * len(out_shape),
-        scratch_shapes=[pltpu.VMEM((8 * (arrived[3].shape[0]),) + ghost, jnp.bfloat16)],
+        scratch_shapes=[pltpu.VMEM((8 * (arrived[4].shape[0]),) + ghost, jnp.bfloat16)],
         input_output_aliases={inputs + i: i for i in range(len(sums))},
         compiler_params=PARAMS,
         cost_estimate=pl.CostEstimate(flops=2 * 10**9, bytes_accessed=10**6, transcendentals=0),
@@ -343,7 +352,7 @@
     return pl.pallas_call(
         owner_kernel,
         out_shape=jax.ShapeDtypeStruct((2 * half, OWN * kc2 // 2), jnp.float32),
-        in_specs=[SMEM] + [VMEM] * 7,
+        in_specs=[SMEM] + [VMEM] * (1 + len(parcels)),
         out_specs=VMEM,
         scratch_shapes=[pltpu.VMEM((OWN, half, kc2), jnp.float32)],
         compiler_params=PARAMS,
@@ -353,14 +362,18 @@
 
 def body(a_strips, p_strips, nbr_local, ap_slot, tile_slot, send_rows, owner_map):
     tiles_total = owner_map.shape[1]
-    arrived = exchange(pack(send_rows, p_strips))
-    *sums, ga, pt, info, order = local_part(
-        a_strips, p_strips, nbr_local, ap_slot, tile_slot.shape[2], send_rows.shape[2]
-    )
+
+    def beside(nbr):
+        *results, order = local_part(
+            a_strips, p_strips, nbr, ap_slot, tile_slot.shape[2], send_rows.shape[2]
+        )
+        return results, order
+
+    (*sums, ga, pt, info, order), arrived = exchange(pack(send_rows, p_strips), nbr_local, beside)
     sums = finish(False, info, order, tile_slot, ga, pt, arrived, sums, tiles_total)
     results = finish(True, info, order, tile_slot, ga, pt, arrived, sums, tiles_total)
     *parcels, own = results[2 + SUMS :]
-    return owner_sums(owner_map, own, exchange(parcels))
+    return owner_sums(owner_map, own, exchange(parcels)[1])
 
 
 def solution(mesh):

time: 62.9 us -> 60.7 us (0.965)
  Pallas kernels: 27.4 us -> 25.3 us
  local copies, waits for them, and re-layouts: 1.97 us -> 0.1 us
  waiting for transfers between devices: 8.95 us -> 10.6 us
    pallas_call x1, Pallas kernels: 3.56 us -> 1.5 us  [pack(): pl.pallas_call(pack_kernel, out_shape=[pltpu.VMEM((len(cells) * ghosts,)...]
    unnamed x16 -> x12, local copies, waits for them, and re-layouts: 1.93 us -> 0.03 us
    ppermute x12, waiting for transfers between devices: 8.95 us -> 10.6 us  [moved(): return lax.ppermute(x, ('dom', 'grp'), pairs)]
  transfers between devices with their start and end apart: 12 -> 12, of which waited for: 5 -> 4; matrix products, arithmetic and copies ran while one was open for 0% -> 0% of each run, Pallas kernels for 25% -> 29%
where the time goes in v4:
time: 60.7 us; the launch traced here: 59.6 us
  Pallas kernels  25.3 us (42%)
  starting transfers between devices  23.3 us (38%)
  waiting for transfers between devices  10.6 us (17%)
    ppermute x12, starting transfers between devices, moved(): return lax.ppermute(x, ('dom', 'grp'), pairs)  23.3 us
    pallas_call x1, Pallas kernels, local_part(): pl.pallas_call(functools.partial(local_kernel, ghosts, slots), out_shape=...  11.6 us
    ppermute x12, waiting for transfers between devices, moved(): return lax.ppermute(x, ('dom', 'grp'), pairs)  10.6 us
    pallas_call x2, Pallas kernels, finish(): pl.pallas_call(functools.partial(finish_kernel, late), out_shape=out_shap...  9.32 us
    pallas_call x1, Pallas kernels, owner_sums(): pl.pallas_call(owner_kernel, out_shape=jax.ShapeDtypeStruct((2 * half, OW...  2.9 us
    pallas_call x1, Pallas kernels, pack(): pl.pallas_call(pack_kernel, out_shape=[pltpu.VMEM((len(cells) * ghosts,)...  1.5 us
  transfers between devices with their start and end apart: 12, of which 4 were waited for; matrix products, arithmetic and copies ran while one was open for 0% of the time, Pallas kernels for 29%

profile of v4, /device:TPU:1, one launch (start us, length us, event | category | flops | bytes accessed | tf_op | source)
XLA Modules:
  0.0 59.6 jit_solution(5936505736862752313)
XLA Ops:
  0.0 1.5 %pack.1 = (bf16[18,64,256]{2,1,0:T(8,128)(2,1)S(1)}, bf16[18,64,256]{2,1,0:T(8,128)(2,1)S(1)}, bf16[6,64,256]{2,1,0:T(8,128)(2,1)S(1)}, bf16[6,64,256]{2,1,0:T(8,128)(2,1)S(1)}) custom-call(s32[6,1,8]{2,1,0:T(1,128)} %bitcast.8, bf16[32,64,256]{2,1,0:T(8,128)(2,1)} %p_ref.1), custom_call_target="tpu_custom_call" | custom-call | tf_op jit(solution)/shard_map/pack/pallas_call | solution.py:100
  1.5 0.1 collective-permute-start
  1.6 2.6 %collective-permute-start.1 = (bf16[18,64,256]{2,1,0:T(8,128)(2,1)S(1)}, bf16[18,64,256]{2,1,0:T(8,128)(2,1)S(1)}, u32[]{:S(2)}, u32[]{:S(2)}) collective-permute-start(bf16[18,64,256]{2,1,0:T(8,128)(2,1)S(1)} %get-tuple-element.36), channel_id=1, source_target_pairs={{0,3},{1,2},{2,1},{3,0},{4,7},{5,6},{6,5},{7,4},{8,11},{9,10},{10,... | collective-permute-start | bytes 1769480 | tf_op jit(solution)/shard_map/ppermute | solution.py:35
  4.3 0.0 collective-permute-done.rest_0_
  4.3 0.1 pad_maximum_fusion
  4.4 1.7 %collective-permute-start.4 = (bf16[12,64,256]{2,1,0:T(8,128)(2,1)S(1)}, bf16[12,64,256]{2,1,0:T(8,128)(2,1)S(1)}, u32[]{:S(2)}, u32[]{:S(2)}) collective-permute-start(bf16[12,64,256]{2,1,0:T(8,128)(2,1)S(1)} %get-tuple-element.42), channel_id=1, source_target_pairs={{0,4},{1,5},{2,6},{3,7},{4,8},{5,9},{6,10},{7,11},{8,12},{9,13},{1... | collective-permute-start | bytes 1179656 | tf_op jit(solution)/shard_map/ppermute | solution.py:35
  6.1 3.1 %collective-permute-start.5 = (bf16[12,64,256]{2,1,0:T(8,128)(2,1)S(1)}, bf16[12,64,256]{2,1,0:T(8,128)(2,1)S(1)}, u32[]{:S(2)}, u32[]{:S(2)}) collective-permute-start(bf16[12,64,256]{2,1,0:T(8,128)(2,1)S(1)} %get-tuple-element.43), channel_id=1, source_target_pairs={{0,28},{1,29},{2,30},{3,31},{4,0},{5,1},{6,2},{7,3},{8,4},{9,5},{1... | collective-permute-start | bytes 1179656 | tf_op jit(solution)/shard_map/ppermute | solution.py:35
  9.2 0.0 copy-done
  9.2 0.0 copy-start.1
  9.3 11.6 %local_part.1 = (f32[288,64,128]{2,1,0:T(8,128)S(1)}, f32[288,64,128]{2,1,0:T(8,128)S(1)}, bf16[392,64,64]{2,1,0:T(8,128)(2,1)S(1)}, bf16[32,128,128]{2,1,0:T(8,...) custom-call(s32[7,32]{1,0:T(8,128)S(1)} %bitcast.7, s32[7,4,32]{2,1,0:T(4,128)S(1)} %bitcast.6, ...), custom_call_target="tpu_custom_call" | custom-call | flops 5000000000 | bytes 10000000 | tf_op jit(solution)/shard_map/local_part/pallas_call | solution.py:190
  20.9 0.0 collective-permute-done.1.rest_1_
  20.9 1.8 %collective-permute-start.3 = (bf16[6,64,256]{2,1,0:T(8,128)(2,1)S(1)}, bf16[6,64,256]{2,1,0:T(8,128)(2,1)S(1)}, u32[]{:S(2)}, u32[]{:S(2)}) collective-permute-start(bf16[6,64,256]{2,1,0:T(8,128)(2,1)S(1)} %get-tuple-element.57), channel_id=1, source_target_pairs={{0,28},{1,29},{2,30},{3,31},{4,0},{5,1},{6,2},{7,3},{8,4},{9,5},{1... | collective-permute-start | bytes 589832 | tf_op jit(solution)/shard_map/ppermute | solution.py:35
  22.8 0.0 collective-permute-start.2
  22.8 4.1 %collective-permute-done.4.rest_2_ = bf16[12,64,256]{2,1,0:T(8,128)(2,1)S(1)} collective-permute-done((bf16[12,64,256]{2,1,0:T(8,128)(2,1)S(1)}, bf16[12,64,256]{2,1,0:T(8,128)(2,1)S(1)}, u32[]{:S(2)}, u32[]{:S(2)}) %collective-permute-start.4) | collective-permute-done | bytes 393248 | tf_op jit(solution)/shard_map/ppermute | solution.py:35
  26.9 0.0 collective-permute-done.5.rest_3_
  26.9 5.8 %early_part.1 = (f32[288,64,128]{2,1,0:T(8,128)S(1)}, f32[288,64,128]{2,1,0:T(8,128)S(1)}, f32[72,32,128]{2,1,0:T(8,128)S(1)}, f32[72,32,128]{2,1,0:T(8,128)S(1)...) custom-call(s32[1960]{0:T(1024)S(1)} %get-tuple-element.35.info_ref, ...), custom_call_target="tpu_custom_call", output_to_operand_aliasing={{0}: (9, {}), {1}: (10, {})} | custom-call | flops 2000000000 | bytes 1000000 | tf_op jit(solution)/shard_map/early_part/pallas_call | solution.py:305
  32.7 0.2 collective-permute-done.3.rest_1_
  33.0 0.0 collective-permute-done.2.rest_0_
  33.0 3.5 %late_part.1 = (f32[288,64,128]{2,1,0:T(8,128)S(1)}, f32[288,64,128]{2,1,0:T(8,128)S(1)}, f32[72,32,128]{2,1,0:T(8,128)S(1)}, f32[72,32,128]{2,1,0:T(8,128)S(1)}...) custom-call(s32[1960]{0:T(1024)S(1)} %get-tuple-element.35.info_ref,, ...), custom_call_target="tpu_custom_call", output_to_operand_aliasing={{0}: (7, {}), {1}: (8, {}), {2}: (9, {}), {3}: (10, {}), {4... | custom-call | flops 2000000000 | bytes 1000000 | tf_op jit(solution)/shard_map/late_part/pallas_call | solution.py:305
  36.5 1.9 %collective-permute-start.6 = (bf16[24,32,128]{2,1,0:T(8,128)(2,1)S(1)}, bf16[24,32,128]{2,1,0:T(8,128)(2,1)S(1)}, u32[]{:S(2)}, u32[]{:S(2)}) collective-permute-start(bf16[24,32,128]{2,1,0:T(8,128)(2,1)S(1)} %get-tuple-element.53), channel_id=1, source_target_pairs={{0,1},{1,0},{2,3},{3,2},{4,5},{5,4},{6,7},{7,6},{8,9},{9,8},{10,11... | collective-permute-start | bytes 589832 | tf_op jit(solution)/shard_map/ppermute | solution.py:35
  38.4 1.2 %collective-permute-start.7 = (bf16[24,32,128]{2,1,0:T(8,128)(2,1)S(1)}, bf16[24,32,128]{2,1,0:T(8,128)(2,1)S(1)}, u32[]{:S(2)}, u32[]{:S(2)}) collective-permute-start(bf16[24,32,128]{2,1,0:T(8,128)(2,1)S(1)} %get-tuple-element.54), channel_id=1, source_target_pairs={{0,3},{1,2},{2,1},{3,0},{4,7},{5,6},{6,5},{7,4},{8,11},{9,10},{10,... | collective-permute-start | bytes 589832 | tf_op jit(solution)/shard_map/ppermute | solution.py:35
  39.5 0.0 collective-permute-done.6.rest_1_
  39.6 2.2 %collective-permute-start.8 = (bf16[16,32,128]{2,1,0:T(8,128)(2,1)S(1)}, bf16[16,32,128]{2,1,0:T(8,128)(2,1)S(1)}, u32[]{:S(2)}, u32[]{:S(2)}) collective-permute-start(bf16[16,32,128]{2,1,0:T(8,128)(2,1)S(1)} %pad_maximum_fusion.2), channel_id=1, source_target_pairs={{0,4},{1,5},{2,6},{3,7},{4,8},{5,9},{6,10},{7,11},{8,12},{9,13},{1... | collective-permute-start | bytes 393224 | tf_op jit(solution)/shard_map/ppermute | solution.py:35
  41.8 3.1 %collective-permute-start.9 = (bf16[16,32,128]{2,1,0:T(8,128)(2,1)S(1)}, bf16[16,32,128]{2,1,0:T(8,128)(2,1)S(1)}, u32[]{:S(2)}, u32[]{:S(2)}) collective-permute-start(bf16[16,32,128]{2,1,0:T(8,128)(2,1)S(1)} %pad_maximum_fusion.3), channel_id=1, source_target_pairs={{0,28},{1,29},{2,30},{3,31},{4,0},{5,1},{6,2},{7,3},{8,4},{9,5},{1... | collective-permute-start | bytes 393224 | tf_op jit(solution)/shard_map/ppermute | solution.py:35
  45.0 0.0 collective-permute-done.7.rest_2_
  45.0 5.5 %collective-permute-start.11 = (bf16[8,32,128]{2,1,0:T(8,128)(2,1)S(1)}, bf16[8,32,128]{2,1,0:T(8,128)(2,1)S(1)}, u32[]{:S(2)}, u32[]{:S(2)}) collective-permute-start(bf16[8,32,128]{2,1,0:T(8,128)(2,1)S(1)} %get-tuple-element.61), channel_id=1, source_target_pairs={{0,28},{1,29},{2,30},{3,31},{4,0},{5,1},{6,2},{7,3},{8,4},{9,5},{1... | collective-permute-start | bytes 196616 | tf_op jit(solution)/shard_map/ppermute | solution.py:35
  50.5 0.0 collective-permute-start.10
  50.5 1.6 %collective-permute-done.11.rest_6_ = bf16[8,32,128]{2,1,0:T(8,128)(2,1)S(1)} collective-permute-done((bf16[8,32,128]{2,1,0:T(8,128)(2,1)S(1)}, bf16[8,32,128]{2,1,0:T(8,128)(2,1)S(1)}, u32[]{:S(2)}, u32[]{:S(2)}) %collective-permute-start.11) | collective-permute-done | bytes 65568 | tf_op jit(solution)/shard_map/ppermute | solution.py:35
  52.1 4.6 %collective-permute-done.10.rest_5_ = bf16[8,32,128]{2,1,0:T(8,128)(2,1)S(1)} collective-permute-done((bf16[8,32,128]{2,1,0:T(8,128)(2,1)S(1)}, bf16[8,32,128]{2,1,0:T(8,128)(2,1)S(1)}, u32[]{:S(2)}, u32[]{:S(2)}) %collective-permute-start.10) | collective-permute-done | bytes 65568 | tf_op jit(solution)/shard_map/ppermute | solution.py:35
  56.7 0.0 collective-permute-done.8.rest_3_
  56.7 0.0 collective-permute-done.9.rest_4_
  56.7 2.9 %owner_sums.1 = f32[64,8192]{1,0:T(8,128)} custom-call(s32[1,72]{1,0:T(1,128)S(1)} %copy-done.2, f32[8,32,128]{2,1,0:T(8,128)S(1)} %get-tuple-element.52.rest_0_, bf16[24,32,128]{2,1,0:T(8,128)(2,1)S(1)} %collective-permute-done.6.rest_1_, bf16[24,32,128]{2,1,0:T(8,128)(2,1)S(1)} %collective-permute-done.7.rest_2_, ...), custom_call_target="tpu_custom_call" | custom-call | tf_op jit(solution)/shard_map/owner_sums/pallas_call | solution.py:352
  (16 shorter events, 0.1 us)
Async XLA Ops:
  0.0 9.2 %copy-start = (bf16[32,64,256]{2,1,0:T(8,128)(2,1)S(1)}, bf16[32,64,256]{2,1,0:T(8,128)(2,1)}, u32[]{:S(2)}) copy-start(bf16[32,64,256]{2,1,0:T(8,128)(2,1)} %p_ref.1) | copy-start | bytes 3145732
  0.0 9.2 %copy-start.5 = (s32[32,7]{0,1:T(8,128)S(1)}, s32[32,7]{0,1:T(8,128)}, u32[]{:S(2)}) copy-start(s32[32,7]{0,1:T(8,128)} %param.9) | copy-start | bytes 2692
  0.0 9.2 %copy-start.4 = (s32[32,7,4]{0,2,1:T(4,128)S(1)}, s32[32,7,4]{0,2,1:T(4,128)}, u32[]{:S(2)}) copy-start(s32[32,7,4]{0,2,1:T(4,128)} %param.10) | copy-start | bytes 10756
  0.0 9.2 %copy-start.3 = (bf16[32,64,448]{2,1,0:T(8,128)(2,1)S(1)}, bf16[32,64,448]{2,1,0:T(8,128)(2,1)}, u32[]{:S(2)}) copy-start(bf16[32,64,448]{2,1,0:T(8,128)(2,1)} %a_ref.1) | copy-start | bytes 5505028
  1.5 2.7 %collective-permute-start = (bf16[18,64,256]{2,1,0:T(8,128)(2,1)S(1)}, bf16[18,64,256]{2,1,0:T(8,128)(2,1)S(1)}, u32[]{:S(2)}, u32[]{:S(2)}) collective-permute-start(bf16[18,64,256]{2,1,0:T(8,128)(2,1)S(1)} %get-tuple-element.32), channel_id=1, source_target_pairs={{0,1},{1,0},{2,3},{3,2},{4,5},{5,4},{6,7},{7,6},{8,9},{9,8},{10,11... | collective-permute-start | bytes 1769480 | tf_op jit(solution)/shard_map/ppermute | solution.py:35
  1.6 19.3 %collective-permute-start.1 = (bf16[18,64,256]{2,1,0:T(8,128)(2,1)S(1)}, bf16[18,64,256]{2,1,0:T(8,128)(2,1)S(1)}, u32[]{:S(2)}, u32[]{:S(2)}) collective-permute-start(bf16[18,64,256]{2,1,0:T(8,128)(2,1)S(1)} %get-tuple-element.36), channel_id=1, source_target_pairs={{0,3},{1,2},{2,1},{3,0},{4,7},{5,6},{6,5},{7,4},{8,11},{9,10},{10,... | collective-permute-start | bytes 1769480 | tf_op jit(solution)/shard_map/ppermute | solution.py:35
  4.4 22.5 %collective-permute-start.4 = (bf16[12,64,256]{2,1,0:T(8,128)(2,1)S(1)}, bf16[12,64,256]{2,1,0:T(8,128)(2,1)S(1)}, u32[]{:S(2)}, u32[]{:S(2)}) collective-permute-start(bf16[12,64,256]{2,1,0:T(8,128)(2,1)S(1)} %get-tuple-element.42), channel_id=1, source_target_pairs={{0,4},{1,5},{2,6},{3,7},{4,8},{5,9},{6,10},{7,11},{8,12},{9,13},{1... | collective-permute-start | bytes 1179656 | tf_op jit(solution)/shard_map/ppermute | solution.py:35
  6.1 20.8 %collective-permute-start.5 = (bf16[12,64,256]{2,1,0:T(8,128)(2,1)S(1)}, bf16[12,64,256]{2,1,0:T(8,128)(2,1)S(1)}, u32[]{:S(2)}, u32[]{:S(2)}) collective-permute-start(bf16[12,64,256]{2,1,0:T(8,128)(2,1)S(1)} %get-tuple-element.43), channel_id=1, source_target_pairs={{0,28},{1,29},{2,30},{3,31},{4,0},{5,1},{6,2},{7,3},{8,4},{9,5},{1... | collective-permute-start | bytes 1179656 | tf_op jit(solution)/shard_map/ppermute | solution.py:35
  9.2 17.7 %copy-start.1 = (s32[32,4,8]{0,2,1:T(8,128)S(1)}, s32[32,4,8]{0,2,1:T(8,128)}, u32[]{:S(2)}) copy-start(s32[32,4,8]{0,2,1:T(8,128)} %param.11) | copy-start | bytes 12292
  20.9 12.0 %collective-permute-start.3 = (bf16[6,64,256]{2,1,0:T(8,128)(2,1)S(1)}, bf16[6,64,256]{2,1,0:T(8,128)(2,1)S(1)}, u32[]{:S(2)}, u32[]{:S(2)}) collective-permute-start(bf16[6,64,256]{2,1,0:T(8,128)(2,1)S(1)} %get-tuple-element.57), channel_id=1, source_target_pairs={{0,28},{1,29},{2,30},{3,31},{4,0},{5,1},{6,2},{7,3},{8,4},{9,5},{1... | collective-permute-start | bytes 589832 | tf_op jit(solution)/shard_map/ppermute | solution.py:35
  22.8 10.2 %collective-permute-start.2 = (bf16[6,64,256]{2,1,0:T(8,128)(2,1)S(1)}, bf16[6,64,256]{2,1,0:T(8,128)(2,1)S(1)}, u32[]{:S(2)}, u32[]{:S(2)}) collective-permute-start(bf16[6,64,256]{2,1,0:T(8,128)(2,1)S(1)} %get-tuple-element.58), channel_id=1, source_target_pairs={{0,4},{1,5},{2,6},{3,7},{4,8},{5,9},{6,10},{7,11},{8,12},{9,13},{1... | collective-permute-start | bytes 589832 | tf_op jit(solution)/shard_map/ppermute | solution.py:35
  33.0 23.7 %copy-start.2 = (s32[1,72]{1,0:T(1,128)S(1)}, s32[1,72]{1,0:T(1,128)}, u32[]{:S(2)}) copy-start(s32[1,72]{1,0:T(1,128)} %owner_ref.1) | copy-start | bytes 868
  36.5 3.1 %collective-permute-start.6 = (bf16[24,32,128]{2,1,0:T(8,128)(2,1)S(1)}, bf16[24,32,128]{2,1,0:T(8,128)(2,1)S(1)}, u32[]{:S(2)}, u32[]{:S(2)}) collective-permute-start(bf16[24,32,128]{2,1,0:T(8,128)(2,1)S(1)} %get-tuple-element.53), channel_id=1, source_target_pairs={{0,1},{1,0},{2,3},{3,2},{4,5},{5,4},{6,7},{7,6},{8,9},{9,8},{10,11... | collective-permute-start | bytes 589832 | tf_op jit(solution)/shard_map/ppermute | solution.py:35
  38.4 6.6 %collective-permute-start.7 = (bf16[24,32,128]{2,1,0:T(8,128)(2,1)S(1)}, bf16[24,32,128]{2,1,0:T(8,128)(2,1)S(1)}, u32[]{:S(2)}, u32[]{:S(2)}) collective-permute-start(bf16[24,32,128]{2,1,0:T(8,128)(2,1)S(1)} %get-tuple-element.54), channel_id=1, source_target_pairs={{0,3},{1,2},{2,1},{3,0},{4,7},{5,6},{6,5},{7,4},{8,11},{9,10},{10,... | collective-permute-start | bytes 589832 | tf_op jit(solution)/shard_map/ppermute | solution.py:35
  39.6 17.1 %collective-permute-start.8 = (bf16[16,32,128]{2,1,0:T(8,128)(2,1)S(1)}, bf16[16,32,128]{2,1,0:T(8,128)(2,1)S(1)}, u32[]{:S(2)}, u32[]{:S(2)}) collective-permute-start(bf16[16,32,128]{2,1,0:T(8,128)(2,1)S(1)} %pad_maximum_fusion.2), channel_id=1, source_target_pairs={{0,4},{1,5},{2,6},{3,7},{4,8},{5,9},{6,10},{7,11},{8,12},{9,13},{1... | collective-permute-start | bytes 393224 | tf_op jit(solution)/shard_map/ppermute | solution.py:35
  41.8 14.8 %collective-permute-start.9 = (bf16[16,32,128]{2,1,0:T(8,128)(2,1)S(1)}, bf16[16,32,128]{2,1,0:T(8,128)(2,1)S(1)}, u32[]{:S(2)}, u32[]{:S(2)}) collective-permute-start(bf16[16,32,128]{2,1,0:T(8,128)(2,1)S(1)} %pad_maximum_fusion.3), channel_id=1, source_target_pairs={{0,28},{1,29},{2,30},{3,31},{4,0},{5,1},{6,2},{7,3},{8,4},{9,5},{1... | collective-permute-start | bytes 393224 | tf_op jit(solution)/shard_map/ppermute | solution.py:35
  45.0 7.1 %collective-permute-start.11 = (bf16[8,32,128]{2,1,0:T(8,128)(2,1)S(1)}, bf16[8,32,128]{2,1,0:T(8,128)(2,1)S(1)}, u32[]{:S(2)}, u32[]{:S(2)}) collective-permute-start(bf16[8,32,128]{2,1,0:T(8,128)(2,1)S(1)} %get-tuple-element.61), channel_id=1, source_target_pairs={{0,28},{1,29},{2,30},{3,31},{4,0},{5,1},{6,2},{7,3},{8,4},{9,5},{1... | collective-permute-start | bytes 196616 | tf_op jit(solution)/shard_map/ppermute | solution.py:35
  50.5 6.2 %collective-permute-start.10 = (bf16[8,32,128]{2,1,0:T(8,128)(2,1)S(1)}, bf16[8,32,128]{2,1,0:T(8,128)(2,1)S(1)}, u32[]{:S(2)}, u32[]{:S(2)}) collective-permute-start(bf16[8,32,128]{2,1,0:T(8,128)(2,1)S(1)} %get-tuple-element.62), channel_id=1, source_target_pairs={{0,4},{1,5},{2,6},{3,7},{4,8},{5,9},{6,10},{7,11},{8,12},{9,13},{1... | collective-permute-start | bytes 196616 | tf_op jit(solution)/shard_map/ppermute | solution.py:35

commit v5 on v4

v5 whole, which is shorter than its diff:
```python
import functools

import jax
import jax.numpy as jnp
from jax import lax
from jax.experimental import pallas as pl
from jax.experimental.pallas import tpu as pltpu
from jax.sharding import PartitionSpec as P

OWN = 128
GROUP = 4
STEP = 4
SUMS = 4
OWNER_SUMS = 1
SMEM = pl.BlockSpec(memory_space=pltpu.SMEM)
VMEM = pl.BlockSpec(memory_space=pltpu.VMEM)
HBM = pl.BlockSpec(memory_space=pltpu.HBM)
PARAMS = pltpu.CompilerParams(vmem_limit_bytes=8 * 1024 * 1024)


def moved(x, a, along):
    domains, groups = lax.axis_size("dom"), lax.axis_size("grp")

    def target(j):
        if along == "pair":
            return j ^ 1
        if along == "far":
            return (j - 1 + 2 * (j % 2)) % groups
        return j

    pairs = [
        (i * groups + j, (i + a) % domains * groups + target(j))
        for i in range(domains)
        for j in range(groups)
    ]
    return lax.ppermute(x, ("dom", "grp"), pairs)


def resident(x):
    return pltpu.with_memory_space_constraint(x, pltpu.VMEM)


def exchange_rows(parts, nbr_local, local_work):
    pair, far, up, down = parts
    size = up.shape[0]
    pair, far = moved(pair, 0, "pair"), moved(far, 0, "far")
    up, down = jnp.concatenate([up, pair[size : 2 * size]]), jnp.concatenate([down, pair[2 * size :]])
    up, down, nbr_local = lax.optimization_barrier((up, down, nbr_local))
    *results, small = local_work(nbr_local)
    far, small = lax.optimization_barrier((far, small))
    up, down = moved(up, 1, "own"), moved(down, -1, "own")
    up_far = moved(far[size : 2 * size], 1, "own")
    down_far = moved(far[2 * size :], -1, "own")
    return (*results, small), (pair, far, up, down, up_far, down_far)


def exchange_tiles(parts, owner_map, first_sums):
    pair, far, up, down, up_far, down_far = parts
    size = up.shape[0]
    pair = moved(pair, 0, "pair")
    up_far, down_far = moved(up_far, 1, "own"), moved(down_far, -1, "own")
    up, down = jnp.concatenate([up, pair[size : 2 * size]]), jnp.concatenate([down, pair[2 * size :]])
    up, down, owner_map = lax.optimization_barrier((up, down, owner_map))
    sums, small = first_sums(pair, owner_map)
    up_far, down_far, small = lax.optimization_barrier((up_far, down_far, small))
    far = moved(jnp.concatenate([far, up_far, down_far]), 0, "far")
    return (*sums, small), (far, moved(up, 1, "own"), moved(down, -1, "own"))


def pair_offset():
    return 1 - 2 * (lax.axis_index("grp") % 2)


def sent_rows(offset):
    return (4 + offset, 7 + offset, 1 + offset), (4 - offset, 7 - offset, 1 - offset), (7,), (1,)


def arrived_rows(offset):
    return (4 + offset,), (4 - offset,), (1, 1 + offset), (7, 7 + offset), (1 - offset,), (7 - offset,)


def sent_tiles(offset):
    return (4 + offset, 7 + offset, 1 + offset), (4 - offset,), (7,), (1,), (7 - offset,), (1 - offset,)


def arrived_tiles(offset):
    return (4 - offset, 1 - offset, 7 - offset), (1, 1 + offset), (7, 7 + offset)


STAGES = ((0, 1), (2, 3), (4, 5))


def neighbour_of(cell):
    return cell - jnp.where(cell > 4, 1, 0)


def pack_kernel(send_hbm, p_hbm, *rest):
    outs, (send_ref, p_ref, sems) = rest[:-3], rest[-3:]
    ghosts = send_ref.shape[0]
    copies = [
        pltpu.make_async_copy(send_hbm, send_ref, sems.at[0]),
        pltpu.make_async_copy(p_hbm, p_ref, sems.at[1]),
    ]
    for copy in copies:
        copy.start()
    for copy in copies:
        copy.wait()
    for out, cells in zip(outs, sent_rows(pair_offset())):
        for at, cell in enumerate(cells):
            p = neighbour_of(cell)
            for g in range(ghosts):
                out[at * ghosts + g] = p_ref[send_ref[g, 0, p]]


def pack(send_rows, p_strips):
    ghosts = send_rows.shape[2]
    send = send_rows.transpose(2, 0, 1)
    return pl.pallas_call(
        pack_kernel,
        out_shape=[
            pltpu.VMEM((len(cells) * ghosts,) + p_strips.shape[1:], p_strips.dtype)
            for cells in sent_rows(1)
        ],
        in_specs=[HBM, HBM],
        out_specs=[VMEM] * 4,
        scratch_shapes=[
            pltpu.SMEM(send.shape, jnp.int32),
            pltpu.VMEM(p_strips.shape, p_strips.dtype),
            pltpu.SemaphoreType.DMA((2,)),
        ],
        compiler_params=PARAMS,
        name="pack",
    )(
        pltpu.with_memory_space_constraint(send, pltpu.HBM),
        pltpu.with_memory_space_constraint(p_strips, pltpu.HBM),
    )


def local_kernel(ghosts, slots, nbr_ref, ap_ref, a_ref, p_ref, *rest):
    even_ref, odd_ref, ga_ref, pt_ref, info_ref, order_ref, stage_ref, middle_ref = rest
    blocks, pieces, elements = ap_ref.shape
    kb = a_ref.shape[1]
    kc = p_ref.shape[2] // pieces
    stride = slots + 1
    stages = len(STAGES)
    capacity = ga_ref.shape[0]
    offset = pair_offset()
    for cell in (0, 1, 2, 3, 5, 6, 7, 8):
        stage = jnp.int32(cell // 3 != 1)
        if cell // 3 != 1 and cell % 3 != 1:
            stage = 1 + (cell % 3 - 1 == -offset).astype(jnp.int32)
        for g in range(ghosts):
            stage_ref[(cell - (cell > 4)) * ghosts + g] = stage

    def element(e, carry):
        counts, members = list(carry[:stages]), list(carry[stages:])
        for ref in (even_ref, odd_ref):
            ref[pl.ds(e * stride, stride)] = jnp.zeros((stride,) + ref.shape[1:], jnp.float32)
        last = jnp.int32(0)
        for j in range(blocks):
            n = nbr_ref[j, e]
            ghost = n >= elements
            a = a_ref[e, :, j * kb : (j + 1) * kb]
            product = jnp.dot(
                a, p_ref[jnp.where(ghost, 0, n)], preferred_element_type=jnp.float32
            )
            for k in range(pieces):
                row = e * stride + jnp.where(ghost, slots, ap_ref[j, k, e])
                piece = product[:, (k // 2) * 2 * kc : (k // 2 + 1) * 2 * kc]
                ref = odd_ref if k % 2 else even_ref
                ref[row] += piece
            if j > 0:
                stage = jnp.where(ghost, stage_ref[jnp.where(ghost, n - elements, 0)], 0)
                at = counts[0]
                for s in range(1, stages):
                    at = jnp.where(stage == s, s * capacity + counts[s], at)
                for k in range(pieces):
                    info_ref[at * (pieces + 2) + k] = e * stride + ap_ref[j, k, e]
                info_ref[at * (pieces + 2) + pieces] = n - elements
                listed = sum(counts)
                info_ref[at * (pieces + 2) + pieces + 1] = listed
                ga_ref[listed] = a
                for s in range(stages):
                    counts[s] += (ghost & (stage == s)).astype(jnp.int32)
                last = jnp.maximum(last, stage)
        first, middle, final = members
        order_ref[jnp.where(last == 2, elements - 1 - final, first)] = e
        middle_ref[middle] = e
        for s in range(stages):
            members[s] += (last == s).astype(jnp.int32)
        pt = p_ref[e].astype(jnp.float32).T.reshape(pieces, 2, kc // 2, kb)
        pt_ref[e, :, :kb] = pt[:, 0].reshape(pieces * kc // 2, kb).astype(jnp.bfloat16)
        pt_ref[e, :, kb:] = pt[:, 1].reshape(pieces * kc // 2, kb).astype(jnp.bfloat16)
        return *counts, *members

    totals = lax.fori_loop(0, elements, element, (jnp.int32(0),) * (2 * stages))
    counts, (first, middle, _) = totals[:stages], totals[stages:]

    def place(i, carry):
        order_ref[first + i] = middle_ref[i]
        return carry

    lax.fori_loop(0, middle, place, 0)
    for s in range(stages):
        for u in range(GROUP):
            at = s * capacity + counts[s] + u
            for k in range(pieces):
                info_ref[at * (pieces + 2) + k] = slots
            info_ref[at * (pieces + 2) + pieces] = 0
            info_ref[at * (pieces + 2) + pieces + 1] = 0
        order_ref[elements + s] = (counts[s] + GROUP - 1) // GROUP
    order_ref[elements + stages] = 0
    order_ref[elements + stages + 1] = first // STEP
    order_ref[elements + stages + 2] = (first + middle) // STEP
    order_ref[elements + stages + 3] = elements // STEP


def local_part(a_strips, p_strips, nbr_local, ap_slot, slots, ghosts):
    elements, kb, _ = a_strips.shape
    blocks, pieces = ap_slot.shape[1:]
    kc = p_strips.shape[2] // pieces
    capacity = elements * (blocks - 1) + GROUP
    sums = pltpu.VMEM((elements * (slots + 1), kb, 2 * kc), jnp.float32)
    return pl.pallas_call(
        functools.partial(local_kernel, ghosts, slots),
        out_shape=[
            sums,
            sums,
            pltpu.VMEM((capacity, kb, kb), jnp.bfloat16),
            pltpu.VMEM((elements, pieces * kc // 2, 2 * kb), jnp.bfloat16),
            jax.ShapeDtypeStruct((len(STAGES) * capacity * (pieces + 2),), jnp.int32),
            jax.ShapeDtypeStruct((elements + 2 * len(STAGES) + 1,), jnp.int32),
        ],
        in_specs=[SMEM, SMEM, VMEM, VMEM],
        out_specs=[VMEM] * 4 + [SMEM] * 2,
        scratch_shapes=[pltpu.SMEM((8 * ghosts,), jnp.int32), pltpu.SMEM((elements + 1,), jnp.int32)],
        compiler_params=PARAMS,
        cost_estimate=pl.CostEstimate(flops=5 * 10**9, bytes_accessed=10**7, transcendentals=0),
        name="local_part",
    )(nbr_local.T, ap_slot.transpose(1, 2, 0), a_strips, p_strips)


def finish_kernel(stage, info_ref, order_ref, tile_ref, ga_ref, pt_ref, *rest):
    parts = STAGES[stage]
    stages = len(STAGES)
    arrived, rest = rest[: len(parts)], rest[len(parts) :]
    rest = rest[2 + SUMS * (stage > 0) :]
    even_ref, odd_ref, *tiles = rest[: 2 + SUMS]
    sent, ghost_ref = rest[2 + SUMS : -1], rest[-1]
    pieces, slots, elements = tile_ref.shape
    kb, kc2 = even_ref.shape[1:]
    half = kc2 // 4
    stride = slots + 1
    ghosts = ghost_ref.shape[0] // 8
    first = ga_ref.shape[0] * stage
    offset = pair_offset()
    for part, ref in zip(parts, arrived):
        for at, cell in enumerate(arrived_rows(offset)[part]):
            rows = pl.ds(neighbour_of(cell) * ghosts, ghosts)
            ghost_ref[rows] = ref[at * ghosts : (at + 1) * ghosts]
    if stage == 0:
        for ref in tiles:
            ref[...] = jnp.zeros_like(ref)
    left = lax.broadcasted_iota(jnp.int32, (kb, kc2), 1) < kc2 // 2

    def ghost_group(i, carry):
        for u in range(GROUP):
            at = first + i * GROUP + u
            product = jnp.dot(
                ga_ref[info_ref[at * (pieces + 2) + pieces + 1]],
                ghost_ref[info_ref[at * (pieces + 2) + pieces]],
                preferred_element_type=jnp.float32,
            )
            for k in range(pieces):
                ref = odd_ref if k % 2 else even_ref
                ref[info_ref[at * (pieces + 2) + k]] += product[
                    :, (k // 2) * kc2 : (k // 2 + 1) * kc2
                ]
        return carry

    lax.fori_loop(0, order_ref[elements + stage], ghost_group, 0)
    zero = jnp.zeros((kb, kc2), jnp.bfloat16)

    def one(e):
        pt = pt_ref[e]
        for pair in range(slots // 2):
            columns = []
            for q in (2 * pair, 2 * pair + 1):
                x = jnp.where(left, even_ref[e * stride + q], odd_ref[e * stride + q])
                y = (x + pltpu.roll(x, kc2 // 2, 1)).astype(jnp.bfloat16)
                columns.append(
                    jnp.concatenate([jnp.where(left, y, zero), jnp.where(left, zero, y)], axis=0)
                )
            terms = jnp.dot(
                pt, jnp.concatenate(columns, axis=1), preferred_element_type=jnp.float32
            )
            for k in range(pieces):
                for u in range(2):
                    ref = tiles[(2 * k + u) % SUMS]
                    ref[tile_ref[k, 2 * pair + u, e]] += terms[
                        k * half : (k + 1) * half, u * kc2 : (u + 1) * kc2
                    ]

    def step(i, carry):
        for u in range(STEP):
            one(order_ref[i * STEP + u])
        return carry

    begin = elements + stages + stage
    lax.fori_loop(order_ref[begin], order_ref[begin + 1], step, 0)
    if stage < stages - 1:
        return
    capacity = sent[-1].shape[0]

    def total(cell):
        rows = pl.ds(cell * capacity, capacity)
        return functools.reduce(jnp.add, [ref[rows] for ref in tiles])

    for out, cells in zip(sent, sent_tiles(offset)):
        for at, cell in enumerate(cells):
            out[at * capacity : (at + 1) * capacity] = total(cell).astype(out.dtype)
    sent[-1][...] = total(4)


def finish(stage, info, order, tile_slot, ga, pt, arrived, sums, tiles_total):
    parts = STAGES[stage]
    kb, kc2 = sums[0].shape[1:]
    half = kc2 // 4
    capacity = tiles_total // 9
    out_shape = [pltpu.VMEM(x.shape, x.dtype) for x in sums[:2]]
    out_shape += [pltpu.VMEM((tiles_total, half, kc2), jnp.float32)] * SUMS
    if stage == len(STAGES) - 1:
        out_shape += [
            pltpu.VMEM((len(cells) * capacity, half, kc2), jnp.bfloat16) for cells in sent_tiles(1)
        ]
        out_shape += [pltpu.VMEM((capacity, half, kc2), jnp.float32)]
    inputs = 5 + len(parts)
    return pl.pallas_call(
        functools.partial(finish_kernel, stage),
        out_shape=out_shape,
        in_specs=[SMEM] * 3 + [VMEM] * (2 + len(parts) + len(sums)),
        out_specs=[VMEM] * len(out_shape),
        scratch_shapes=[
            pltpu.VMEM((8 * arrived[4].shape[0],) + arrived[4].shape[1:], jnp.bfloat16)
        ],
        input_output_aliases={inputs + i: i for i in range(len(sums))},
        compiler_params=PARAMS,
        cost_estimate=pl.CostEstimate(flops=2 * 10**9, bytes_accessed=10**6, transcendentals=0),
        name=("first_part", "middle_part", "last_part")[stage],
    )(
        info,
        order,
        tile_slot.transpose(1, 2, 0),
        resident(ga),
        resident(pt),
        *(resident(arrived[part]) for part in parts),
        *sums,
    )


def add_tiles(owner_ref, sums, cell, parcel, at, capacity):
    for g in range(capacity):
        ref = sums[g % len(sums)]
        ref[owner_ref[0, cell * capacity + g]] += parcel[at * capacity + g].astype(jnp.float32)


def first_sums_kernel(owner_ref, own, pair, *rest):
    sums, small = rest[:-1], rest[-1]
    for ref in sums:
        ref[...] = jnp.zeros_like(ref)
    capacity = own.shape[0]
    add_tiles(owner_ref, sums, 4, own, 0, capacity)
    add_tiles(owner_ref, sums, 4 + pair_offset(), pair, 0, capacity)
    small[...] = jnp.zeros_like(small)


def first_sums(own, pair, owner_map):
    _, half, kc2 = own.shape
    *sums, small = pl.pallas_call(
        first_sums_kernel,
        out_shape=[pltpu.VMEM((OWN, half, kc2), jnp.float32)] * OWNER_SUMS
        + [jax.ShapeDtypeStruct((8, 128), jnp.float32)],
        in_specs=[SMEM, VMEM, VMEM],
        out_specs=[VMEM] * (OWNER_SUMS + 1),
        compiler_params=PARAMS,
        cost_estimate=pl.CostEstimate(flops=10**9, bytes_accessed=10**6, transcendentals=0),
        name="first_sums",
    )(owner_map, resident(own), resident(pair))
    return sums, small


def more_sums_kernel(owner_ref, up, down, *rest):
    sums = rest[-OWNER_SUMS:]
    capacity = owner_ref.shape[1] // 9
    for parcel, cells in zip((up, down), arrived_tiles(pair_offset())[1:]):
        for at, cell in enumerate(cells):
            add_tiles(owner_ref, sums, cell, parcel, at, capacity)


def more_sums(owner_map, sums, up, down):
    return pl.pallas_call(
        more_sums_kernel,
        out_shape=[pltpu.VMEM(x.shape, x.dtype) for x in sums],
        in_specs=[SMEM] + [VMEM] * (2 + len(sums)),
        out_specs=[VMEM] * len(sums),
        input_output_aliases={3 + i: i for i in range(len(sums))},
        compiler_params=PARAMS,
        cost_estimate=pl.CostEstimate(flops=10**9, bytes_accessed=10**6, transcendentals=0),
        name="more_sums",
    )(owner_map, resident(up), resident(down), *sums)


def owner_kernel(owner_ref, far, *rest):
    sums, (out_ref, stage_ref, sems) = rest[-3 - OWNER_SUMS : -3], rest[-3:]
    capacity = owner_ref.shape[1] // 9
    for at, cell in enumerate(arrived_tiles(pair_offset())[0]):
        add_tiles(owner_ref, sums, cell, far, at, capacity)
    owned, half, kc2 = sums[0].shape
    left = lax.broadcasted_iota(jnp.int32, (8, kc2), 1) < kc2 // 2
    copies = []
    for row in range(0, half, 8):
        for i in range(owned // 2):
            first = functools.reduce(jnp.add, [ref[2 * i, row : row + 8] for ref in sums])
            second = functools.reduce(jnp.add, [ref[2 * i + 1, row : row + 8] for ref in sums])
            columns = pl.ds(i * kc2, kc2)
            stage_ref[row : row + 8, columns] = jnp.where(
                left, first, pltpu.roll(second, kc2 // 2, 1)
            )
            stage_ref[half + row : half + row + 8, columns] = jnp.where(
                left, pltpu.roll(first, kc2 // 2, 1), second
            )
        for at in (row, half + row):
            rows = pl.ds(at, 8)
            copies.append(
                pltpu.make_async_copy(stage_ref.at[rows], out_ref.at[rows], sems.at[len(copies)])
            )
            copies[-1].start()
    for copy in copies:
        copy.wait()


def owner_sums(owner_map, sums, small, far):
    _, half, kc2 = sums[0].shape
    out = jax.ShapeDtypeStruct((2 * half, OWN * kc2 // 2), jnp.float32)
    results = pl.pallas_call(
        owner_kernel,
        out_shape=[pltpu.VMEM(x.shape, x.dtype) for x in sums] + [out],
        in_specs=[SMEM] + [VMEM] * (1 + len(sums)) + [HBM],
        out_specs=[VMEM] * len(sums) + [HBM],
        scratch_shapes=[
            pltpu.VMEM(out.shape, out.dtype),
            pltpu.SemaphoreType.DMA((2 * half // 8,)),
        ],
        input_output_aliases={2 + i: i for i in range(len(sums))},
        compiler_params=PARAMS,
        name="owner_sums",
    )(owner_map, resident(far), *sums, small)
    return results[-1]


def body(a_strips, p_strips, nbr_local, ap_slot, tile_slot, send_rows, owner_map):
    tiles_total = owner_map.shape[1]

    def local_work(nbr):
        return local_part(
            a_strips, p_strips, nbr, ap_slot, tile_slot.shape[2], send_rows.shape[2]
        )

    (*sums, ga, pt, info, order), arrived = exchange_rows(
        pack(send_rows, p_strips), nbr_local, local_work
    )
    for stage in range(len(STAGES)):
        sums = finish(stage, info, order, tile_slot, ga, pt, arrived, sums, tiles_total)
    *parcels, own = sums[2 + SUMS :]
    (*sums, small), (far, up, down) = exchange_tiles(
        parcels, owner_map, functools.partial(first_sums, own)
    )
    sums = more_sums(owner_map, sums, up, down)
    return owner_sums(owner_map, sums, small, far)


def solution(mesh):
    placed = (
        P(("dom", "grp"), None, None),
        P(("dom", "grp"), None, None),
        P(("dom", "grp"), None),
        P(("dom", "grp"), None, None),
        P(("dom", "grp"), None, None),
        P(("dom", "grp"), None, None),
        P(("dom", "grp"), None),
    )
    return jax.shard_map(
        body, mesh=mesh, in_specs=placed, out_specs=P(None, ("dom", "grp")), check_vma=False
    )
```

time: 60.7 us -> 58.2 us (0.959); the launches traced: 59.6 us -> 57.7 us
  Pallas kernels: 25.3 us -> 28.8 us
  waiting for transfers between devices: 10.6 us -> 7.65 us
  starting transfers between devices: 23.3 us -> 20.9 us
    ppermute x12, waiting for transfers between devices: 10.6 us -> 7.65 us  [moved(): return lax.ppermute(x, ('dom', 'grp'), pairs)]
    ppermute x12, starting transfers between devices: 23.3 us -> 20.9 us  [moved(): return lax.ppermute(x, ('dom', 'grp'), pairs)]
    pallas_call x3 -> x6, Pallas kernels: 12.2 us -> 14.3 us  [the longest x3 10.7 us: finish(): pl.pallas_call(functools.partial(finish_kernel, stage), out_shape=out_sha...]
    pallas_call x1, Pallas kernels: 11.6 us -> 13 us  [local_part(): pl.pallas_call(functools.partial(local_kernel, ghosts, slots), out_shape=...]
  transfers between devices with their start and end apart: 12 -> 12, of which waited for: 4 -> 2; matrix products, arithmetic and copies ran while one was open for 0% -> 0% of each run, Pallas kernels for 29% -> 37%
where the time goes in v5:
time: 58.2 us; the launch traced here: 57.7 us
  Pallas kernels  28.8 us (49%)
  starting transfers between devices  20.9 us (36%)
  waiting for transfers between devices  7.65 us (13%)
    ppermute x12, starting transfers between devices, moved(): return lax.ppermute(x, ('dom', 'grp'), pairs)  20.9 us
    pallas_call x1, Pallas kernels, local_part(): pl.pallas_call(functools.partial(local_kernel, ghosts, slots), out_shape=...  13 us
    pallas_call x3, Pallas kernels, finish(): pl.pallas_call(functools.partial(finish_kernel, stage), out_shape=out_sha...  10.7 us
    ppermute x12, waiting for transfers between devices, moved(): return lax.ppermute(x, ('dom', 'grp'), pairs)  7.65 us
    pallas_call x1, Pallas kernels, owner_sums(): pl.pallas_call(owner_kernel, out_shape=[pltpu.VMEM(x.shape, x.dtype) for...  2.24 us
    pallas_call x1, Pallas kernels, pack(): pl.pallas_call(pack_kernel, out_shape=[pltpu.VMEM((len(cells) * ghosts,)...  1.5 us
  transfers between devices with their start and end apart: 12, of which 2 were waited for; matrix products, arithmetic and copies ran while one was open for 0% of the time, Pallas kernels for 37%

profile of v5, /device:TPU:1, one launch (start us, length us, event | category | flops | bytes accessed | tf_op | source)
XLA Modules:
  0.0 57.7 jit_solution(12079263908577640495)
XLA Ops:
  0.0 1.5 %pack.1 = (bf16[18,64,256]{2,1,0:T(8,128)(2,1)S(1)}, bf16[18,64,256]{2,1,0:T(8,128)(2,1)S(1)}, bf16[6,64,256]{2,1,0:T(8,128)(2,1)S(1)}, bf16[6,64,256]{2,1,0:T(8,128)(2,1)S(1)}) custom-call(s32[6,1,8]{2,1,0:T(1,128)} %bitcast.9, bf16[32,64,256]{2,1,0:T(8,128)(2,1)} %p_ref.1), custom_call_target="tpu_custom_call" | custom-call | tf_op jit(solution)/shard_map/pack/pallas_call | solution.py:118
  1.5 0.1 collective-permute-start
  1.6 2.6 %collective-permute-start.1 = (bf16[18,64,256]{2,1,0:T(8,128)(2,1)S(1)}, bf16[18,64,256]{2,1,0:T(8,128)(2,1)S(1)}, u32[]{:S(2)}, u32[]{:S(2)}) collective-permute-start(bf16[18,64,256]{2,1,0:T(8,128)(2,1)S(1)} %get-tuple-element.53), channel_id=1, source_target_pairs={{0,3},{1,2},{2,1},{3,0},{4,7},{5,6},{6,5},{7,4},{8,11},{9,10},{10,... | collective-permute-start | bytes 1769480 | tf_op jit(solution)/shard_map/ppermute | solution.py:36
  4.3 0.0 collective-permute-done.rest_0_
  4.3 0.1 pad_maximum_fusion
  4.4 1.7 %collective-permute-start.4 = (bf16[12,64,256]{2,1,0:T(8,128)(2,1)S(1)}, bf16[12,64,256]{2,1,0:T(8,128)(2,1)S(1)}, u32[]{:S(2)}, u32[]{:S(2)}) collective-permute-start(bf16[12,64,256]{2,1,0:T(8,128)(2,1)S(1)} %get-tuple-element.59), channel_id=1, source_target_pairs={{0,4},{1,5},{2,6},{3,7},{4,8},{5,9},{6,10},{7,11},{8,12},{9,13},{1... | collective-permute-start | bytes 1179656 | tf_op jit(solution)/shard_map/ppermute | solution.py:36
  6.1 3.1 %collective-permute-start.5 = (bf16[12,64,256]{2,1,0:T(8,128)(2,1)S(1)}, bf16[12,64,256]{2,1,0:T(8,128)(2,1)S(1)}, u32[]{:S(2)}, u32[]{:S(2)}) collective-permute-start(bf16[12,64,256]{2,1,0:T(8,128)(2,1)S(1)} %get-tuple-element.60), channel_id=1, source_target_pairs={{0,28},{1,29},{2,30},{3,31},{4,0},{5,1},{6,2},{7,3},{8,4},{9,5},{1... | collective-permute-start | bytes 1179656 | tf_op jit(solution)/shard_map/ppermute | solution.py:36
  9.2 0.0 copy-start.1
  9.3 13.0 %local_part.1 = (f32[288,64,128]{2,1,0:T(8,128)S(1)}, f32[288,64,128]{2,1,0:T(8,128)S(1)}, bf16[196,64,64]{2,1,0:T(8,128)(2,1)S(1)}, bf16[32,128,128]{2,1,0:T(8,...) custom-call(s32[7,32]{1,0:T(8,128)S(1)} %bitcast.8, s32[7,4,32]{2,1,0:T(4,128)S(1)} %bitcast.7, ...), custom_call_target="tpu_custom_call" | custom-call | flops 5000000000 | bytes 10000000 | tf_op jit(solution)/shard_map/local_part/pallas_call | solution.py:224
  22.2 0.0 collective-permute-done.1.rest_1_
  22.3 1.5 %collective-permute-start.3 = (bf16[6,64,256]{2,1,0:T(8,128)(2,1)S(1)}, bf16[6,64,256]{2,1,0:T(8,128)(2,1)S(1)}, u32[]{:S(2)}, u32[]{:S(2)}) collective-permute-start(bf16[6,64,256]{2,1,0:T(8,128)(2,1)S(1)} %get-tuple-element.91), channel_id=1, source_target_pairs={{0,28},{1,29},{2,30},{3,31},{4,0},{5,1},{6,2},{7,3},{8,4},{9,5},{1... | collective-permute-start | bytes 589832 | tf_op jit(solution)/shard_map/ppermute | solution.py:36
  23.8 0.1 collective-permute-start.2
  23.8 3.1 %first_part.1 = (f32[288,64,128]{2,1,0:T(8,128)S(1)}, f32[288,64,128]{2,1,0:T(8,128)S(1)}, f32[72,32,128]{2,1,0:T(8,128)S(1)}, f32[72,32,128]{2,1,0:T(8,128)S(1)...) custom-call(s32[3528]{0:T(1024)S(1)} %get-tuple-element.52.info_ref, ...), custom_call_target="tpu_custom_call", output_to_operand_aliasing={{0}: (7, {}), {1}: (8, {})} | custom-call | flops 2000000000 | bytes 1000000 | tf_op jit(solution)/shard_map/first_part/pallas_call | solution.py:338
  26.9 0.0 collective-permute-done.4.rest_0_
  26.9 0.0 collective-permute-done.5.rest_1_
  26.9 4.0 %middle_part.1 = (f32[288,64,128]{2,1,0:T(8,128)S(1)}, f32[288,64,128]{2,1,0:T(8,128)S(1)}, f32[72,32,128]{2,1,0:T(8,128)S(1)}, f32[72,32,128]{2,1,0:T(8,128)S(1...) custom-call(s32[3528]{0:T(1024)S(1)} %get-tuple-element.52.info_ref,, ...), custom_call_target="tpu_custom_call", output_to_operand_aliasing={{0}: (7, {}), {1}: (8, {}), {2}: (9, {}), {3}: (10, {}), {4... | custom-call | flops 2000000000 | bytes 1000000 | tf_op jit(solution)/shard_map/middle_part/pallas_call | solution.py:338
  30.9 2.7 %collective-permute-done.3.rest_1_ = bf16[6,64,256]{2,1,0:T(8,128)(2,1)S(1)} collective-permute-done((bf16[6,64,256]{2,1,0:T(8,128)(2,1)S(1)}, bf16[6,64,256]{2,1,0:T(8,128)(2,1)S(1)}, u32[]{:S(2)}, u32[]{:S(2)}) %collective-permute-start.3) | collective-permute-done | bytes 196640 | tf_op jit(solution)/shard_map/ppermute | solution.py:36
  33.5 0.0 collective-permute-done.2.rest_0_
  33.5 3.7 %last_part.1 = (f32[288,64,128]{2,1,0:T(8,128)S(1)}, f32[288,64,128]{2,1,0:T(8,128)S(1)}, f32[72,32,128]{2,1,0:T(8,128)S(1)}, f32[72,32,128]{2,1,0:T(8,128)S(1)}...) custom-call(s32[3528]{0:T(1024)S(1)} %get-tuple-element.52.info_ref,, ...), custom_call_target="tpu_custom_call", output_to_operand_aliasing={{0}: (7, {}), {1}: (8, {}), {2}: (9, {}), {3}: (10, {}), {4... | custom-call | flops 2000000000 | bytes 1000000 | tf_op jit(solution)/shard_map/last_part/pallas_call | solution.py:338
  37.2 1.0 %collective-permute-start.8 = (bf16[24,32,128]{2,1,0:T(8,128)(2,1)S(1)}, bf16[24,32,128]{2,1,0:T(8,128)(2,1)S(1)}, u32[]{:S(2)}, u32[]{:S(2)}) collective-permute-start(bf16[24,32,128]{2,1,0:T(8,128)(2,1)S(1)} %get-tuple-element.79), channel_id=1, source_target_pairs={{0,1},{1,0},{2,3},{3,2},{4,5},{5,4},{6,7},{7,6},{8,9},{9,8},{10,11... | collective-permute-start | bytes 589832 | tf_op jit(solution)/shard_map/ppermute | solution.py:36
  38.2 0.0 collective-permute-start.6
  38.3 4.1 %collective-permute-start.7 = (bf16[8,32,128]{2,1,0:T(8,128)(2,1)S(1)}, bf16[8,32,128]{2,1,0:T(8,128)(2,1)S(1)}, u32[]{:S(2)}, u32[]{:S(2)}) collective-permute-start(bf16[8,32,128]{2,1,0:T(8,128)(2,1)S(1)} %get-tuple-element.77), channel_id=1, source_target_pairs={{0,28},{1,29},{2,30},{3,31},{4,0},{5,1},{6,2},{7,3},{8,4},{9,5},{1... | collective-permute-start | bytes 196616 | tf_op jit(solution)/shard_map/ppermute | solution.py:36
  42.4 0.0 collective-permute-done.8.pair
  42.5 0.1 collective-permute-start.10
  42.6 4.1 %collective-permute-start.11 = (bf16[16,32,128]{2,1,0:T(8,128)(2,1)S(1)}, bf16[16,32,128]{2,1,0:T(8,128)(2,1)S(1)}, u32[]{:S(2)}, u32[]{:S(2)}) collective-permute-start(bf16[16,32,128]{2,1,0:T(8,128)(2,1)S(1)} %pad_maximum_fusion.4), channel_id=1, source_target_pairs={{0,28},{1,29},{2,30},{3,31},{4,0},{5,1},{6,2},{7,3},{8,4},{9,5},{1... | collective-permute-start | bytes 393224 | tf_op jit(solution)/shard_map/ppermute | solution.py:36
  46.7 0.7 %first_sums.1 = (f32[128,32,128]{2,1,0:T(8,128)S(1)}, f32[8,128]{1,0:T(8,128)S(1)}) custom-call(s32[1,72]{1,0:T(1,128)S(1)} %copy-done.2, f32[8,32,128]{2,1,0:T(8,128)S(1)} %get-tuple-element.82.own, bf16[24,32,128]{2,1,0:T(8,128)(2,1)S(1)} %collective-permute-done.8.pair), custom_call_target="tpu_custom_call" | custom-call | flops 1000000000 | bytes 1000000 | tf_op jit(solution)/shard_map/first_sums/pallas_call | solution.py:379
  47.4 0.0 collective-permute-done.6
  47.5 0.0 collective-permute-done.7
  47.5 2.3 %collective-permute-start.9 = (bf16[24,32,128]{2,1,0:T(8,128)(2,1)S(1)}, bf16[24,32,128]{2,1,0:T(8,128)(2,1)S(1)}, u32[]{:S(2)}, u32[]{:S(2)}) collective-permute-start(bf16[24,32,128]{2,1,0:T(8,128)(2,1)S(1)} %pad_maximum_fusion.2), channel_id=1, source_target_pairs={{0,3},{1,2},{2,1},{3,0},{4,7},{5,6},{6,5},{7,4},{8,11},{9,10},{10,... | collective-permute-start | bytes 589832 | tf_op jit(solution)/shard_map/ppermute | solution.py:36
  49.8 0.7 %more_sums.1.rest_0_ = f32[128,32,128]{2,1,0:T(8,128)S(1)} custom-call(s32[1,72]{1,0:T(1,128)S(1)} %copy-done.2, bf16[16,32,128]{2,1,0:T(8,128)(2,1)S(1)} %collective-permute-done.10.up, bf16[16,32,128]{2,1,0:T(8,128)(2,1)S(1)} %collective-permute-done.11.down, f32[128,32,128]{2,1,0:T(8,128)S(1)} %get-tuple-element.88.rest_0_), custom_call_target="tpu_custom_call", output_to_operand_aliasing={{}: (3, {})} | custom-call | flops 1000000000 | bytes 1000000 | tf_op jit(solution)/shard_map/more_sums/pallas_call | solution.py:401
  50.5 5.0 %collective-permute-done.9.far = bf16[24,32,128]{2,1,0:T(8,128)(2,1)S(1)} collective-permute-done((bf16[24,32,128]{2,1,0:T(8,128)(2,1)S(1)}, bf16[24,32,128]{2,1,0:T(8,128)(2,1)S(1)}, u32[]{:S(2)}, u32[]{:S(2)}) %collective-permute-start.9) | collective-permute-done | bytes 196640 | tf_op jit(solution)/shard_map/ppermute | solution.py:36
  55.5 2.2 %owner_sums.1 = (f32[128,32,128]{2,1,0:T(8,128)S(1)}, f32[64,8192]{1,0:T(8,128)}) custom-call(s32[1,72]{1,0:T(1,128)S(1)} %copy-done.2, bf16[24,32,128]{2,1,0:T(8,128)(2,1)S(1)} %collective-permute-done.9.far, f32[128,32,128]{2,1,0:T(8,128)S(1)} %more_sums.1.rest_0_, f32[8,128]{1,0:T(8,128)S(1)} %get-tuple-element.89.rest_1_), custom_call_target="tpu_custom_call", output_to_operand_aliasing={{0}: (2, {})} | custom-call | tf_op jit(solution)/shard_map/owner_sums/pallas_call | solution.py:445
  (19 shorter events, 0.1 us)
Async XLA Ops:
  0.0 9.2 %copy-start = (bf16[32,64,256]{2,1,0:T(8,128)(2,1)S(1)}, bf16[32,64,256]{2,1,0:T(8,128)(2,1)}, u32[]{:S(2)}) copy-start(bf16[32,64,256]{2,1,0:T(8,128)(2,1)} %p_ref.1) | copy-start | bytes 3145732
  0.0 9.2 %copy-start.5 = (s32[32,7]{0,1:T(8,128)S(1)}, s32[32,7]{0,1:T(8,128)}, u32[]{:S(2)}) copy-start(s32[32,7]{0,1:T(8,128)} %param.9) | copy-start | bytes 2692
  0.0 9.2 %copy-start.4 = (s32[32,7,4]{0,2,1:T(4,128)S(1)}, s32[32,7,4]{0,2,1:T(4,128)}, u32[]{:S(2)}) copy-start(s32[32,7,4]{0,2,1:T(4,128)} %param.10) | copy-start | bytes 10756
  0.0 9.2 %copy-start.3 = (bf16[32,64,448]{2,1,0:T(8,128)(2,1)S(1)}, bf16[32,64,448]{2,1,0:T(8,128)(2,1)}, u32[]{:S(2)}) copy-start(bf16[32,64,448]{2,1,0:T(8,128)(2,1)} %a_ref.1) | copy-start | bytes 5505028
  1.5 2.7 %collective-permute-start = (bf16[18,64,256]{2,1,0:T(8,128)(2,1)S(1)}, bf16[18,64,256]{2,1,0:T(8,128)(2,1)S(1)}, u32[]{:S(2)}, u32[]{:S(2)}) collective-permute-start(bf16[18,64,256]{2,1,0:T(8,128)(2,1)S(1)} %get-tuple-element.49), channel_id=1, source_target_pairs={{0,1},{1,0},{2,3},{3,2},{4,5},{5,4},{6,7},{7,6},{8,9},{9,8},{10,11... | collective-permute-start | bytes 1769480 | tf_op jit(solution)/shard_map/ppermute | solution.py:36
  1.6 20.6 %collective-permute-start.1 = (bf16[18,64,256]{2,1,0:T(8,128)(2,1)S(1)}, bf16[18,64,256]{2,1,0:T(8,128)(2,1)S(1)}, u32[]{:S(2)}, u32[]{:S(2)}) collective-permute-start(bf16[18,64,256]{2,1,0:T(8,128)(2,1)S(1)} %get-tuple-element.53), channel_id=1, source_target_pairs={{0,3},{1,2},{2,1},{3,0},{4,7},{5,6},{6,5},{7,4},{8,11},{9,10},{10,... | collective-permute-start | bytes 1769480 | tf_op jit(solution)/shard_map/ppermute | solution.py:36
  4.4 22.5 %collective-permute-start.4 = (bf16[12,64,256]{2,1,0:T(8,128)(2,1)S(1)}, bf16[12,64,256]{2,1,0:T(8,128)(2,1)S(1)}, u32[]{:S(2)}, u32[]{:S(2)}) collective-permute-start(bf16[12,64,256]{2,1,0:T(8,128)(2,1)S(1)} %get-tuple-element.59), channel_id=1, source_target_pairs={{0,4},{1,5},{2,6},{3,7},{4,8},{5,9},{6,10},{7,11},{8,12},{9,13},{1... | collective-permute-start | bytes 1179656 | tf_op jit(solution)/shard_map/ppermute | solution.py:36
  6.1 20.8 %collective-permute-start.5 = (bf16[12,64,256]{2,1,0:T(8,128)(2,1)S(1)}, bf16[12,64,256]{2,1,0:T(8,128)(2,1)S(1)}, u32[]{:S(2)}, u32[]{:S(2)}) collective-permute-start(bf16[12,64,256]{2,1,0:T(8,128)(2,1)S(1)} %get-tuple-element.60), channel_id=1, source_target_pairs={{0,28},{1,29},{2,30},{3,31},{4,0},{5,1},{6,2},{7,3},{8,4},{9,5},{1... | collective-permute-start | bytes 1179656 | tf_op jit(solution)/shard_map/ppermute | solution.py:36
  9.2 14.6 %copy-start.1 = (s32[32,4,8]{0,2,1:T(8,128)S(1)}, s32[32,4,8]{0,2,1:T(8,128)}, u32[]{:S(2)}) copy-start(s32[32,4,8]{0,2,1:T(8,128)} %param.11) | copy-start | bytes 12292
  22.3 11.2 %collective-permute-start.3 = (bf16[6,64,256]{2,1,0:T(8,128)(2,1)S(1)}, bf16[6,64,256]{2,1,0:T(8,128)(2,1)S(1)}, u32[]{:S(2)}, u32[]{:S(2)}) collective-permute-start(bf16[6,64,256]{2,1,0:T(8,128)(2,1)S(1)} %get-tuple-element.91), channel_id=1, source_target_pairs={{0,28},{1,29},{2,30},{3,31},{4,0},{5,1},{6,2},{7,3},{8,4},{9,5},{1... | collective-permute-start | bytes 589832 | tf_op jit(solution)/shard_map/ppermute | solution.py:36
  23.8 9.8 %collective-permute-start.2 = (bf16[6,64,256]{2,1,0:T(8,128)(2,1)S(1)}, bf16[6,64,256]{2,1,0:T(8,128)(2,1)S(1)}, u32[]{:S(2)}, u32[]{:S(2)}) collective-permute-start(bf16[6,64,256]{2,1,0:T(8,128)(2,1)S(1)} %get-tuple-element.92), channel_id=1, source_target_pairs={{0,4},{1,5},{2,6},{3,7},{4,8},{5,9},{6,10},{7,11},{8,12},{9,13},{1... | collective-permute-start | bytes 589832 | tf_op jit(solution)/shard_map/ppermute | solution.py:36
  33.5 13.2 %copy-start.2 = (s32[1,72]{1,0:T(1,128)S(1)}, s32[1,72]{1,0:T(1,128)}, u32[]{:S(2)}) copy-start(s32[1,72]{1,0:T(1,128)} %owner_ref.4) | copy-start | bytes 868
  37.2 5.2 %collective-permute-start.8 = (bf16[24,32,128]{2,1,0:T(8,128)(2,1)S(1)}, bf16[24,32,128]{2,1,0:T(8,128)(2,1)S(1)}, u32[]{:S(2)}, u32[]{:S(2)}) collective-permute-start(bf16[24,32,128]{2,1,0:T(8,128)(2,1)S(1)} %get-tuple-element.79), channel_id=1, source_target_pairs={{0,1},{1,0},{2,3},{3,2},{4,5},{5,4},{6,7},{7,6},{8,9},{9,8},{10,11... | collective-permute-start | bytes 589832 | tf_op jit(solution)/shard_map/ppermute | solution.py:36
  38.2 9.2 %collective-permute-start.6 = (bf16[8,32,128]{2,1,0:T(8,128)(2,1)S(1)}, bf16[8,32,128]{2,1,0:T(8,128)(2,1)S(1)}, u32[]{:S(2)}, u32[]{:S(2)}) collective-permute-start(bf16[8,32,128]{2,1,0:T(8,128)(2,1)S(1)} %get-tuple-element.76), channel_id=1, source_target_pairs={{0,4},{1,5},{2,6},{3,7},{4,8},{5,9},{6,10},{7,11},{8,12},{9,13},{1... | collective-permute-start | bytes 196616 | tf_op jit(solution)/shard_map/ppermute | solution.py:36
  38.3 9.2 %collective-permute-start.7 = (bf16[8,32,128]{2,1,0:T(8,128)(2,1)S(1)}, bf16[8,32,128]{2,1,0:T(8,128)(2,1)S(1)}, u32[]{:S(2)}, u32[]{:S(2)}) collective-permute-start(bf16[8,32,128]{2,1,0:T(8,128)(2,1)S(1)} %get-tuple-element.77), channel_id=1, source_target_pairs={{0,28},{1,29},{2,30},{3,31},{4,0},{5,1},{6,2},{7,3},{8,4},{9,5},{1... | collective-permute-start | bytes 196616 | tf_op jit(solution)/shard_map/ppermute | solution.py:36
  42.5 7.4 %collective-permute-start.10 = (bf16[16,32,128]{2,1,0:T(8,128)(2,1)S(1)}, bf16[16,32,128]{2,1,0:T(8,128)(2,1)S(1)}, u32[]{:S(2)}, u32[]{:S(2)}) collective-permute-start(bf16[16,32,128]{2,1,0:T(8,128)(2,1)S(1)} %pad_maximum_fusion.3), channel_id=1, source_target_pairs={{0,4},{1,5},{2,6},{3,7},{4,8},{5,9},{6,10},{7,11},{8,12},{9,13},{1... | collective-permute-start | bytes 393224 | tf_op jit(solution)/shard_map/ppermute | solution.py:36
  42.6 7.3 %collective-permute-start.11 = (bf16[16,32,128]{2,1,0:T(8,128)(2,1)S(1)}, bf16[16,32,128]{2,1,0:T(8,128)(2,1)S(1)}, u32[]{:S(2)}, u32[]{:S(2)}) collective-permute-start(bf16[16,32,128]{2,1,0:T(8,128)(2,1)S(1)} %pad_maximum_fusion.4), channel_id=1, source_target_pairs={{0,28},{1,29},{2,30},{3,31},{4,0},{5,1},{6,2},{7,3},{8,4},{9,5},{1... | collective-permute-start | bytes 393224 | tf_op jit(solution)/shard_map/ppermute | solution.py:36
  47.5 8.0 %collective-permute-start.9 = (bf16[24,32,128]{2,1,0:T(8,128)(2,1)S(1)}, bf16[24,32,128]{2,1,0:T(8,128)(2,1)S(1)}, u32[]{:S(2)}, u32[]{:S(2)}) collective-permute-start(bf16[24,32,128]{2,1,0:T(8,128)(2,1)S(1)} %pad_maximum_fusion.2), channel_id=1, source_target_pairs={{0,3},{1,2},{2,1},{3,0},{4,7},{5,6},{6,5},{7,4},{8,11},{9,10},{10,... | collective-permute-start | bytes 589832 | tf_op jit(solution)/shard_map/ppermute | solution.py:36

commit v6 on v5

--- a/solution.py
+++ b/solution.py
@@ -54,17 +54,15 @@
     return (*results, small), (pair, far, up, down, up_far, down_far)
 
 
-def exchange_tiles(parts, owner_map, first_sums):
-    pair, far, up, down, up_far, down_far = parts
-    size = up.shape[0]
-    pair = moved(pair, 0, "pair")
-    up_far, down_far = moved(up_far, 1, "own"), moved(down_far, -1, "own")
-    up, down = jnp.concatenate([up, pair[size : 2 * size]]), jnp.concatenate([down, pair[2 * size :]])
-    up, down, owner_map = lax.optimization_barrier((up, down, owner_map))
-    sums, small = first_sums(pair, owner_map)
-    up_far, down_far, small = lax.optimization_barrier((up_far, down_far, small))
-    far = moved(jnp.concatenate([far, up_far, down_far]), 0, "far")
-    return (*sums, small), (far, moved(up, 1, "own"), moved(down, -1, "own"))
+def exchange_tiles(parts, first_sums):
+    up, down, far, up_far, down_far, pair = parts
+    size = pair.shape[0]
+    up, down, far = moved(up, 1, "own"), moved(down, -1, "own"), moved(far, 0, "far")
+    up_far, down_far = moved(up_far, 1, "far"), moved(down_far, -1, "far")
+    sums, small = first_sums()
+    up, down, small = lax.optimization_barrier((up, down, small))
+    pair = moved(jnp.concatenate([pair, up[size:], down[size:]]), 0, "pair")
+    return sums, small, (up, down, far, up_far, down_far, pair)
 
 
 def pair_offset():
@@ -80,11 +78,11 @@
 
 
 def sent_tiles(offset):
-    return (4 + offset, 7 + offset, 1 + offset), (4 - offset,), (7,), (1,), (7 - offset,), (1 - offset,)
+    return (7, 7 + offset), (1, 1 + offset), (4 - offset,), (7 - offset,), (1 - offset,), (4 + offset,)
 
 
 def arrived_tiles(offset):
-    return (4 - offset, 1 - offset, 7 - offset), (1, 1 + offset), (7, 7 + offset)
+    return (1,), (7,), (4 - offset,), (1 - offset,), (7 - offset,), (4 + offset, 1 + offset, 7 + offset)
 
 
 STAGES = ((0, 1), (2, 3), (4, 5))
@@ -364,57 +362,55 @@
         ref[owner_ref[0, cell * capacity + g]] += parcel[at * capacity + g].astype(jnp.float32)
 
 
-def first_sums_kernel(owner_ref, own, pair, *rest):
+def first_sums_kernel(owner_ref, own, *rest):
     sums, small = rest[:-1], rest[-1]
     for ref in sums:
         ref[...] = jnp.zeros_like(ref)
-    capacity = own.shape[0]
-    add_tiles(owner_ref, sums, 4, own, 0, capacity)
-    add_tiles(owner_ref, sums, 4 + pair_offset(), pair, 0, capacity)
+    add_tiles(owner_ref, sums, 4, own, 0, own.shape[0])
     small[...] = jnp.zeros_like(small)
 
 
-def first_sums(own, pair, owner_map):
+def first_sums(owner_map, own):
     _, half, kc2 = own.shape
     *sums, small = pl.pallas_call(
         first_sums_kernel,
         out_shape=[pltpu.VMEM((OWN, half, kc2), jnp.float32)] * OWNER_SUMS
         + [jax.ShapeDtypeStruct((8, 128), jnp.float32)],
-        in_specs=[SMEM, VMEM, VMEM],
+        in_specs=[SMEM, VMEM],
         out_specs=[VMEM] * (OWNER_SUMS + 1),
         compiler_params=PARAMS,
         cost_estimate=pl.CostEstimate(flops=10**9, bytes_accessed=10**6, transcendentals=0),
         name="first_sums",
-    )(owner_map, resident(own), resident(pair))
+    )(owner_map, resident(own))
     return sums, small
 
 
-def more_sums_kernel(owner_ref, up, down, *rest):
-    sums = rest[-OWNER_SUMS:]
+def more_sums_kernel(owner_ref, *rest):
+    arrived, sums = rest[: -2 * OWNER_SUMS], rest[-OWNER_SUMS:]
     capacity = owner_ref.shape[1] // 9
-    for parcel, cells in zip((up, down), arrived_tiles(pair_offset())[1:]):
-        for at, cell in enumerate(cells):
-            add_tiles(owner_ref, sums, cell, parcel, at, capacity)
-
-
-def more_sums(owner_map, sums, up, down):
+    for parcel, cells in zip(arrived, arrived_tiles(pair_offset())):
+        add_tiles(owner_ref, sums, cells[0], parcel, 0, capacity)
+
+
+def more_sums(owner_map, sums, arrived):
+    inputs = 1 + len(arrived)
     return pl.pallas_call(
         more_sums_kernel,
         out_shape=[pltpu.VMEM(x.shape, x.dtype) for x in sums],
-        in_specs=[SMEM] + [VMEM] * (2 + len(sums)),
+        in_specs=[SMEM] + [VMEM] * (len(arrived) + len(sums)),
         out_specs=[VMEM] * len(sums),
-        input_output_aliases={3 + i: i for i in range(len(sums))},
-        compiler_params=PARAMS,
-        cost_estimate=pl.CostEstimate(flops=10**9, bytes_accessed=10**6, transcendentals=0),
+        input_output_aliases={inputs + i: i for i in range(len(sums))},
+        compiler_params=PARAMS,
+        cost_estimate=pl.CostEstimate(flops=2 * 10**10, bytes_accessed=10**6, transcendentals=0),
         name="more_sums",
-    )(owner_map, resident(up), resident(down), *sums)
-
-
-def owner_kernel(owner_ref, far, *rest):
+    )(owner_map, *map(resident, arrived), *sums)
+
+
+def owner_kernel(owner_ref, pair, *rest):
     sums, (out_ref, stage_ref, sems) = rest[-3 - OWNER_SUMS : -3], rest[-3:]
     capacity = owner_ref.shape[1] // 9
-    for at, cell in enumerate(arrived_tiles(pair_offset())[0]):
-        add_tiles(owner_ref, sums, cell, far, at, capacity)
+    for at, cell in enumerate(arrived_tiles(pair_offset())[-1]):
+        add_tiles(owner_ref, sums, cell, pair, at, capacity)
     owned, half, kc2 = sums[0].shape
     left = lax.broadcasted_iota(jnp.int32, (8, kc2), 1) < kc2 // 2
     copies = []
@@ -439,7 +435,7 @@
         copy.wait()
 
 
-def owner_sums(owner_map, sums, small, far):
+def owner_sums(owner_map, sums, small, pair):
     _, half, kc2 = sums[0].shape
     out = jax.ShapeDtypeStruct((2 * half, OWN * kc2 // 2), jnp.float32)
     results = pl.pallas_call(
@@ -454,7 +450,7 @@
         input_output_aliases={2 + i: i for i in range(len(sums))},
         compiler_params=PARAMS,
         name="owner_sums",
-    )(owner_map, resident(far), *sums, small)
+    )(owner_map, resident(pair), *sums, small)
     return results[-1]
 
 
@@ -472,11 +468,11 @@
     for stage in range(len(STAGES)):
         sums = finish(stage, info, order, tile_slot, ga, pt, arrived, sums, tiles_total)
     *parcels, own = sums[2 + SUMS :]
-    (*sums, small), (far, up, down) = exchange_tiles(
-        parcels, owner_map, functools.partial(first_sums, own)
-    )
-    sums = more_sums(owner_map, sums, up, down)
-    return owner_sums(owner_map, sums, small, far)
+    sums, small, (*parcels, pair) = exchange_tiles(
+        parcels, functools.partial(first_sums, owner_map, own)
+    )
+    sums = more_sums(owner_map, sums, parcels)
+    return owner_sums(owner_map, sums, small, pair)
 
 
 def solution(mesh):

time: 58.2 us -> 54.4 us (0.935)
  waiting for transfers between devices: 7.65 us -> 3.75 us
    ppermute x12, waiting for transfers between devices: 7.65 us -> 3.75 us  [moved(): return lax.ppermute(x, ('dom', 'grp'), pairs)]
  transfers between devices with their start and end apart: 12 -> 12, of which waited for: 2 -> 2; matrix products, arithmetic and copies ran while one was open for 0% -> 0% of each run, Pallas kernels for 37% -> 39%
where the time goes in v6:
time: 54.4 us; the launch traced here: 54.3 us
  Pallas kernels  28.8 us (53%)
  starting transfers between devices  21.4 us (39%)
  waiting for transfers between devices  3.75 us (7%)
    ppermute x12, starting transfers between devices, moved(): return lax.ppermute(x, ('dom', 'grp'), pairs)  21.4 us
    pallas_call x1, Pallas kernels, local_part(): pl.pallas_call(functools.partial(local_kernel, ghosts, slots), out_shape=...  13 us
    pallas_call x3, Pallas kernels, finish(): pl.pallas_call(functools.partial(finish_kernel, stage), out_shape=out_sha...  10.7 us
    ppermute x12, waiting for transfers between devices, moved(): return lax.ppermute(x, ('dom', 'grp'), pairs)  3.75 us
    pallas_call x1, Pallas kernels, owner_sums(): pl.pallas_call(owner_kernel, out_shape=[pltpu.VMEM(x.shape, x.dtype) for...  2.24 us
    pallas_call x1, Pallas kernels, pack(): pl.pallas_call(pack_kernel, out_shape=[pltpu.VMEM((len(cells) * ghosts,)...  1.5 us
  transfers between devices with their start and end apart: 12, of which 2 were waited for; matrix products, arithmetic and copies ran while one was open for 0% of the time, Pallas kernels for 39%

profile of v6, /device:TPU:1, one launch (start us, length us, event | category | flops | bytes accessed | tf_op | source)
XLA Modules:
  0.0 54.3 jit_solution(808547339584452486)
XLA Ops:
  0.0 1.5 %pack.1 = (bf16[18,64,256]{2,1,0:T(8,128)(2,1)S(1)}, bf16[18,64,256]{2,1,0:T(8,128)(2,1)S(1)}, bf16[6,64,256]{2,1,0:T(8,128)(2,1)S(1)}, bf16[6,64,256]{2,1,0:T(8,128)(2,1)S(1)}) custom-call(s32[6,1,8]{2,1,0:T(1,128)} %bitcast.9, bf16[32,64,256]{2,1,0:T(8,128)(2,1)} %p_ref.1), custom_call_target="tpu_custom_call" | custom-call | tf_op jit(solution)/shard_map/pack/pallas_call | solution.py:116
  1.5 0.1 collective-permute-start
  1.6 2.6 %collective-permute-start.1 = (bf16[18,64,256]{2,1,0:T(8,128)(2,1)S(1)}, bf16[18,64,256]{2,1,0:T(8,128)(2,1)S(1)}, u32[]{:S(2)}, u32[]{:S(2)}) collective-permute-start(bf16[18,64,256]{2,1,0:T(8,128)(2,1)S(1)} %get-tuple-element.50), channel_id=1, source_target_pairs={{0,3},{1,2},{2,1},{3,0},{4,7},{5,6},{6,5},{7,4},{8,11},{9,10},{10,... | collective-permute-start | bytes 1769480 | tf_op jit(solution)/shard_map/ppermute | solution.py:36
  4.3 0.0 collective-permute-done.rest_0_
  4.3 0.1 pad_maximum_fusion
  4.4 1.7 %collective-permute-start.4 = (bf16[12,64,256]{2,1,0:T(8,128)(2,1)S(1)}, bf16[12,64,256]{2,1,0:T(8,128)(2,1)S(1)}, u32[]{:S(2)}, u32[]{:S(2)}) collective-permute-start(bf16[12,64,256]{2,1,0:T(8,128)(2,1)S(1)} %get-tuple-element.56), channel_id=1, source_target_pairs={{0,4},{1,5},{2,6},{3,7},{4,8},{5,9},{6,10},{7,11},{8,12},{9,13},{1... | collective-permute-start | bytes 1179656 | tf_op jit(solution)/shard_map/ppermute | solution.py:36
  6.1 3.1 %collective-permute-start.5 = (bf16[12,64,256]{2,1,0:T(8,128)(2,1)S(1)}, bf16[12,64,256]{2,1,0:T(8,128)(2,1)S(1)}, u32[]{:S(2)}, u32[]{:S(2)}) collective-permute-start(bf16[12,64,256]{2,1,0:T(8,128)(2,1)S(1)} %get-tuple-element.57), channel_id=1, source_target_pairs={{0,28},{1,29},{2,30},{3,31},{4,0},{5,1},{6,2},{7,3},{8,4},{9,5},{1... | collective-permute-start | bytes 1179656 | tf_op jit(solution)/shard_map/ppermute | solution.py:36
  9.2 0.0 copy-start.1
  9.3 13.0 %local_part.1 = (f32[288,64,128]{2,1,0:T(8,128)S(1)}, f32[288,64,128]{2,1,0:T(8,128)S(1)}, bf16[196,64,64]{2,1,0:T(8,128)(2,1)S(1)}, bf16[32,128,128]{2,1,0:T(8,...) custom-call(s32[7,32]{1,0:T(8,128)S(1)} %bitcast.8, s32[7,4,32]{2,1,0:T(4,128)S(1)} %bitcast.7, ...), custom_call_target="tpu_custom_call" | custom-call | flops 5000000000 | bytes 10000000 | tf_op jit(solution)/shard_map/local_part/pallas_call | solution.py:222
  22.2 0.0 collective-permute-done.1.rest_1_
  22.3 1.5 %collective-permute-start.3 = (bf16[6,64,256]{2,1,0:T(8,128)(2,1)S(1)}, bf16[6,64,256]{2,1,0:T(8,128)(2,1)S(1)}, u32[]{:S(2)}, u32[]{:S(2)}) collective-permute-start(bf16[6,64,256]{2,1,0:T(8,128)(2,1)S(1)} %get-tuple-element.85), channel_id=1, source_target_pairs={{0,28},{1,29},{2,30},{3,31},{4,0},{5,1},{6,2},{7,3},{8,4},{9,5},{1... | collective-permute-start | bytes 589832 | tf_op jit(solution)/shard_map/ppermute | solution.py:36
  23.8 0.1 collective-permute-start.2
  23.8 3.1 %first_part.1 = (f32[288,64,128]{2,1,0:T(8,128)S(1)}, f32[288,64,128]{2,1,0:T(8,128)S(1)}, f32[72,32,128]{2,1,0:T(8,128)S(1)}, f32[72,32,128]{2,1,0:T(8,128)S(1)...) custom-call(s32[3528]{0:T(1024)S(1)} %get-tuple-element.49.info_ref, ...), custom_call_target="tpu_custom_call", output_to_operand_aliasing={{0}: (7, {}), {1}: (8, {})} | custom-call | flops 2000000000 | bytes 1000000 | tf_op jit(solution)/shard_map/first_part/pallas_call | solution.py:336
  26.9 0.0 collective-permute-done.4.rest_0_
  26.9 0.0 collective-permute-done.5.rest_1_
  26.9 4.0 %middle_part.1 = (f32[288,64,128]{2,1,0:T(8,128)S(1)}, f32[288,64,128]{2,1,0:T(8,128)S(1)}, f32[72,32,128]{2,1,0:T(8,128)S(1)}, f32[72,32,128]{2,1,0:T(8,128)S(1...) custom-call(s32[3528]{0:T(1024)S(1)} %get-tuple-element.49.info_ref,, ...), custom_call_target="tpu_custom_call", output_to_operand_aliasing={{0}: (7, {}), {1}: (8, {}), {2}: (9, {}), {3}: (10, {}), {4... | custom-call | flops 2000000000 | bytes 1000000 | tf_op jit(solution)/shard_map/middle_part/pallas_call | solution.py:336
  30.9 2.7 %collective-permute-done.3.rest_1_ = bf16[6,64,256]{2,1,0:T(8,128)(2,1)S(1)} collective-permute-done((bf16[6,64,256]{2,1,0:T(8,128)(2,1)S(1)}, bf16[6,64,256]{2,1,0:T(8,128)(2,1)S(1)}, u32[]{:S(2)}, u32[]{:S(2)}) %collective-permute-start.3) | collective-permute-done | bytes 196640 | tf_op jit(solution)/shard_map/ppermute | solution.py:36
  33.5 0.0 collective-permute-done.2.rest_0_
  33.5 3.7 %last_part.1 = (f32[288,64,128]{2,1,0:T(8,128)S(1)}, f32[288,64,128]{2,1,0:T(8,128)S(1)}, f32[72,32,128]{2,1,0:T(8,128)S(1)}, f32[72,32,128]{2,1,0:T(8,128)S(1)}...) custom-call(s32[3528]{0:T(1024)S(1)} %get-tuple-element.49.info_ref,, ...), custom_call_target="tpu_custom_call", output_to_operand_aliasing={{0}: (7, {}), {1}: (8, {}), {2}: (9, {}), {3}: (10, {}), {4... | custom-call | flops 2000000000 | bytes 1000000 | tf_op jit(solution)/shard_map/last_part/pallas_call | solution.py:336
  37.2 0.1 collective-permute-start.6
  37.3 4.1 %collective-permute-start.7 = (bf16[16,32,128]{2,1,0:T(8,128)(2,1)S(1)}, bf16[16,32,128]{2,1,0:T(8,128)(2,1)S(1)}, u32[]{:S(2)}, u32[]{:S(2)}) collective-permute-start(bf16[16,32,128]{2,1,0:T(8,128)(2,1)S(1)} %get-tuple-element.74), channel_id=1, source_target_pairs={{0,28},{1,29},{2,30},{3,31},{4,0},{5,1},{6,2},{7,3},{8,4},{9,5},{1... | collective-permute-start | bytes 393224 | tf_op jit(solution)/shard_map/ppermute | solution.py:36
  41.4 2.6 %collective-permute-start.9 = (bf16[8,32,128]{2,1,0:T(8,128)(2,1)S(1)}, bf16[8,32,128]{2,1,0:T(8,128)(2,1)S(1)}, u32[]{:S(2)}, u32[]{:S(2)}) collective-permute-start(bf16[8,32,128]{2,1,0:T(8,128)(2,1)S(1)} %get-tuple-element.79), channel_id=1, source_target_pairs={{0,3},{1,2},{2,1},{3,0},{4,7},{5,6},{6,5},{7,4},{8,11},{9,10},{10,... | collective-permute-start | bytes 196616 | tf_op jit(solution)/shard_map/ppermute | solution.py:36
  44.1 0.0 collective-permute-start.10
  44.1 5.3 %collective-permute-start.11 = (bf16[8,32,128]{2,1,0:T(8,128)(2,1)S(1)}, bf16[8,32,128]{2,1,0:T(8,128)(2,1)S(1)}, u32[]{:S(2)}, u32[]{:S(2)}) collective-permute-start(bf16[8,32,128]{2,1,0:T(8,128)(2,1)S(1)} %get-tuple-element.81), channel_id=1, source_target_pairs={{0,31},{1,30},{2,29},{3,28},{4,3},{5,2},{6,1},{7,0},{8,7},{9,6},{1... | collective-permute-start | bytes 196616 | tf_op jit(solution)/shard_map/ppermute | solution.py:36
  49.4 0.7 %first_sums.1 = (f32[128,32,128]{2,1,0:T(8,128)S(1)}, f32[8,128]{1,0:T(8,128)S(1)}) custom-call(s32[1,72]{1,0:T(1,128)S(1)} %copy-done.2, f32[8,32,128]{2,1,0:T(8,128)S(1)} %get-tuple-element.75.own), custom_call_target="tpu_custom_call" | custom-call | flops 1000000000 | bytes 1000000 | tf_op jit(solution)/shard_map/first_sums/pallas_call | solution.py:375
  50.1 0.0 collective-permute-done.6.rest_0_
  50.1 0.0 collective-permute-done.7.rest_1_
  50.2 0.1 collective-permute-start.8
  50.3 0.0 collective-permute-done.9.rest_2_
  50.3 1.1 %collective-permute-done.10.rest_3_ = bf16[8,32,128]{2,1,0:T(8,128)(2,1)S(1)} collective-permute-done((bf16[8,32,128]{2,1,0:T(8,128)(2,1)S(1)}, bf16[8,32,128]{2,1,0:T(8,128)(2,1)S(1)}, u32[]{:S(2)}, u32[]{:S(2)}) %collective-permute-start.10) | collective-permute-done | bytes 65568 | tf_op jit(solution)/shard_map/ppermute | solution.py:36
  51.3 0.7 %more_sums.1.rest_0_ = f32[128,32,128]{2,1,0:T(8,128)S(1)} custom-call(s32[1,72]{1,0:T(1,128)S(1)} %copy-done.2, bf16[16,32,128]{2,1,0:T(8,128)(2,1)S(1)} %collective-permute-done.6.rest_0_, bf16[16,32,128]{2,1,0:T(8,128)(2,1)S(1)} %collective-permute-done.7.rest_1_, ...), custom_call_target="tpu_custom_call", output_to_operand_aliasing={{}: (6, {})} | custom-call | flops 20000000000 | bytes 1000000 | tf_op jit(solution)/shard_map/more_sums/pallas_call | solution.py:397
  52.1 2.2 %owner_sums.1 = (f32[128,32,128]{2,1,0:T(8,128)S(1)}, f32[64,8192]{1,0:T(8,128)}) custom-call(s32[1,72]{1,0:T(1,128)S(1)} %copy-done.2, bf16[24,32,128]{2,1,0:T(8,128)(2,1)S(1)} %collective-permute-done.8.pair, f32[128,32,128]{2,1,0:T(8,128)S(1)} %more_sums.1.rest_0_, f32[8,128]{1,0:T(8,128)S(1)} %get-tuple-element.83.rest_1_), custom_call_target="tpu_custom_call", output_to_operand_aliasing={{0}: (2, {})} | custom-call | tf_op jit(solution)/shard_map/owner_sums/pallas_call | solution.py:441
  (18 shorter events, 0.1 us)
Async XLA Ops:
  0.0 9.2 %copy-start = (bf16[32,64,256]{2,1,0:T(8,128)(2,1)S(1)}, bf16[32,64,256]{2,1,0:T(8,128)(2,1)}, u32[]{:S(2)}) copy-start(bf16[32,64,256]{2,1,0:T(8,128)(2,1)} %p_ref.1) | copy-start | bytes 3145732
  0.0 9.2 %copy-start.5 = (s32[32,7]{0,1:T(8,128)S(1)}, s32[32,7]{0,1:T(8,128)}, u32[]{:S(2)}) copy-start(s32[32,7]{0,1:T(8,128)} %param.9) | copy-start | bytes 2692
  0.0 9.2 %copy-start.4 = (s32[32,7,4]{0,2,1:T(4,128)S(1)}, s32[32,7,4]{0,2,1:T(4,128)}, u32[]{:S(2)}) copy-start(s32[32,7,4]{0,2,1:T(4,128)} %param.10) | copy-start | bytes 10756
  0.0 9.2 %copy-start.3 = (bf16[32,64,448]{2,1,0:T(8,128)(2,1)S(1)}, bf16[32,64,448]{2,1,0:T(8,128)(2,1)}, u32[]{:S(2)}) copy-start(bf16[32,64,448]{2,1,0:T(8,128)(2,1)} %a_ref.1) | copy-start | bytes 5505028
  1.5 2.7 %collective-permute-start = (bf16[18,64,256]{2,1,0:T(8,128)(2,1)S(1)}, bf16[18,64,256]{2,1,0:T(8,128)(2,1)S(1)}, u32[]{:S(2)}, u32[]{:S(2)}) collective-permute-start(bf16[18,64,256]{2,1,0:T(8,128)(2,1)S(1)} %get-tuple-element.46), channel_id=1, source_target_pairs={{0,1},{1,0},{2,3},{3,2},{4,5},{5,4},{6,7},{7,6},{8,9},{9,8},{10,11... | collective-permute-start | bytes 1769480 | tf_op jit(solution)/shard_map/ppermute | solution.py:36
  1.6 20.6 %collective-permute-start.1 = (bf16[18,64,256]{2,1,0:T(8,128)(2,1)S(1)}, bf16[18,64,256]{2,1,0:T(8,128)(2,1)S(1)}, u32[]{:S(2)}, u32[]{:S(2)}) collective-permute-start(bf16[18,64,256]{2,1,0:T(8,128)(2,1)S(1)} %get-tuple-element.50), channel_id=1, source_target_pairs={{0,3},{1,2},{2,1},{3,0},{4,7},{5,6},{6,5},{7,4},{8,11},{9,10},{10,... | collective-permute-start | bytes 1769480 | tf_op jit(solution)/shard_map/ppermute | solution.py:36
  4.4 22.5 %collective-permute-start.4 = (bf16[12,64,256]{2,1,0:T(8,128)(2,1)S(1)}, bf16[12,64,256]{2,1,0:T(8,128)(2,1)S(1)}, u32[]{:S(2)}, u32[]{:S(2)}) collective-permute-start(bf16[12,64,256]{2,1,0:T(8,128)(2,1)S(1)} %get-tuple-element.56), channel_id=1, source_target_pairs={{0,4},{1,5},{2,6},{3,7},{4,8},{5,9},{6,10},{7,11},{8,12},{9,13},{1... | collective-permute-start | bytes 1179656 | tf_op jit(solution)/shard_map/ppermute | solution.py:36
  6.1 20.8 %collective-permute-start.5 = (bf16[12,64,256]{2,1,0:T(8,128)(2,1)S(1)}, bf16[12,64,256]{2,1,0:T(8,128)(2,1)S(1)}, u32[]{:S(2)}, u32[]{:S(2)}) collective-permute-start(bf16[12,64,256]{2,1,0:T(8,128)(2,1)S(1)} %get-tuple-element.57), channel_id=1, source_target_pairs={{0,28},{1,29},{2,30},{3,31},{4,0},{5,1},{6,2},{7,3},{8,4},{9,5},{1... | collective-permute-start | bytes 1179656 | tf_op jit(solution)/shard_map/ppermute | solution.py:36
  9.2 14.6 %copy-start.1 = (s32[32,4,8]{0,2,1:T(8,128)S(1)}, s32[32,4,8]{0,2,1:T(8,128)}, u32[]{:S(2)}) copy-start(s32[32,4,8]{0,2,1:T(8,128)} %param.11) | copy-start | bytes 12292
  22.3 11.3 %collective-permute-start.3 = (bf16[6,64,256]{2,1,0:T(8,128)(2,1)S(1)}, bf16[6,64,256]{2,1,0:T(8,128)(2,1)S(1)}, u32[]{:S(2)}, u32[]{:S(2)}) collective-permute-start(bf16[6,64,256]{2,1,0:T(8,128)(2,1)S(1)} %get-tuple-element.85), channel_id=1, source_target_pairs={{0,28},{1,29},{2,30},{3,31},{4,0},{5,1},{6,2},{7,3},{8,4},{9,5},{1... | collective-permute-start | bytes 589832 | tf_op jit(solution)/shard_map/ppermute | solution.py:36
  23.8 9.8 %collective-permute-start.2 = (bf16[6,64,256]{2,1,0:T(8,128)(2,1)S(1)}, bf16[6,64,256]{2,1,0:T(8,128)(2,1)S(1)}, u32[]{:S(2)}, u32[]{:S(2)}) collective-permute-start(bf16[6,64,256]{2,1,0:T(8,128)(2,1)S(1)} %get-tuple-element.86), channel_id=1, source_target_pairs={{0,4},{1,5},{2,6},{3,7},{4,8},{5,9},{6,10},{7,11},{8,12},{9,13},{1... | collective-permute-start | bytes 589832 | tf_op jit(solution)/shard_map/ppermute | solution.py:36
  33.5 15.9 %copy-start.2 = (s32[1,72]{1,0:T(1,128)S(1)}, s32[1,72]{1,0:T(1,128)}, u32[]{:S(2)}) copy-start(s32[1,72]{1,0:T(1,128)} %owner_ref.5) | copy-start | bytes 868
  37.2 12.9 %collective-permute-start.6 = (bf16[16,32,128]{2,1,0:T(8,128)(2,1)S(1)}, bf16[16,32,128]{2,1,0:T(8,128)(2,1)S(1)}, u32[]{:S(2)}, u32[]{:S(2)}) collective-permute-start(bf16[16,32,128]{2,1,0:T(8,128)(2,1)S(1)} %get-tuple-element.73), channel_id=1, source_target_pairs={{0,4},{1,5},{2,6},{3,7},{4,8},{5,9},{6,10},{7,11},{8,12},{9,13},{1... | collective-permute-start | bytes 393224 | tf_op jit(solution)/shard_map/ppermute | solution.py:36
  37.3 12.8 %collective-permute-start.7 = (bf16[16,32,128]{2,1,0:T(8,128)(2,1)S(1)}, bf16[16,32,128]{2,1,0:T(8,128)(2,1)S(1)}, u32[]{:S(2)}, u32[]{:S(2)}) collective-permute-start(bf16[16,32,128]{2,1,0:T(8,128)(2,1)S(1)} %get-tuple-element.74), channel_id=1, source_target_pairs={{0,28},{1,29},{2,30},{3,31},{4,0},{5,1},{6,2},{7,3},{8,4},{9,5},{1... | collective-permute-start | bytes 393224 | tf_op jit(solution)/shard_map/ppermute | solution.py:36
  41.4 8.8 %collective-permute-start.9 = (bf16[8,32,128]{2,1,0:T(8,128)(2,1)S(1)}, bf16[8,32,128]{2,1,0:T(8,128)(2,1)S(1)}, u32[]{:S(2)}, u32[]{:S(2)}) collective-permute-start(bf16[8,32,128]{2,1,0:T(8,128)(2,1)S(1)} %get-tuple-element.79), channel_id=1, source_target_pairs={{0,3},{1,2},{2,1},{3,0},{4,7},{5,6},{6,5},{7,4},{8,11},{9,10},{10,... | collective-permute-start | bytes 196616 | tf_op jit(solution)/shard_map/ppermute | solution.py:36
  44.1 7.3 %collective-permute-start.10 = (bf16[8,32,128]{2,1,0:T(8,128)(2,1)S(1)}, bf16[8,32,128]{2,1,0:T(8,128)(2,1)S(1)}, u32[]{:S(2)}, u32[]{:S(2)}) collective-permute-start(bf16[8,32,128]{2,1,0:T(8,128)(2,1)S(1)} %get-tuple-element.80), channel_id=1, source_target_pairs={{0,7},{1,6},{2,5},{3,4},{4,11},{5,10},{6,9},{7,8},{8,15},{9,14},{1... | collective-permute-start | bytes 196616 | tf_op jit(solution)/shard_map/ppermute | solution.py:36
  44.1 7.3 %collective-permute-start.11 = (bf16[8,32,128]{2,1,0:T(8,128)(2,1)S(1)}, bf16[8,32,128]{2,1,0:T(8,128)(2,1)S(1)}, u32[]{:S(2)}, u32[]{:S(2)}) collective-permute-start(bf16[8,32,128]{2,1,0:T(8,128)(2,1)S(1)} %get-tuple-element.81), channel_id=1, source_target_pairs={{0,31},{1,30},{2,29},{3,28},{4,3},{5,2},{6,1},{7,0},{8,7},{9,6},{1... | collective-permute-start | bytes 196616 | tf_op jit(solution)/shard_map/ppermute | solution.py:36
  50.2 1.9 %collective-permute-start.8 = (bf16[24,32,128]{2,1,0:T(8,128)(2,1)S(1)}, bf16[24,32,128]{2,1,0:T(8,128)(2,1)S(1)}, u32[]{:S(2)}, u32[]{:S(2)}) collective-permute-start(bf16[24,32,128]{2,1,0:T(8,128)(2,1)S(1)} %pad_maximum_fusion.2), channel_id=1, source_target_pairs={{0,1},{1,0},{2,3},{3,2},{4,5},{5,4},{6,7},{7,6},{8,9},{9,8},{10,11... | collective-permute-start | bytes 589832 | tf_op jit(solution)/shard_map/ppermute | solution.py:36

commit v7 on v6

--- a/solution.py
+++ b/solution.py
@@ -8,7 +8,7 @@
 from jax.sharding import PartitionSpec as P
 
 OWN = 128
-GROUP = 4
+GROUP = 12
 STEP = 4
 SUMS = 4
 OWNER_SUMS = 1
@@ -38,6 +38,10 @@
 
 def resident(x):
     return pltpu.with_memory_space_constraint(x, pltpu.VMEM)
+
+
+def scalar(x):
+    return pltpu.with_memory_space_constraint(x, pltpu.SMEM)
 
 
 def exchange_rows(parts, nbr_local, local_work):
@@ -58,8 +62,9 @@
     up, down, far, up_far, down_far, pair = parts
     size = pair.shape[0]
     up, down, far = moved(up, 1, "own"), moved(down, -1, "own"), moved(far, 0, "far")
+    sums, small = first_sums()
+    up_far, down_far, small = lax.optimization_barrier((up_far, down_far, small))
     up_far, down_far = moved(up_far, 1, "far"), moved(down_far, -1, "far")
-    sums, small = first_sums()
     up, down, small = lax.optimization_barrier((up, down, small))
     pair = moved(jnp.concatenate([pair, up[size:], down[size:]]), 0, "pair")
     return sums, small, (up, down, far, up_far, down_far, pair)
@@ -226,8 +231,8 @@
             sums,
             pltpu.VMEM((capacity, kb, kb), jnp.bfloat16),
             pltpu.VMEM((elements, pieces * kc // 2, 2 * kb), jnp.bfloat16),
-            jax.ShapeDtypeStruct((len(STAGES) * capacity * (pieces + 2),), jnp.int32),
-            jax.ShapeDtypeStruct((elements + 2 * len(STAGES) + 1,), jnp.int32),
+            pltpu.SMEM((len(STAGES) * capacity * (pieces + 2),), jnp.int32),
+            pltpu.SMEM((elements + 2 * len(STAGES) + 1,), jnp.int32),
         ],
         in_specs=[SMEM, SMEM, VMEM, VMEM],
         out_specs=[VMEM] * 4 + [SMEM] * 2,
@@ -235,7 +240,7 @@
         compiler_params=PARAMS,
         cost_estimate=pl.CostEstimate(flops=5 * 10**9, bytes_accessed=10**7, transcendentals=0),
         name="local_part",
-    )(nbr_local.T, ap_slot.transpose(1, 2, 0), a_strips, p_strips)
+    )(scalar(nbr_local.T), scalar(ap_slot.transpose(1, 2, 0)), a_strips, p_strips)
 
 
 def finish_kernel(stage, info_ref, order_ref, tile_ref, ga_ref, pt_ref, *rest):
@@ -299,13 +304,17 @@
                         k * half : (k + 1) * half, u * kc2 : (u + 1) * kc2
                     ]
 
-    def step(i, carry):
-        for u in range(STEP):
-            one(order_ref[i * STEP + u])
+    def step(i, carry, size=STEP):
+        for u in range(size):
+            one(order_ref[i + u])
         return carry
 
-    begin = elements + stages + stage
-    lax.fori_loop(order_ref[begin], order_ref[begin + 1], step, 0)
+    begin, end = order_ref[elements + stages + stage], order_ref[elements + stages + stage + 1]
+    doubles = (end - begin) // 3
+    lax.fori_loop(0, doubles, lambda i, carry: step((begin + 3 * i) * STEP, carry, 3 * STEP), 0)
+
+    lax.fori_loop(begin + 3 * doubles, end, lambda i, carry: step(i * STEP, carry), 0)
+
     if stage < stages - 1:
         return
     capacity = sent[-1].shape[0]
@@ -346,9 +355,9 @@
         cost_estimate=pl.CostEstimate(flops=2 * 10**9, bytes_accessed=10**6, transcendentals=0),
         name=("first_part", "middle_part", "last_part")[stage],
     )(
-        info,
-        order,
-        tile_slot.transpose(1, 2, 0),
+        scalar(info),
+        scalar(order),
+        scalar(tile_slot.transpose(1, 2, 0)),
         resident(ga),
         resident(pt),
         *(resident(arrived[part]) for part in parts),
@@ -381,7 +390,7 @@
         compiler_params=PARAMS,
         cost_estimate=pl.CostEstimate(flops=10**9, bytes_accessed=10**6, transcendentals=0),
         name="first_sums",
-    )(owner_map, resident(own))
+    )(scalar(owner_map), resident(own))
     return sums, small
 
 
@@ -403,14 +412,15 @@
         compiler_params=PARAMS,
         cost_estimate=pl.CostEstimate(flops=2 * 10**10, bytes_accessed=10**6, transcendentals=0),
         name="more_sums",
-    )(owner_map, *map(resident, arrived), *sums)
-
-
-def owner_kernel(owner_ref, pair, *rest):
+    )(scalar(owner_map), *map(resident, arrived), *sums)
+
+
+def owner_kernel(owner_ref, *rest):
     sums, (out_ref, stage_ref, sems) = rest[-3 - OWNER_SUMS : -3], rest[-3:]
     capacity = owner_ref.shape[1] // 9
-    for at, cell in enumerate(arrived_tiles(pair_offset())[-1]):
-        add_tiles(owner_ref, sums, cell, pair, at, capacity)
+    for parcel, cells in zip(rest, arrived_tiles(pair_offset())[3:]):
+        for at, cell in enumerate(cells):
+            add_tiles(owner_ref, sums, cell, parcel, at, capacity)
     owned, half, kc2 = sums[0].shape
     left = lax.broadcasted_iota(jnp.int32, (8, kc2), 1) < kc2 // 2
     copies = []
@@ -435,22 +445,22 @@
         copy.wait()
 
 
-def owner_sums(owner_map, sums, small, pair):
+def owner_sums(owner_map, sums, small, parcels):
     _, half, kc2 = sums[0].shape
     out = jax.ShapeDtypeStruct((2 * half, OWN * kc2 // 2), jnp.float32)
     results = pl.pallas_call(
         owner_kernel,
         out_shape=[pltpu.VMEM(x.shape, x.dtype) for x in sums] + [out],
-        in_specs=[SMEM] + [VMEM] * (1 + len(sums)) + [HBM],
+        in_specs=[SMEM] + [VMEM] * (len(parcels) + len(sums)) + [HBM],
         out_specs=[VMEM] * len(sums) + [HBM],
         scratch_shapes=[
             pltpu.VMEM(out.shape, out.dtype),
             pltpu.SemaphoreType.DMA((2 * half // 8,)),
         ],
-        input_output_aliases={2 + i: i for i in range(len(sums))},
+        input_output_aliases={1 + len(parcels) + i: i for i in range(len(sums))},
         compiler_params=PARAMS,
         name="owner_sums",
-    )(owner_map, resident(pair), *sums, small)
+    )(scalar(owner_map), *map(resident, parcels), *sums, small)
     return results[-1]
 
 
@@ -468,11 +478,9 @@
     for stage in range(len(STAGES)):
         sums = finish(stage, info, order, tile_slot, ga, pt, arrived, sums, tiles_total)
     *parcels, own = sums[2 + SUMS :]
-    sums, small, (*parcels, pair) = exchange_tiles(
-        parcels, functools.partial(first_sums, owner_map, own)
-    )
-    sums = more_sums(owner_map, sums, parcels)
-    return owner_sums(owner_map, sums, small, pair)
+    sums, small, parcels = exchange_tiles(parcels, functools.partial(first_sums, owner_map, own))
+    sums = more_sums(owner_map, sums, parcels[:3])
+    return owner_sums(owner_map, sums, small, parcels[3:])
 
 
 def solution(mesh):

time: 54.4 us -> 53.4 us (0.982)
  Pallas kernels: 28.8 us -> 25.4 us
  waiting for transfers between devices: 3.75 us -> 5.63 us
    pallas_call x3, Pallas kernels: 10.7 us -> 7.86 us  [finish(): pl.pallas_call(functools.partial(finish_kernel, stage), out_shape=out_sha...]
    ppermute x12, waiting for transfers between devices: 3.75 us -> 5.63 us  [moved(): return lax.ppermute(x, ('dom', 'grp'), pairs)]
    pallas_call x1, Pallas kernels: 13 us -> 12.4 us  [local_part(): pl.pallas_call(functools.partial(local_kernel, ghosts, slots), out_shape=...]
  transfers between devices with their start and end apart: 12 -> 12, of which waited for: 2 -> 3; matrix products, arithmetic and copies ran while one was open for 0% -> 0% of each run, Pallas kernels for 39% -> 36%
where the time goes in v7:
time: 53.4 us; the launch traced here: 53.2 us
  Pallas kernels  25.4 us (48%)
  starting transfers between devices  21.9 us (41%)
  waiting for transfers between devices  5.63 us (11%)
    ppermute x12, starting transfers between devices, moved(): return lax.ppermute(x, ('dom', 'grp'), pairs)  21.9 us
    pallas_call x1, Pallas kernels, local_part(): pl.pallas_call(functools.partial(local_kernel, ghosts, slots), out_shape=...  12.4 us
    pallas_call x3, Pallas kernels, finish(): pl.pallas_call(functools.partial(finish_kernel, stage), out_shape=out_sha...  7.86 us
    ppermute x12, waiting for transfers between devices, moved(): return lax.ppermute(x, ('dom', 'grp'), pairs)  5.63 us
    pallas_call x1, Pallas kernels, owner_sums(): pl.pallas_call(owner_kernel, out_shape=[pltpu.VMEM(x.shape, x.dtype) for...  2.3 us
    pallas_call x1, Pallas kernels, pack(): pl.pallas_call(pack_kernel, out_shape=[pltpu.VMEM((len(cells) * ghosts,)...  1.5 us
  transfers between devices with their start and end apart: 12, of which 3 were waited for; matrix products, arithmetic and copies ran while one was open for 0% of the time, Pallas kernels for 36%

profile of v7, /device:TPU:1, one launch (start us, length us, event | category | flops | bytes accessed | tf_op | source)
XLA Modules:
  0.0 53.2 jit_solution(2432034322016091610)
XLA Ops:
  0.0 1.5 %pack.1 = (bf16[18,64,256]{2,1,0:T(8,128)(2,1)S(1)}, bf16[18,64,256]{2,1,0:T(8,128)(2,1)S(1)}, bf16[6,64,256]{2,1,0:T(8,128)(2,1)S(1)}, bf16[6,64,256]{2,1,0:T(8,128)(2,1)S(1)}) custom-call(s32[6,1,8]{2,1,0:T(1,128)} %bitcast.9, bf16[32,64,256]{2,1,0:T(8,128)(2,1)} %p_ref.1), custom_call_target="tpu_custom_call" | custom-call | tf_op jit(solution)/shard_map/pack/pallas_call | solution.py:121
  1.5 0.1 collective-permute-start
  1.6 2.6 %collective-permute-start.1 = (bf16[18,64,256]{2,1,0:T(8,128)(2,1)S(1)}, bf16[18,64,256]{2,1,0:T(8,128)(2,1)S(1)}, u32[]{:S(2)}, u32[]{:S(2)}) collective-permute-start(bf16[18,64,256]{2,1,0:T(8,128)(2,1)S(1)} %get-tuple-element.53), channel_id=1, source_target_pairs={{0,3},{1,2},{2,1},{3,0},{4,7},{5,6},{6,5},{7,4},{8,11},{9,10},{10,... | collective-permute-start | bytes 1769480 | tf_op jit(solution)/shard_map/ppermute | solution.py:36
  4.3 0.0 collective-permute-done.rest_0_
  4.3 0.1 pad_maximum_fusion
  4.4 1.7 %collective-permute-start.4 = (bf16[12,64,256]{2,1,0:T(8,128)(2,1)S(1)}, bf16[12,64,256]{2,1,0:T(8,128)(2,1)S(1)}, u32[]{:S(2)}, u32[]{:S(2)}) collective-permute-start(bf16[12,64,256]{2,1,0:T(8,128)(2,1)S(1)} %get-tuple-element.59), channel_id=1, source_target_pairs={{0,4},{1,5},{2,6},{3,7},{4,8},{5,9},{6,10},{7,11},{8,12},{9,13},{1... | collective-permute-start | bytes 1179656 | tf_op jit(solution)/shard_map/ppermute | solution.py:36
  6.1 3.1 %collective-permute-start.5 = (bf16[12,64,256]{2,1,0:T(8,128)(2,1)S(1)}, bf16[12,64,256]{2,1,0:T(8,128)(2,1)S(1)}, u32[]{:S(2)}, u32[]{:S(2)}) collective-permute-start(bf16[12,64,256]{2,1,0:T(8,128)(2,1)S(1)} %get-tuple-element.60), channel_id=1, source_target_pairs={{0,28},{1,29},{2,30},{3,31},{4,0},{5,1},{6,2},{7,3},{8,4},{9,5},{1... | collective-permute-start | bytes 1179656 | tf_op jit(solution)/shard_map/ppermute | solution.py:36
  9.2 0.0 copy-start.1
  9.3 12.4 %local_part.1 = (f32[288,64,128]{2,1,0:T(8,128)S(1)}, f32[288,64,128]{2,1,0:T(8,128)S(1)}, bf16[204,64,64]{2,1,0:T(8,128)(2,1)S(1)}, bf16[32,128,128]{2,1,0:T(8,...) custom-call(s32[7,32]{1,0:T(8,128)S(1)} %bitcast.8, s32[7,4,32]{2,1,0:T(4,128)S(1)} %bitcast.7, ...), custom_call_target="tpu_custom_call" | custom-call | flops 5000000000 | bytes 10000000 | tf_op jit(solution)/shard_map/local_part/pallas_call | solution.py:227
  21.7 0.0 collective-permute-done.1.rest_1_
  21.7 1.5 %collective-permute-start.3 = (bf16[6,64,256]{2,1,0:T(8,128)(2,1)S(1)}, bf16[6,64,256]{2,1,0:T(8,128)(2,1)S(1)}, u32[]{:S(2)}, u32[]{:S(2)}) collective-permute-start(bf16[6,64,256]{2,1,0:T(8,128)(2,1)S(1)} %get-tuple-element.91), channel_id=1, source_target_pairs={{0,28},{1,29},{2,30},{3,31},{4,0},{5,1},{6,2},{7,3},{8,4},{9,5},{1... | collective-permute-start | bytes 589832 | tf_op jit(solution)/shard_map/ppermute | solution.py:36
  23.2 0.0 collective-permute-start.2
  23.2 2.6 %first_part.1 = (f32[288,64,128]{2,1,0:T(8,128)S(1)}, f32[288,64,128]{2,1,0:T(8,128)S(1)}, f32[72,32,128]{2,1,0:T(8,128)S(1)}, f32[72,32,128]{2,1,0:T(8,128)S(1)...) custom-call(s32[3672]{0:T(1024)S(4)} %get-tuple-element.52.info_ref, ...), custom_call_target="tpu_custom_call", output_to_operand_aliasing={{0}: (7, {}), {1}: (8, {})} | custom-call | flops 2000000000 | bytes 1000000 | tf_op jit(solution)/shard_map/first_part/pallas_call | solution.py:345
  25.8 1.1 %collective-permute-done.4.rest_0_ = bf16[12,64,256]{2,1,0:T(8,128)(2,1)S(1)} collective-permute-done((bf16[12,64,256]{2,1,0:T(8,128)(2,1)S(1)}, bf16[12,64,256]{2,1,0:T(8,128)(2,1)S(1)}, u32[]{:S(2)}, u32[]{:S(2)}) %collective-permute-start.4) | collective-permute-done | bytes 393248 | tf_op jit(solution)/shard_map/ppermute | solution.py:36
  26.9 0.0 collective-permute-done.5.rest_1_
  26.9 2.7 %middle_part.1 = (f32[288,64,128]{2,1,0:T(8,128)S(1)}, f32[288,64,128]{2,1,0:T(8,128)S(1)}, f32[72,32,128]{2,1,0:T(8,128)S(1)}, f32[72,32,128]{2,1,0:T(8,128)S(1...) custom-call(s32[3672]{0:T(1024)S(4)} %get-tuple-element.52.info_ref,, ...), custom_call_target="tpu_custom_call", output_to_operand_aliasing={{0}: (7, {}), {1}: (8, {}), {2}: (9, {}), {3}: (10, {}), {4... | custom-call | flops 2000000000 | bytes 1000000 | tf_op jit(solution)/shard_map/middle_part/pallas_call | solution.py:345
  29.6 3.4 %collective-permute-done.3.rest_1_ = bf16[6,64,256]{2,1,0:T(8,128)(2,1)S(1)} collective-permute-done((bf16[6,64,256]{2,1,0:T(8,128)(2,1)S(1)}, bf16[6,64,256]{2,1,0:T(8,128)(2,1)S(1)}, u32[]{:S(2)}, u32[]{:S(2)}) %collective-permute-start.3) | collective-permute-done | bytes 196640 | tf_op jit(solution)/shard_map/ppermute | solution.py:36
  33.0 0.0 collective-permute-done.2.rest_0_
  33.0 2.6 %last_part.1 = (f32[288,64,128]{2,1,0:T(8,128)S(1)}, f32[288,64,128]{2,1,0:T(8,128)S(1)}, f32[72,32,128]{2,1,0:T(8,128)S(1)}, f32[72,32,128]{2,1,0:T(8,128)S(1)}...) custom-call(s32[3672]{0:T(1024)S(4)} %get-tuple-element.52.info_ref,, ...), custom_call_target="tpu_custom_call", output_to_operand_aliasing={{0}: (7, {}), {1}: (8, {}), {2}: (9, {}), {3}: (10, {}), {4... | custom-call | flops 2000000000 | bytes 1000000 | tf_op jit(solution)/shard_map/last_part/pallas_call | solution.py:345
  35.6 0.4 collective-permute-start.8
  36.0 3.8 %collective-permute-start.9 = (bf16[16,32,128]{2,1,0:T(8,128)(2,1)S(1)}, bf16[16,32,128]{2,1,0:T(8,128)(2,1)S(1)}, u32[]{:S(2)}, u32[]{:S(2)}) collective-permute-start(bf16[16,32,128]{2,1,0:T(8,128)(2,1)S(1)} %get-tuple-element.83), channel_id=1, source_target_pairs={{0,28},{1,29},{2,30},{3,31},{4,0},{5,1},{6,2},{7,3},{8,4},{9,5},{1... | collective-permute-start | bytes 393224 | tf_op jit(solution)/shard_map/ppermute | solution.py:36
  39.8 3.1 %collective-permute-start.11 = (bf16[8,32,128]{2,1,0:T(8,128)(2,1)S(1)}, bf16[8,32,128]{2,1,0:T(8,128)(2,1)S(1)}, u32[]{:S(2)}, u32[]{:S(2)}) collective-permute-start(bf16[8,32,128]{2,1,0:T(8,128)(2,1)S(1)} %get-tuple-element.87), channel_id=1, source_target_pairs={{0,3},{1,2},{2,1},{3,0},{4,7},{5,6},{6,5},{7,4},{8,11},{9,10},{10,... | collective-permute-start | bytes 196616 | tf_op jit(solution)/shard_map/ppermute | solution.py:36
  42.9 0.7 %first_sums.1 = (f32[128,32,128]{2,1,0:T(8,128)S(1)}, f32[8,128]{1,0:T(8,128)S(1)}) custom-call(s32[1,72]{1,0:T(1,128)S(1)} %copy-done.2, f32[8,32,128]{2,1,0:T(8,128)S(1)} %get-tuple-element.77.own), custom_call_target="tpu_custom_call" | custom-call | flops 1000000000 | bytes 1000000 | tf_op jit(solution)/shard_map/first_sums/pallas_call | solution.py:384
  43.6 0.1 collective-permute-start.6
  43.7 5.3 %collective-permute-start.7 = (bf16[8,32,128]{2,1,0:T(8,128)(2,1)S(1)}, bf16[8,32,128]{2,1,0:T(8,128)(2,1)S(1)}, u32[]{:S(2)}, u32[]{:S(2)}) collective-permute-start(bf16[8,32,128]{2,1,0:T(8,128)(2,1)S(1)} %get-tuple-element.80), channel_id=1, source_target_pairs={{0,31},{1,30},{2,29},{3,28},{4,3},{5,2},{6,1},{7,0},{8,7},{9,6},{1... | collective-permute-start | bytes 196616 | tf_op jit(solution)/shard_map/ppermute | solution.py:36
  49.0 0.0 collective-permute-done.8.rest_0_
  49.0 0.0 collective-permute-done.9.rest_1_
  49.0 0.1 collective-permute-start.10
  49.1 0.0 collective-permute-done.11.rest_2_
  49.1 0.7 %more_sums.1.rest_3_ = f32[128,32,128]{2,1,0:T(8,128)S(1)} custom-call(s32[1,72]{1,0:T(1,128)S(1)} %copy-done.2, bf16[16,32,128]{2,1,0:T(8,128)(2,1)S(1)} %collective-permute-done.8.rest_0_, bf16[16,32,128]{2,1,0:T(8,128)(2,1)S(1)} %collective-permute-done.9.rest_1_, ...), custom_call_target="tpu_custom_call", output_to_operand_aliasing={{}: (4, {})} | custom-call | flops 20000000000 | bytes 1000000 | tf_op jit(solution)/shard_map/more_sums/pallas_call | solution.py:406
  49.8 1.1 %collective-permute-done.6.rest_0_ = bf16[8,32,128]{2,1,0:T(8,128)(2,1)S(1)} collective-permute-done((bf16[8,32,128]{2,1,0:T(8,128)(2,1)S(1)}, bf16[8,32,128]{2,1,0:T(8,128)(2,1)S(1)}, u32[]{:S(2)}, u32[]{:S(2)}) %collective-permute-start.6) | collective-permute-done | bytes 65568 | tf_op jit(solution)/shard_map/ppermute | solution.py:36
  50.9 2.3 %owner_sums.1 = (f32[128,32,128]{2,1,0:T(8,128)S(1)}, f32[64,8192]{1,0:T(8,128)}) custom-call(s32[1,72]{1,0:T(1,128)S(1)} %copy-done.2, bf16[8,32,128]{2,1,0:T(8,128)(2,1)S(1)} %collective-permute-done.6.rest_0_, bf16[8,32,128]{2,1,0:T(8,128)(2,1)S(1)} %collective-permute-done.7.rest_1_, ...), custom_call_target="tpu_custom_call", output_to_operand_aliasing={{0}: (4, {})} | custom-call | tf_op jit(solution)/shard_map/owner_sums/pallas_call | solution.py:451
  (18 shorter events, 0.1 us)
Async XLA Ops:
  0.0 9.2 %copy-start = (bf16[32,64,256]{2,1,0:T(8,128)(2,1)S(1)}, bf16[32,64,256]{2,1,0:T(8,128)(2,1)}, u32[]{:S(2)}) copy-start(bf16[32,64,256]{2,1,0:T(8,128)(2,1)} %p_ref.1) | copy-start | bytes 3145732
  0.0 9.2 %copy-start.5 = (s32[32,7]{0,1:T(8,128)S(1)}, s32[32,7]{0,1:T(8,128)}, u32[]{:S(2)}) copy-start(s32[32,7]{0,1:T(8,128)} %param.9) | copy-start | bytes 2692
  0.0 9.2 %copy-start.4 = (s32[32,7,4]{0,2,1:T(4,128)S(1)}, s32[32,7,4]{0,2,1:T(4,128)}, u32[]{:S(2)}) copy-start(s32[32,7,4]{0,2,1:T(4,128)} %param.10) | copy-start | bytes 10756
  0.0 9.2 %copy-start.3 = (bf16[32,64,448]{2,1,0:T(8,128)(2,1)S(1)}, bf16[32,64,448]{2,1,0:T(8,128)(2,1)}, u32[]{:S(2)}) copy-start(bf16[32,64,448]{2,1,0:T(8,128)(2,1)} %a_ref.1) | copy-start | bytes 5505028
  1.5 2.7 %collective-permute-start = (bf16[18,64,256]{2,1,0:T(8,128)(2,1)S(1)}, bf16[18,64,256]{2,1,0:T(8,128)(2,1)S(1)}, u32[]{:S(2)}, u32[]{:S(2)}) collective-permute-start(bf16[18,64,256]{2,1,0:T(8,128)(2,1)S(1)} %get-tuple-element.49), channel_id=1, source_target_pairs={{0,1},{1,0},{2,3},{3,2},{4,5},{5,4},{6,7},{7,6},{8,9},{9,8},{10,11... | collective-permute-start | bytes 1769480 | tf_op jit(solution)/shard_map/ppermute | solution.py:36
  1.6 20.0 %collective-permute-start.1 = (bf16[18,64,256]{2,1,0:T(8,128)(2,1)S(1)}, bf16[18,64,256]{2,1,0:T(8,128)(2,1)S(1)}, u32[]{:S(2)}, u32[]{:S(2)}) collective-permute-start(bf16[18,64,256]{2,1,0:T(8,128)(2,1)S(1)} %get-tuple-element.53), channel_id=1, source_target_pairs={{0,3},{1,2},{2,1},{3,0},{4,7},{5,6},{6,5},{7,4},{8,11},{9,10},{10,... | collective-permute-start | bytes 1769480 | tf_op jit(solution)/shard_map/ppermute | solution.py:36
  4.4 22.5 %collective-permute-start.4 = (bf16[12,64,256]{2,1,0:T(8,128)(2,1)S(1)}, bf16[12,64,256]{2,1,0:T(8,128)(2,1)S(1)}, u32[]{:S(2)}, u32[]{:S(2)}) collective-permute-start(bf16[12,64,256]{2,1,0:T(8,128)(2,1)S(1)} %get-tuple-element.59), channel_id=1, source_target_pairs={{0,4},{1,5},{2,6},{3,7},{4,8},{5,9},{6,10},{7,11},{8,12},{9,13},{1... | collective-permute-start | bytes 1179656 | tf_op jit(solution)/shard_map/ppermute | solution.py:36
  6.1 20.8 %collective-permute-start.5 = (bf16[12,64,256]{2,1,0:T(8,128)(2,1)S(1)}, bf16[12,64,256]{2,1,0:T(8,128)(2,1)S(1)}, u32[]{:S(2)}, u32[]{:S(2)}) collective-permute-start(bf16[12,64,256]{2,1,0:T(8,128)(2,1)S(1)} %get-tuple-element.60), channel_id=1, source_target_pairs={{0,28},{1,29},{2,30},{3,31},{4,0},{5,1},{6,2},{7,3},{8,4},{9,5},{1... | collective-permute-start | bytes 1179656 | tf_op jit(solution)/shard_map/ppermute | solution.py:36
  9.2 14.0 %copy-start.1 = (s32[32,4,8]{0,2,1:T(8,128)S(1)}, s32[32,4,8]{0,2,1:T(8,128)}, u32[]{:S(2)}) copy-start(s32[32,4,8]{0,2,1:T(8,128)} %param.11) | copy-start | bytes 12292
  21.7 11.3 %collective-permute-start.3 = (bf16[6,64,256]{2,1,0:T(8,128)(2,1)S(1)}, bf16[6,64,256]{2,1,0:T(8,128)(2,1)S(1)}, u32[]{:S(2)}, u32[]{:S(2)}) collective-permute-start(bf16[6,64,256]{2,1,0:T(8,128)(2,1)S(1)} %get-tuple-element.91), channel_id=1, source_target_pairs={{0,28},{1,29},{2,30},{3,31},{4,0},{5,1},{6,2},{7,3},{8,4},{9,5},{1... | collective-permute-start | bytes 589832 | tf_op jit(solution)/shard_map/ppermute | solution.py:36
  23.2 9.8 %collective-permute-start.2 = (bf16[6,64,256]{2,1,0:T(8,128)(2,1)S(1)}, bf16[6,64,256]{2,1,0:T(8,128)(2,1)S(1)}, u32[]{:S(2)}, u32[]{:S(2)}) collective-permute-start(bf16[6,64,256]{2,1,0:T(8,128)(2,1)S(1)} %get-tuple-element.92), channel_id=1, source_target_pairs={{0,4},{1,5},{2,6},{3,7},{4,8},{5,9},{6,10},{7,11},{8,12},{9,13},{1... | collective-permute-start | bytes 589832 | tf_op jit(solution)/shard_map/ppermute | solution.py:36
  33.0 9.9 %copy-start.2 = (s32[1,72]{1,0:T(1,128)S(1)}, s32[1,72]{1,0:T(1,128)}, u32[]{:S(2)}) copy-start(s32[1,72]{1,0:T(1,128)} %owner_ref.5) | copy-start | bytes 868
  35.6 13.4 %collective-permute-start.8 = (bf16[16,32,128]{2,1,0:T(8,128)(2,1)S(1)}, bf16[16,32,128]{2,1,0:T(8,128)(2,1)S(1)}, u32[]{:S(2)}, u32[]{:S(2)}) collective-permute-start(bf16[16,32,128]{2,1,0:T(8,128)(2,1)S(1)} %get-tuple-element.82), channel_id=1, source_target_pairs={{0,4},{1,5},{2,6},{3,7},{4,8},{5,9},{6,10},{7,11},{8,12},{9,13},{1... | collective-permute-start | bytes 393224 | tf_op jit(solution)/shard_map/ppermute | solution.py:36
  36.0 13.0 %collective-permute-start.9 = (bf16[16,32,128]{2,1,0:T(8,128)(2,1)S(1)}, bf16[16,32,128]{2,1,0:T(8,128)(2,1)S(1)}, u32[]{:S(2)}, u32[]{:S(2)}) collective-permute-start(bf16[16,32,128]{2,1,0:T(8,128)(2,1)S(1)} %get-tuple-element.83), channel_id=1, source_target_pairs={{0,28},{1,29},{2,30},{3,31},{4,0},{5,1},{6,2},{7,3},{8,4},{9,5},{1... | collective-permute-start | bytes 393224 | tf_op jit(solution)/shard_map/ppermute | solution.py:36
  39.8 9.3 %collective-permute-start.11 = (bf16[8,32,128]{2,1,0:T(8,128)(2,1)S(1)}, bf16[8,32,128]{2,1,0:T(8,128)(2,1)S(1)}, u32[]{:S(2)}, u32[]{:S(2)}) collective-permute-start(bf16[8,32,128]{2,1,0:T(8,128)(2,1)S(1)} %get-tuple-element.87), channel_id=1, source_target_pairs={{0,3},{1,2},{2,1},{3,0},{4,7},{5,6},{6,5},{7,4},{8,11},{9,10},{10,... | collective-permute-start | bytes 196616 | tf_op jit(solution)/shard_map/ppermute | solution.py:36
  43.6 7.3 %collective-permute-start.6 = (bf16[8,32,128]{2,1,0:T(8,128)(2,1)S(1)}, bf16[8,32,128]{2,1,0:T(8,128)(2,1)S(1)}, u32[]{:S(2)}, u32[]{:S(2)}) collective-permute-start(bf16[8,32,128]{2,1,0:T(8,128)(2,1)S(1)} %get-tuple-element.79), channel_id=1, source_target_pairs={{0,7},{1,6},{2,5},{3,4},{4,11},{5,10},{6,9},{7,8},{8,15},{9,14},{1... | collective-permute-start | bytes 196616 | tf_op jit(solution)/shard_map/ppermute | solution.py:36
  43.7 7.3 %collective-permute-start.7 = (bf16[8,32,128]{2,1,0:T(8,128)(2,1)S(1)}, bf16[8,32,128]{2,1,0:T(8,128)(2,1)S(1)}, u32[]{:S(2)}, u32[]{:S(2)}) collective-permute-start(bf16[8,32,128]{2,1,0:T(8,128)(2,1)S(1)} %get-tuple-element.80), channel_id=1, source_target_pairs={{0,31},{1,30},{2,29},{3,28},{4,3},{5,2},{6,1},{7,0},{8,7},{9,6},{1... | collective-permute-start | bytes 196616 | tf_op jit(solution)/shard_map/ppermute | solution.py:36
  49.0 1.9 %collective-permute-start.10 = (bf16[24,32,128]{2,1,0:T(8,128)(2,1)S(1)}, bf16[24,32,128]{2,1,0:T(8,128)(2,1)S(1)}, u32[]{:S(2)}, u32[]{:S(2)}) collective-permute-start(bf16[24,32,128]{2,1,0:T(8,128)(2,1)S(1)} %pad_maximum_fusion.2), channel_id=1, source_target_pairs={{0,1},{1,0},{2,3},{3,2},{4,5},{5,4},{6,7},{7,6},{8,9},{9,8},{10,11... | collective-permute-start | bytes 589832 | tf_op jit(solution)/shard_map/ppermute | solution.py:36

commit v8 on v7

--- a/solution.py
+++ b/solution.py
@@ -18,20 +18,20 @@
 PARAMS = pltpu.CompilerParams(vmem_limit_bytes=8 * 1024 * 1024)
 
 
-def moved(x, a, along):
-    domains, groups = lax.axis_size("dom"), lax.axis_size("grp")
-
-    def target(j):
-        if along == "pair":
-            return j ^ 1
-        if along == "far":
-            return (j - 1 + 2 * (j % 2)) % groups
-        return j
-
+def partner(index, kind, count):
+    if kind == "pair":
+        return index ^ 1
+    if kind == "far":
+        return (index - 1 + 2 * (index % 2)) % count
+    return index
+
+
+def moved(x, row, column):
+    rows, columns = lax.axis_size("dom"), lax.axis_size("grp")
     pairs = [
-        (i * groups + j, (i + a) % domains * groups + target(j))
-        for i in range(domains)
-        for j in range(groups)
+        (i * columns + j, partner(i, row, rows) * columns + partner(j, column, columns))
+        for i in range(rows)
+        for j in range(columns)
     ]
     return lax.ppermute(x, ("dom", "grp"), pairs)
 
@@ -45,49 +45,54 @@
 
 
 def exchange_rows(parts, nbr_local, local_work):
-    pair, far, up, down = parts
-    size = up.shape[0]
-    pair, far = moved(pair, 0, "pair"), moved(far, 0, "far")
-    up, down = jnp.concatenate([up, pair[size : 2 * size]]), jnp.concatenate([down, pair[2 * size :]])
-    up, down, nbr_local = lax.optimization_barrier((up, down, nbr_local))
+    pair, far, near, away = parts
+    size = near.shape[0]
+    pair, far = moved(pair, "own", "pair"), moved(far, "own", "far")
+    near = jnp.concatenate([near, pair[size : 2 * size]])
+    away = jnp.concatenate([away, pair[2 * size :]])
+    near, away, nbr_local = lax.optimization_barrier((near, away, nbr_local))
     *results, small = local_work(nbr_local)
     far, small = lax.optimization_barrier((far, small))
-    up, down = moved(up, 1, "own"), moved(down, -1, "own")
-    up_far = moved(far[size : 2 * size], 1, "own")
-    down_far = moved(far[2 * size :], -1, "own")
-    return (*results, small), (pair, far, up, down, up_far, down_far)
+    near, away = moved(near, "pair", "own"), moved(away, "far", "own")
+    near_far = moved(far[size : 2 * size], "pair", "own")
+    away_far = moved(far[2 * size :], "far", "own")
+    return (*results, small), (pair, far, near, away, near_far, away_far)
 
 
 def exchange_tiles(parts, first_sums):
-    up, down, far, up_far, down_far, pair = parts
+    near, away, far, near_far, away_far, pair = parts
     size = pair.shape[0]
-    up, down, far = moved(up, 1, "own"), moved(down, -1, "own"), moved(far, 0, "far")
+    near, away = moved(near, "pair", "own"), moved(away, "far", "own")
+    far = moved(far, "own", "far")
     sums, small = first_sums()
-    up_far, down_far, small = lax.optimization_barrier((up_far, down_far, small))
-    up_far, down_far = moved(up_far, 1, "far"), moved(down_far, -1, "far")
-    up, down, small = lax.optimization_barrier((up, down, small))
-    pair = moved(jnp.concatenate([pair, up[size:], down[size:]]), 0, "pair")
-    return sums, small, (up, down, far, up_far, down_far, pair)
-
-
-def pair_offset():
-    return 1 - 2 * (lax.axis_index("grp") % 2)
-
-
-def sent_rows(offset):
-    return (4 + offset, 7 + offset, 1 + offset), (4 - offset, 7 - offset, 1 - offset), (7,), (1,)
-
-
-def arrived_rows(offset):
-    return (4 + offset,), (4 - offset,), (1, 1 + offset), (7, 7 + offset), (1 - offset,), (7 - offset,)
-
-
-def sent_tiles(offset):
-    return (7, 7 + offset), (1, 1 + offset), (4 - offset,), (7 - offset,), (1 - offset,), (4 + offset,)
-
-
-def arrived_tiles(offset):
-    return (1,), (7,), (4 - offset,), (1 - offset,), (7 - offset,), (4 + offset, 1 + offset, 7 + offset)
+    near_far, away_far = moved(near_far, "pair", "far"), moved(away_far, "far", "far")
+    near, away, small = lax.optimization_barrier((near, away, small))
+    pair = moved(jnp.concatenate([pair, near[size:], away[size:]]), "own", "pair")
+    return sums, small, (near, away, far, near_far, away_far, pair)
+
+
+def offsets():
+    return 3 - 6 * (lax.axis_index("dom") % 2), 1 - 2 * (lax.axis_index("grp") % 2)
+
+
+def sent_rows(row, column):
+    pair, far = 4 + column, 4 - column
+    return (pair, pair + row, pair - row), (far, far + row, far - row), (4 + row,), (4 - row,)
+
+
+def arrived_rows(row, column):
+    pair, far = 4 + column, 4 - column
+    return (pair,), (far,), (4 + row, pair + row), (4 - row, pair - row), (far + row,), (far - row,)
+
+
+def sent_tiles(row, column):
+    pair, far = 4 + column, 4 - column
+    return (4 + row, pair + row), (4 - row, pair - row), (far,), (far + row,), (far - row,), (pair,)
+
+
+def arrived_tiles(row, column):
+    pair, far = 4 + column, 4 - column
+    return (4 + row,), (4 - row,), (far,), (far + row,), (far - row,), (pair, pair + row, pair - row)
 
 
 STAGES = ((0, 1), (2, 3), (4, 5))
@@ -108,7 +113,7 @@
         copy.start()
     for copy in copies:
         copy.wait()
-    for out, cells in zip(outs, sent_rows(pair_offset())):
+    for out, cells in zip(outs, sent_rows(*offsets())):
         for at, cell in enumerate(cells):
             p = neighbour_of(cell)
             for g in range(ghosts):
@@ -122,7 +127,7 @@
         pack_kernel,
         out_shape=[
             pltpu.VMEM((len(cells) * ghosts,) + p_strips.shape[1:], p_strips.dtype)
-            for cells in sent_rows(1)
+            for cells in sent_rows(3, 1)
         ],
         in_specs=[HBM, HBM],
         out_specs=[VMEM] * 4,
@@ -147,7 +152,7 @@
     stride = slots + 1
     stages = len(STAGES)
     capacity = ga_ref.shape[0]
-    offset = pair_offset()
+    offset = offsets()[1]
     for cell in (0, 1, 2, 3, 5, 6, 7, 8):
         stage = jnp.int32(cell // 3 != 1)
         if cell // 3 != 1 and cell % 3 != 1:
@@ -256,9 +261,8 @@
     stride = slots + 1
     ghosts = ghost_ref.shape[0] // 8
     first = ga_ref.shape[0] * stage
-    offset = pair_offset()
     for part, ref in zip(parts, arrived):
-        for at, cell in enumerate(arrived_rows(offset)[part]):
+        for at, cell in enumerate(arrived_rows(*offsets())[part]):
             rows = pl.ds(neighbour_of(cell) * ghosts, ghosts)
             ghost_ref[rows] = ref[at * ghosts : (at + 1) * ghosts]
     if stage == 0:
@@ -323,7 +327,7 @@
         rows = pl.ds(cell * capacity, capacity)
         return functools.reduce(jnp.add, [ref[rows] for ref in tiles])
 
-    for out, cells in zip(sent, sent_tiles(offset)):
+    for out, cells in zip(sent, sent_tiles(*offsets())):
         for at, cell in enumerate(cells):
             out[at * capacity : (at + 1) * capacity] = total(cell).astype(out.dtype)
     sent[-1][...] = total(4)
@@ -338,7 +342,7 @@
     out_shape += [pltpu.VMEM((tiles_total, half, kc2), jnp.float32)] * SUMS
     if stage == len(STAGES) - 1:
         out_shape += [
-            pltpu.VMEM((len(cells) * capacity, half, kc2), jnp.bfloat16) for cells in sent_tiles(1)
+            pltpu.VMEM((len(cells) * capacity, half, kc2), jnp.bfloat16) for cells in sent_tiles(3, 1)
         ]
         out_shape += [pltpu.VMEM((capacity, half, kc2), jnp.float32)]
     inputs = 5 + len(parts)
@@ -397,7 +401,7 @@
 def more_sums_kernel(owner_ref, *rest):
     arrived, sums = rest[: -2 * OWNER_SUMS], rest[-OWNER_SUMS:]
     capacity = owner_ref.shape[1] // 9
-    for parcel, cells in zip(arrived, arrived_tiles(pair_offset())):
+    for parcel, cells in zip(arrived, arrived_tiles(*offsets())):
         add_tiles(owner_ref, sums, cells[0], parcel, 0, capacity)
 
 
@@ -418,7 +422,7 @@
 def owner_kernel(owner_ref, *rest):
     sums, (out_ref, stage_ref, sems) = rest[-3 - OWNER_SUMS : -3], rest[-3:]
     capacity = owner_ref.shape[1] // 9
-    for parcel, cells in zip(rest, arrived_tiles(pair_offset())[3:]):
+    for parcel, cells in zip(rest, arrived_tiles(*offsets())[3:]):
         for at, cell in enumerate(cells):
             add_tiles(owner_ref, sums, cell, parcel, at, capacity)
     owned, half, kc2 = sums[0].shape

time: 53.4 us -> 51.9 us (0.972)
  starting transfers between devices: 21.9 us -> 19.3 us
  waiting for transfers between devices: 5.63 us -> 6.26 us
    ppermute x12, starting transfers between devices: 21.9 us -> 19.3 us  [moved(): return lax.ppermute(x, ('dom', 'grp'), pairs)]
    ppermute x12, waiting for transfers between devices: 5.63 us -> 6.26 us  [moved(): return lax.ppermute(x, ('dom', 'grp'), pairs)]
  transfers between devices with their start and end apart: 12 -> 12, of which waited for: 3 -> 3; matrix products, arithmetic and copies ran while one was open for 0% -> 0% of each run, Pallas kernels for 36% -> 37%
where the time goes in v8:
time: 51.9 us; the launch traced here: 51.4 us
  Pallas kernels  25.5 us (49%)
  starting transfers between devices  19.3 us (37%)
  waiting for transfers between devices  6.26 us (12%)
    ppermute x12, starting transfers between devices, moved(): return lax.ppermute(x, ('dom', 'grp'), pairs)  19.3 us
    pallas_call x1, Pallas kernels, local_part(): pl.pallas_call(functools.partial(local_kernel, ghosts, slots), out_shape=...  12.4 us
    pallas_call x3, Pallas kernels, finish(): pl.pallas_call(functools.partial(finish_kernel, stage), out_shape=out_sha...  7.89 us
    ppermute x12, waiting for transfers between devices, moved(): return lax.ppermute(x, ('dom', 'grp'), pairs)  6.26 us
    pallas_call x1, Pallas kernels, owner_sums(): pl.pallas_call(owner_kernel, out_shape=[pltpu.VMEM(x.shape, x.dtype) for...  2.3 us
    pallas_call x1, Pallas kernels, pack(): pl.pallas_call(pack_kernel, out_shape=[pltpu.VMEM((len(cells) * ghosts,)...  1.5 us
  transfers between devices with their start and end apart: 12, of which 3 were waited for; matrix products, arithmetic and copies ran while one was open for 0% of the time, Pallas kernels for 37%

profile of v8, /device:TPU:1, one launch (start us, length us, event | category | flops | bytes accessed | tf_op | source)
XLA Modules:
  0.0 51.4 jit_solution(6843858448077472286)
XLA Ops:
  0.0 1.5 %pack.1 = (bf16[18,64,256]{2,1,0:T(8,128)(2,1)S(1)}, bf16[18,64,256]{2,1,0:T(8,128)(2,1)S(1)}, bf16[6,64,256]{2,1,0:T(8,128)(2,1)S(1)}, bf16[6,64,256]{2,1,0:T(8,128)(2,1)S(1)}) custom-call(s32[6,1,8]{2,1,0:T(1,128)} %bitcast.9, bf16[32,64,256]{2,1,0:T(8,128)(2,1)} %p_ref.1), custom_call_target="tpu_custom_call" | custom-call | tf_op jit(solution)/shard_map/pack/pallas_call | solution.py:126
  1.5 0.1 collective-permute-start
  1.6 2.6 %collective-permute-start.1 = (bf16[18,64,256]{2,1,0:T(8,128)(2,1)S(1)}, bf16[18,64,256]{2,1,0:T(8,128)(2,1)S(1)}, u32[]{:S(2)}, u32[]{:S(2)}) collective-permute-start(bf16[18,64,256]{2,1,0:T(8,128)(2,1)S(1)} %get-tuple-element.50), channel_id=1, source_target_pairs={{0,3},{1,2},{2,1},{3,0},{4,7},{5,6},{6,5},{7,4},{8,11},{9,10},{10,... | collective-permute-start | bytes 1769480 | tf_op jit(solution)/shard_map/ppermute | solution.py:36
  4.3 0.0 collective-permute-done.rest_0_
  4.3 0.1 pad_maximum_fusion
  4.4 1.8 %collective-permute-start.4 = (bf16[12,64,256]{2,1,0:T(8,128)(2,1)S(1)}, bf16[12,64,256]{2,1,0:T(8,128)(2,1)S(1)}, u32[]{:S(2)}, u32[]{:S(2)}) collective-permute-start(bf16[12,64,256]{2,1,0:T(8,128)(2,1)S(1)} %get-tuple-element.56), channel_id=1, source_target_pairs={{0,4},{1,5},{2,6},{3,7},{4,0},{5,1},{6,2},{7,3},{8,12},{9,13},{10,... | collective-permute-start | bytes 1179656 | tf_op jit(solution)/shard_map/ppermute | solution.py:36
  6.1 3.3 %collective-permute-start.5 = (bf16[12,64,256]{2,1,0:T(8,128)(2,1)S(1)}, bf16[12,64,256]{2,1,0:T(8,128)(2,1)S(1)}, u32[]{:S(2)}, u32[]{:S(2)}) collective-permute-start(bf16[12,64,256]{2,1,0:T(8,128)(2,1)S(1)} %get-tuple-element.57), channel_id=1, source_target_pairs={{0,28},{1,29},{2,30},{3,31},{4,8},{5,9},{6,10},{7,11},{8,4},{9,5},... | collective-permute-start | bytes 1179656 | tf_op jit(solution)/shard_map/ppermute | solution.py:36
  9.4 0.0 copy-start.1
  9.4 12.4 %local_part.1 = (f32[288,64,128]{2,1,0:T(8,128)S(1)}, f32[288,64,128]{2,1,0:T(8,128)S(1)}, bf16[204,64,64]{2,1,0:T(8,128)(2,1)S(1)}, bf16[32,128,128]{2,1,0:T(8,...) custom-call(s32[7,32]{1,0:T(8,128)S(1)} %bitcast.8, s32[7,4,32]{2,1,0:T(4,128)S(1)} %bitcast.7, ...), custom_call_target="tpu_custom_call" | custom-call | flops 5000000000 | bytes 10000000 | tf_op jit(solution)/shard_map/local_part/pallas_call | solution.py:232
  21.9 0.0 collective-permute-done.1.rest_1_
  21.9 0.9 %collective-permute-start.3 = (bf16[6,64,256]{2,1,0:T(8,128)(2,1)S(1)}, bf16[6,64,256]{2,1,0:T(8,128)(2,1)S(1)}, u32[]{:S(2)}, u32[]{:S(2)}) collective-permute-start(bf16[6,64,256]{2,1,0:T(8,128)(2,1)S(1)} %get-tuple-element.85), channel_id=1, source_target_pairs={{0,28},{1,29},{2,30},{3,31},{4,8},{5,9},{6,10},{7,11},{8,4},{9,5},... | collective-permute-start | bytes 589832 | tf_op jit(solution)/shard_map/ppermute | solution.py:36
  22.8 0.0 collective-permute-start.2
  22.8 2.0 %first_part.1 = (f32[288,64,128]{2,1,0:T(8,128)S(1)}, f32[288,64,128]{2,1,0:T(8,128)S(1)}, f32[72,32,128]{2,1,0:T(8,128)S(1)}, f32[72,32,128]{2,1,0:T(8,128)S(1)...) custom-call(s32[3672]{0:T(1024)S(4)} %get-tuple-element.49.info_ref, ...), custom_call_target="tpu_custom_call", output_to_operand_aliasing={{0}: (7, {}), {1}: (8, {})} | custom-call | flops 2000000000 | bytes 1000000 | tf_op jit(solution)/shard_map/first_part/pallas_call | solution.py:349
  24.9 0.0 collective-permute-done.4.rest_0_
  24.9 0.0 collective-permute-done.5.rest_1_
  24.9 3.3 %middle_part.1 = (f32[288,64,128]{2,1,0:T(8,128)S(1)}, f32[288,64,128]{2,1,0:T(8,128)S(1)}, f32[72,32,128]{2,1,0:T(8,128)S(1)}, f32[72,32,128]{2,1,0:T(8,128)S(1...) custom-call(s32[3672]{0:T(1024)S(4)} %get-tuple-element.49.info_ref,, ...), custom_call_target="tpu_custom_call", output_to_operand_aliasing={{0}: (7, {}), {1}: (8, {}), {2}: (9, {}), {3}: (10, {}), {4... | custom-call | flops 2000000000 | bytes 1000000 | tf_op jit(solution)/shard_map/middle_part/pallas_call | solution.py:349
  28.2 2.0 %collective-permute-done.3.rest_1_ = bf16[6,64,256]{2,1,0:T(8,128)(2,1)S(1)} collective-permute-done((bf16[6,64,256]{2,1,0:T(8,128)(2,1)S(1)}, bf16[6,64,256]{2,1,0:T(8,128)(2,1)S(1)}, u32[]{:S(2)}, u32[]{:S(2)}) %collective-permute-start.3) | collective-permute-done | bytes 196640 | tf_op jit(solution)/shard_map/ppermute | solution.py:36
  30.1 2.1 %collective-permute-done.2.rest_0_ = bf16[6,64,256]{2,1,0:T(8,128)(2,1)S(1)} collective-permute-done((bf16[6,64,256]{2,1,0:T(8,128)(2,1)S(1)}, bf16[6,64,256]{2,1,0:T(8,128)(2,1)S(1)}, u32[]{:S(2)}, u32[]{:S(2)}) %collective-permute-start.2) | collective-permute-done | bytes 196640 | tf_op jit(solution)/shard_map/ppermute | solution.py:36
  32.2 2.6 %last_part.1 = (f32[288,64,128]{2,1,0:T(8,128)S(1)}, f32[288,64,128]{2,1,0:T(8,128)S(1)}, f32[72,32,128]{2,1,0:T(8,128)S(1)}, f32[72,32,128]{2,1,0:T(8,128)S(1)}...) custom-call(s32[3672]{0:T(1024)S(4)} %get-tuple-element.49.info_ref,, ...), custom_call_target="tpu_custom_call", output_to_operand_aliasing={{0}: (7, {}), {1}: (8, {}), {2}: (9, {}), {3}: (10, {}), {4... | custom-call | flops 2000000000 | bytes 1000000 | tf_op jit(solution)/shard_map/last_part/pallas_call | solution.py:349
  34.8 1.2 %collective-permute-start.8 = (bf16[16,32,128]{2,1,0:T(8,128)(2,1)S(1)}, bf16[16,32,128]{2,1,0:T(8,128)(2,1)S(1)}, u32[]{:S(2)}, u32[]{:S(2)}) collective-permute-start(bf16[16,32,128]{2,1,0:T(8,128)(2,1)S(1)} %get-tuple-element.75), channel_id=1, source_target_pairs={{0,4},{1,5},{2,6},{3,7},{4,0},{5,1},{6,2},{7,3},{8,12},{9,13},{10,... | collective-permute-start | bytes 393224 | tf_op jit(solution)/shard_map/ppermute | solution.py:36
  36.0 3.6 %collective-permute-start.9 = (bf16[16,32,128]{2,1,0:T(8,128)(2,1)S(1)}, bf16[16,32,128]{2,1,0:T(8,128)(2,1)S(1)}, u32[]{:S(2)}, u32[]{:S(2)}) collective-permute-start(bf16[16,32,128]{2,1,0:T(8,128)(2,1)S(1)} %get-tuple-element.76), channel_id=1, source_target_pairs={{0,28},{1,29},{2,30},{3,31},{4,8},{5,9},{6,10},{7,11},{8,4},{9,5},... | collective-permute-start | bytes 393224 | tf_op jit(solution)/shard_map/ppermute | solution.py:36
  39.6 1.5 %collective-permute-start.6 = (bf16[8,32,128]{2,1,0:T(8,128)(2,1)S(1)}, bf16[8,32,128]{2,1,0:T(8,128)(2,1)S(1)}, u32[]{:S(2)}, u32[]{:S(2)}) collective-permute-start(bf16[8,32,128]{2,1,0:T(8,128)(2,1)S(1)} %get-tuple-element.72), channel_id=1, source_target_pairs={{0,7},{1,6},{2,5},{3,4},{4,3},{5,2},{6,1},{7,0},{8,15},{9,14},{10,... | collective-permute-start | bytes 196616 | tf_op jit(solution)/shard_map/ppermute | solution.py:36
  41.0 1.7 %collective-permute-start.7 = (bf16[8,32,128]{2,1,0:T(8,128)(2,1)S(1)}, bf16[8,32,128]{2,1,0:T(8,128)(2,1)S(1)}, u32[]{:S(2)}, u32[]{:S(2)}) collective-permute-start(bf16[8,32,128]{2,1,0:T(8,128)(2,1)S(1)} %get-tuple-element.73), channel_id=1, source_target_pairs={{0,31},{1,30},{2,29},{3,28},{4,11},{5,10},{6,9},{7,8},{8,7},{9,6},... | collective-permute-start | bytes 196616 | tf_op jit(solution)/shard_map/ppermute | solution.py:36
  42.7 1.9 %collective-permute-start.11 = (bf16[8,32,128]{2,1,0:T(8,128)(2,1)S(1)}, bf16[8,32,128]{2,1,0:T(8,128)(2,1)S(1)}, u32[]{:S(2)}, u32[]{:S(2)}) collective-permute-start(bf16[8,32,128]{2,1,0:T(8,128)(2,1)S(1)} %get-tuple-element.81), channel_id=1, source_target_pairs={{0,3},{1,2},{2,1},{3,0},{4,7},{5,6},{6,5},{7,4},{8,11},{9,10},{10,... | collective-permute-start | bytes 196616 | tf_op jit(solution)/shard_map/ppermute | solution.py:36
  44.6 0.7 %first_sums.1 = (f32[128,32,128]{2,1,0:T(8,128)S(1)}, f32[8,128]{1,0:T(8,128)S(1)}) custom-call(s32[1,72]{1,0:T(1,128)S(1)} %copy-done.2, f32[8,32,128]{2,1,0:T(8,128)S(1)} %get-tuple-element.77.own), custom_call_target="tpu_custom_call" | custom-call | flops 1000000000 | bytes 1000000 | tf_op jit(solution)/shard_map/first_sums/pallas_call | solution.py:388
  45.4 0.0 collective-permute-done.9.rest_1_
  45.4 0.7 %collective-permute-start.10 = (bf16[24,32,128]{2,1,0:T(8,128)(2,1)S(1)}, bf16[24,32,128]{2,1,0:T(8,128)(2,1)S(1)}, u32[]{:S(2)}, u32[]{:S(2)}) collective-permute-start(bf16[24,32,128]{2,1,0:T(8,128)(2,1)S(1)} %pad_maximum_fusion.2), channel_id=1, source_target_pairs={{0,1},{1,0},{2,3},{3,2},{4,5},{5,4},{6,7},{7,6},{8,9},{9,8},{10,11... | collective-permute-start | bytes 589832 | tf_op jit(solution)/shard_map/ppermute | solution.py:36
  46.2 2.2 %collective-permute-done.11.rest_2_ = bf16[8,32,128]{2,1,0:T(8,128)(2,1)S(1)} collective-permute-done((bf16[8,32,128]{2,1,0:T(8,128)(2,1)S(1)}, bf16[8,32,128]{2,1,0:T(8,128)(2,1)S(1)}, u32[]{:S(2)}, u32[]{:S(2)}) %collective-permute-start.11) | collective-permute-done | bytes 65568 | tf_op jit(solution)/shard_map/ppermute | solution.py:36
  48.4 0.7 %more_sums.1.rest_3_ = f32[128,32,128]{2,1,0:T(8,128)S(1)} custom-call(s32[1,72]{1,0:T(1,128)S(1)} %copy-done.2, bf16[16,32,128]{2,1,0:T(8,128)(2,1)S(1)} %collective-permute-done.8.rest_0_, bf16[16,32,128]{2,1,0:T(8,128)(2,1)S(1)} %collective-permute-done.9.rest_1_, ...), custom_call_target="tpu_custom_call", output_to_operand_aliasing={{}: (4, {})} | custom-call | flops 20000000000 | bytes 1000000 | tf_op jit(solution)/shard_map/more_sums/pallas_call | solution.py:410
  49.0 0.0 collective-permute-done.6.rest_0_
  49.1 0.0 collective-permute-done.10.rest_2_
  49.1 2.3 %owner_sums.1 = (f32[128,32,128]{2,1,0:T(8,128)S(1)}, f32[64,8192]{1,0:T(8,128)}) custom-call(s32[1,72]{1,0:T(1,128)S(1)} %copy-done.2, bf16[8,32,128]{2,1,0:T(8,128)(2,1)S(1)} %collective-permute-done.6.rest_0_, bf16[8,32,128]{2,1,0:T(8,128)(2,1)S(1)} %collective-permute-done.7.rest_1_, ...), custom_call_target="tpu_custom_call", output_to_operand_aliasing={{0}: (4, {})} | custom-call | tf_op jit(solution)/shard_map/owner_sums/pallas_call | solution.py:455
  (18 shorter events, 0.1 us)
Async XLA Ops:
  0.0 9.4 %copy-start = (bf16[32,64,256]{2,1,0:T(8,128)(2,1)S(1)}, bf16[32,64,256]{2,1,0:T(8,128)(2,1)}, u32[]{:S(2)}) copy-start(bf16[32,64,256]{2,1,0:T(8,128)(2,1)} %p_ref.1) | copy-start | bytes 3145732
  0.0 9.4 %copy-start.5 = (s32[32,7]{0,1:T(8,128)S(1)}, s32[32,7]{0,1:T(8,128)}, u32[]{:S(2)}) copy-start(s32[32,7]{0,1:T(8,128)} %param.9) | copy-start | bytes 2692
  0.0 9.4 %copy-start.4 = (s32[32,7,4]{0,2,1:T(4,128)S(1)}, s32[32,7,4]{0,2,1:T(4,128)}, u32[]{:S(2)}) copy-start(s32[32,7,4]{0,2,1:T(4,128)} %param.10) | copy-start | bytes 10756
  0.0 9.4 %copy-start.3 = (bf16[32,64,448]{2,1,0:T(8,128)(2,1)S(1)}, bf16[32,64,448]{2,1,0:T(8,128)(2,1)}, u32[]{:S(2)}) copy-start(bf16[32,64,448]{2,1,0:T(8,128)(2,1)} %a_ref.1) | copy-start | bytes 5505028
  1.5 2.7 %collective-permute-start = (bf16[18,64,256]{2,1,0:T(8,128)(2,1)S(1)}, bf16[18,64,256]{2,1,0:T(8,128)(2,1)S(1)}, u32[]{:S(2)}, u32[]{:S(2)}) collective-permute-start(bf16[18,64,256]{2,1,0:T(8,128)(2,1)S(1)} %get-tuple-element.46), channel_id=1, source_target_pairs={{0,1},{1,0},{2,3},{3,2},{4,5},{5,4},{6,7},{7,6},{8,9},{9,8},{10,11... | collective-permute-start | bytes 1769480 | tf_op jit(solution)/shard_map/ppermute | solution.py:36
  1.6 20.2 %collective-permute-start.1 = (bf16[18,64,256]{2,1,0:T(8,128)(2,1)S(1)}, bf16[18,64,256]{2,1,0:T(8,128)(2,1)S(1)}, u32[]{:S(2)}, u32[]{:S(2)}) collective-permute-start(bf16[18,64,256]{2,1,0:T(8,128)(2,1)S(1)} %get-tuple-element.50), channel_id=1, source_target_pairs={{0,3},{1,2},{2,1},{3,0},{4,7},{5,6},{6,5},{7,4},{8,11},{9,10},{10,... | collective-permute-start | bytes 1769480 | tf_op jit(solution)/shard_map/ppermute | solution.py:36
  4.4 20.5 %collective-permute-start.4 = (bf16[12,64,256]{2,1,0:T(8,128)(2,1)S(1)}, bf16[12,64,256]{2,1,0:T(8,128)(2,1)S(1)}, u32[]{:S(2)}, u32[]{:S(2)}) collective-permute-start(bf16[12,64,256]{2,1,0:T(8,128)(2,1)S(1)} %get-tuple-element.56), channel_id=1, source_target_pairs={{0,4},{1,5},{2,6},{3,7},{4,0},{5,1},{6,2},{7,3},{8,12},{9,13},{10,... | collective-permute-start | bytes 1179656 | tf_op jit(solution)/shard_map/ppermute | solution.py:36
  6.1 18.7 %collective-permute-start.5 = (bf16[12,64,256]{2,1,0:T(8,128)(2,1)S(1)}, bf16[12,64,256]{2,1,0:T(8,128)(2,1)S(1)}, u32[]{:S(2)}, u32[]{:S(2)}) collective-permute-start(bf16[12,64,256]{2,1,0:T(8,128)(2,1)S(1)} %get-tuple-element.57), channel_id=1, source_target_pairs={{0,28},{1,29},{2,30},{3,31},{4,8},{5,9},{6,10},{7,11},{8,4},{9,5},... | collective-permute-start | bytes 1179656 | tf_op jit(solution)/shard_map/ppermute | solution.py:36
  9.4 13.4 %copy-start.1 = (s32[32,4,8]{0,2,1:T(8,128)S(1)}, s32[32,4,8]{0,2,1:T(8,128)}, u32[]{:S(2)}) copy-start(s32[32,4,8]{0,2,1:T(8,128)} %param.11) | copy-start | bytes 12292
  21.9 8.2 %collective-permute-start.3 = (bf16[6,64,256]{2,1,0:T(8,128)(2,1)S(1)}, bf16[6,64,256]{2,1,0:T(8,128)(2,1)S(1)}, u32[]{:S(2)}, u32[]{:S(2)}) collective-permute-start(bf16[6,64,256]{2,1,0:T(8,128)(2,1)S(1)} %get-tuple-element.85), channel_id=1, source_target_pairs={{0,28},{1,29},{2,30},{3,31},{4,8},{5,9},{6,10},{7,11},{8,4},{9,5},... | collective-permute-start | bytes 589832 | tf_op jit(solution)/shard_map/ppermute | solution.py:36
  22.8 9.4 %collective-permute-start.2 = (bf16[6,64,256]{2,1,0:T(8,128)(2,1)S(1)}, bf16[6,64,256]{2,1,0:T(8,128)(2,1)S(1)}, u32[]{:S(2)}, u32[]{:S(2)}) collective-permute-start(bf16[6,64,256]{2,1,0:T(8,128)(2,1)S(1)} %get-tuple-element.86), channel_id=1, source_target_pairs={{0,4},{1,5},{2,6},{3,7},{4,0},{5,1},{6,2},{7,3},{8,12},{9,13},{10,... | collective-permute-start | bytes 589832 | tf_op jit(solution)/shard_map/ppermute | solution.py:36
  32.2 12.4 %copy-start.2 = (s32[1,72]{1,0:T(1,128)S(1)}, s32[1,72]{1,0:T(1,128)}, u32[]{:S(2)}) copy-start(s32[1,72]{1,0:T(1,128)} %owner_ref.5) | copy-start | bytes 868
  34.8 10.5 %collective-permute-start.8 = (bf16[16,32,128]{2,1,0:T(8,128)(2,1)S(1)}, bf16[16,32,128]{2,1,0:T(8,128)(2,1)S(1)}, u32[]{:S(2)}, u32[]{:S(2)}) collective-permute-start(bf16[16,32,128]{2,1,0:T(8,128)(2,1)S(1)} %get-tuple-element.75), channel_id=1, source_target_pairs={{0,4},{1,5},{2,6},{3,7},{4,0},{5,1},{6,2},{7,3},{8,12},{9,13},{10,... | collective-permute-start | bytes 393224 | tf_op jit(solution)/shard_map/ppermute | solution.py:36
  36.0 9.4 %collective-permute-start.9 = (bf16[16,32,128]{2,1,0:T(8,128)(2,1)S(1)}, bf16[16,32,128]{2,1,0:T(8,128)(2,1)S(1)}, u32[]{:S(2)}, u32[]{:S(2)}) collective-permute-start(bf16[16,32,128]{2,1,0:T(8,128)(2,1)S(1)} %get-tuple-element.76), channel_id=1, source_target_pairs={{0,28},{1,29},{2,30},{3,31},{4,8},{5,9},{6,10},{7,11},{8,4},{9,5},... | collective-permute-start | bytes 393224 | tf_op jit(solution)/shard_map/ppermute | solution.py:36
  39.6 9.5 %collective-permute-start.6 = (bf16[8,32,128]{2,1,0:T(8,128)(2,1)S(1)}, bf16[8,32,128]{2,1,0:T(8,128)(2,1)S(1)}, u32[]{:S(2)}, u32[]{:S(2)}) collective-permute-start(bf16[8,32,128]{2,1,0:T(8,128)(2,1)S(1)} %get-tuple-element.72), channel_id=1, source_target_pairs={{0,7},{1,6},{2,5},{3,4},{4,3},{5,2},{6,1},{7,0},{8,15},{9,14},{10,... | collective-permute-start | bytes 196616 | tf_op jit(solution)/shard_map/ppermute | solution.py:36
  41.0 8.0 %collective-permute-start.7 = (bf16[8,32,128]{2,1,0:T(8,128)(2,1)S(1)}, bf16[8,32,128]{2,1,0:T(8,128)(2,1)S(1)}, u32[]{:S(2)}, u32[]{:S(2)}) collective-permute-start(bf16[8,32,128]{2,1,0:T(8,128)(2,1)S(1)} %get-tuple-element.73), channel_id=1, source_target_pairs={{0,31},{1,30},{2,29},{3,28},{4,11},{5,10},{6,9},{7,8},{8,7},{9,6},... | collective-permute-start | bytes 196616 | tf_op jit(solution)/shard_map/ppermute | solution.py:36
  42.7 5.6 %collective-permute-start.11 = (bf16[8,32,128]{2,1,0:T(8,128)(2,1)S(1)}, bf16[8,32,128]{2,1,0:T(8,128)(2,1)S(1)}, u32[]{:S(2)}, u32[]{:S(2)}) collective-permute-start(bf16[8,32,128]{2,1,0:T(8,128)(2,1)S(1)} %get-tuple-element.81), channel_id=1, source_target_pairs={{0,3},{1,2},{2,1},{3,0},{4,7},{5,6},{6,5},{7,4},{8,11},{9,10},{10,... | collective-permute-start | bytes 196616 | tf_op jit(solution)/shard_map/ppermute | solution.py:36
  45.4 3.6 %collective-permute-start.10 = (bf16[24,32,128]{2,1,0:T(8,128)(2,1)S(1)}, bf16[24,32,128]{2,1,0:T(8,128)(2,1)S(1)}, u32[]{:S(2)}, u32[]{:S(2)}) collective-permute-start(bf16[24,32,128]{2,1,0:T(8,128)(2,1)S(1)} %pad_maximum_fusion.2), channel_id=1, source_target_pairs={{0,1},{1,0},{2,3},{3,2},{4,5},{5,4},{6,7},{7,6},{8,9},{9,8},{10,11... | collective-permute-start | bytes 589832 | tf_op jit(solution)/shard_map/ppermute | solution.py:36

commit v9 on v8

--- a/solution.py
+++ b/solution.py
@@ -102,9 +102,16 @@
     return cell - jnp.where(cell > 4, 1, 0)
 
 
-def pack_kernel(send_hbm, p_hbm, *rest):
-    outs, (send_ref, p_ref, sems) = rest[:-3], rest[-3:]
+def pack_rows(send_ref, p_ref, outs, parts):
     ghosts = send_ref.shape[0]
+    for out, cells in zip(outs, parts):
+        for at, cell in enumerate(cells):
+            p = neighbour_of(cell)
+            for g in range(ghosts):
+                out[at * ghosts + g] = p_ref[send_ref[g, 0, p]]
+
+
+def pack_first_kernel(send_hbm, p_hbm, pair_ref, p_ref, send_ref, sems):
     copies = [
         pltpu.make_async_copy(send_hbm, send_ref, sems.at[0]),
         pltpu.make_async_copy(p_hbm, p_ref, sems.at[1]),
@@ -113,35 +120,41 @@
         copy.start()
     for copy in copies:
         copy.wait()
-    for out, cells in zip(outs, sent_rows(*offsets())):
-        for at, cell in enumerate(cells):
-            p = neighbour_of(cell)
-            for g in range(ghosts):
-                out[at * ghosts + g] = p_ref[send_ref[g, 0, p]]
+    pack_rows(send_ref, p_ref, [pair_ref], sent_rows(*offsets())[:1])
+
+
+def pack_rest_kernel(send_ref, p_ref, *outs):
+    pack_rows(send_ref, p_ref, outs, sent_rows(*offsets())[1:])
 
 
 def pack(send_rows, p_strips):
     ghosts = send_rows.shape[2]
     send = send_rows.transpose(2, 0, 1)
-    return pl.pallas_call(
-        pack_kernel,
-        out_shape=[
-            pltpu.VMEM((len(cells) * ghosts,) + p_strips.shape[1:], p_strips.dtype)
-            for cells in sent_rows(3, 1)
-        ],
+    shapes = [
+        pltpu.VMEM((len(cells) * ghosts,) + p_strips.shape[1:], p_strips.dtype)
+        for cells in sent_rows(3, 1)
+    ]
+    pair, p_here, send = pl.pallas_call(
+        pack_first_kernel,
+        out_shape=[shapes[0], pltpu.VMEM(p_strips.shape, p_strips.dtype), pltpu.SMEM(send.shape, jnp.int32)],
         in_specs=[HBM, HBM],
-        out_specs=[VMEM] * 4,
-        scratch_shapes=[
-            pltpu.SMEM(send.shape, jnp.int32),
-            pltpu.VMEM(p_strips.shape, p_strips.dtype),
-            pltpu.SemaphoreType.DMA((2,)),
-        ],
-        compiler_params=PARAMS,
-        name="pack",
+        out_specs=[VMEM, VMEM, SMEM],
+        scratch_shapes=[pltpu.SemaphoreType.DMA((2,))],
+        compiler_params=PARAMS,
+        name="pack_first",
     )(
         pltpu.with_memory_space_constraint(send, pltpu.HBM),
         pltpu.with_memory_space_constraint(p_strips, pltpu.HBM),
     )
+    rest = pl.pallas_call(
+        pack_rest_kernel,
+        out_shape=shapes[1:],
+        in_specs=[SMEM, VMEM],
+        out_specs=[VMEM] * (len(shapes) - 1),
+        compiler_params=PARAMS,
+        name="pack_rest",
+    )(scalar(send), resident(p_here))
+    return (pair, *rest), p_here
 
 
 def local_kernel(ghosts, slots, nbr_ref, ap_ref, a_ref, p_ref, *rest):
@@ -245,7 +258,7 @@
         compiler_params=PARAMS,
         cost_estimate=pl.CostEstimate(flops=5 * 10**9, bytes_accessed=10**7, transcendentals=0),
         name="local_part",
-    )(scalar(nbr_local.T), scalar(ap_slot.transpose(1, 2, 0)), a_strips, p_strips)
+    )(scalar(nbr_local.T), scalar(ap_slot.transpose(1, 2, 0)), a_strips, resident(p_strips))
 
 
 def finish_kernel(stage, info_ref, order_ref, tile_ref, ga_ref, pt_ref, *rest):
@@ -422,7 +435,7 @@
 def owner_kernel(owner_ref, *rest):
     sums, (out_ref, stage_ref, sems) = rest[-3 - OWNER_SUMS : -3], rest[-3:]
     capacity = owner_ref.shape[1] // 9
-    for parcel, cells in zip(rest, arrived_tiles(*offsets())[3:]):
+    for parcel, cells in zip(rest, arrived_tiles(*offsets())[2:]):
         for at, cell in enumerate(cells):
             add_tiles(owner_ref, sums, cell, parcel, at, capacity)
     owned, half, kc2 = sums[0].shape
@@ -471,20 +484,18 @@
 def body(a_strips, p_strips, nbr_local, ap_slot, tile_slot, send_rows, owner_map):
     tiles_total = owner_map.shape[1]
 
+    outgoing, p_here = pack(send_rows, p_strips)
+
     def local_work(nbr):
-        return local_part(
-            a_strips, p_strips, nbr, ap_slot, tile_slot.shape[2], send_rows.shape[2]
-        )
-
-    (*sums, ga, pt, info, order), arrived = exchange_rows(
-        pack(send_rows, p_strips), nbr_local, local_work
-    )
+        return local_part(a_strips, p_here, nbr, ap_slot, tile_slot.shape[2], send_rows.shape[2])
+
+    (*sums, ga, pt, info, order), arrived = exchange_rows(outgoing, nbr_local, local_work)
     for stage in range(len(STAGES)):
         sums = finish(stage, info, order, tile_slot, ga, pt, arrived, sums, tiles_total)
     *parcels, own = sums[2 + SUMS :]
     sums, small, parcels = exchange_tiles(parcels, functools.partial(first_sums, owner_map, own))
-    sums = more_sums(owner_map, sums, parcels[:3])
-    return owner_sums(owner_map, sums, small, parcels[3:])
+    sums = more_sums(owner_map, sums, parcels[:2])
+    return owner_sums(owner_map, sums, small, parcels[2:])
 
 
 def solution(mesh):

time: 51.9 us -> 51.8 us (level)
  waiting for transfers between devices: 6.26 us -> 7.37 us
  starting transfers between devices: 19.3 us -> 18.5 us
    ppermute x12, waiting for transfers between devices: 6.26 us -> 7.37 us  [moved(): return lax.ppermute(x, ('dom', 'grp'), pairs)]
    ppermute x12, starting transfers between devices: 19.3 us -> 18.5 us  [moved(): return lax.ppermute(x, ('dom', 'grp'), pairs)]
    pallas_call x1 -> x2, Pallas kernels: 1.5 us -> 1.5 us  [the longest x1 1.43 us: pack(): pl.pallas_call(pack_first_kernel, out_shape=[shapes[0], pltpu.VMEM(p_stri...]
  transfers between devices with their start and end apart: 12 -> 12, of which waited for: 3 -> 4; matrix products, arithmetic and copies ran while one was open for 0% -> 0% of each run, Pallas kernels for 37% -> 37%
where the time goes in v9:
time: 51.8 us; the launch traced here: 51.7 us
  Pallas kernels  25.4 us (49%)
  starting transfers between devices  18.5 us (36%)
  waiting for transfers between devices  7.37 us (14%)
    ppermute x12, starting transfers between devices, moved(): return lax.ppermute(x, ('dom', 'grp'), pairs)  18.5 us
    pallas_call x1, Pallas kernels, local_part(): pl.pallas_call(functools.partial(local_kernel, ghosts, slots), out_shape=...  12.4 us
    pallas_call x3, Pallas kernels, finish(): pl.pallas_call(functools.partial(finish_kernel, stage), out_shape=out_sha...  7.9 us
    ppermute x12, waiting for transfers between devices, moved(): return lax.ppermute(x, ('dom', 'grp'), pairs)  7.37 us
    pallas_call x1, Pallas kernels, owner_sums(): pl.pallas_call(owner_kernel, out_shape=[pltpu.VMEM(x.shape, x.dtype) for...  2.35 us
    pallas_call x1, Pallas kernels, pack(): pl.pallas_call(pack_first_kernel, out_shape=[shapes[0], pltpu.VMEM(p_stri...  1.43 us
  transfers between devices with their start and end apart: 12, of which 4 were waited for; matrix products, arithmetic and copies ran while one was open for 0% of the time, Pallas kernels for 37%

profile of v9, /device:TPU:1, one launch (start us, length us, event | category | flops | bytes accessed | tf_op | source)
XLA Modules:
  0.0 51.7 jit_solution(7349737653997099699)
XLA Ops:
  0.0 1.4 %pack_first.1 = (bf16[18,64,256]{2,1,0:T(8,128)(2,1)S(1)}, bf16[32,64,256]{2,1,0:T(8,128)(2,1)S(1)}, s32[6,1,8]{2,1,0:T(1,128)S(4)}) custom-call(s32[6,1,8]{2,1,0:T(1,128)} %bitcast.9, bf16[32,64,256]{2,1,0:T(8,128)(2,1)} %p_hbm.1), custom_call_target="tpu_custom_call" | custom-call | tf_op jit(solution)/shard_map/pack_first/pallas_call | solution.py:137
  1.4 0.1 collective-permute-start
  1.6 0.1 pack_rest.1
  1.6 2.7 %collective-permute-start.1 = (bf16[18,64,256]{2,1,0:T(8,128)(2,1)S(1)}, bf16[18,64,256]{2,1,0:T(8,128)(2,1)S(1)}, u32[]{:S(2)}, u32[]{:S(2)}) collective-permute-start(bf16[18,64,256]{2,1,0:T(8,128)(2,1)S(1)} %get-tuple-element.54), channel_id=1, source_target_pairs={{0,3},{1,2},{2,1},{3,0},{4,7},{5,6},{6,5},{7,4},{8,11},{9,10},{10,... | collective-permute-start | bytes 1769480 | tf_op jit(solution)/shard_map/ppermute | solution.py:36
  4.3 0.0 collective-permute-done.rest_0_
  4.3 0.1 pad_maximum_fusion
  4.4 1.7 %collective-permute-start.4 = (bf16[12,64,256]{2,1,0:T(8,128)(2,1)S(1)}, bf16[12,64,256]{2,1,0:T(8,128)(2,1)S(1)}, u32[]{:S(2)}, u32[]{:S(2)}) collective-permute-start(bf16[12,64,256]{2,1,0:T(8,128)(2,1)S(1)} %get-tuple-element.60), channel_id=1, source_target_pairs={{0,4},{1,5},{2,6},{3,7},{4,0},{5,1},{6,2},{7,3},{8,12},{9,13},{10,... | collective-permute-start | bytes 1179656 | tf_op jit(solution)/shard_map/ppermute | solution.py:36
  6.1 3.3 %collective-permute-start.5 = (bf16[12,64,256]{2,1,0:T(8,128)(2,1)S(1)}, bf16[12,64,256]{2,1,0:T(8,128)(2,1)S(1)}, u32[]{:S(2)}, u32[]{:S(2)}) collective-permute-start(bf16[12,64,256]{2,1,0:T(8,128)(2,1)S(1)} %get-tuple-element.61), channel_id=1, source_target_pairs={{0,28},{1,29},{2,30},{3,31},{4,8},{5,9},{6,10},{7,11},{8,4},{9,5},... | collective-permute-start | bytes 1179656 | tf_op jit(solution)/shard_map/ppermute | solution.py:36
  9.3 12.4 %local_part.1 = (f32[288,64,128]{2,1,0:T(8,128)S(1)}, f32[288,64,128]{2,1,0:T(8,128)S(1)}, bf16[204,64,64]{2,1,0:T(8,128)(2,1)S(1)}, bf16[32,128,128]{2,1,0:T(8,...) custom-call(s32[7,32]{1,0:T(8,128)S(1)} %bitcast.8, s32[7,4,32]{2,1,0:T(4,128)S(1)} %bitcast.7, ...), custom_call_target="tpu_custom_call" | custom-call | flops 5000000000 | bytes 10000000 | tf_op jit(solution)/shard_map/local_part/pallas_call | solution.py:245
  21.7 0.0 collective-permute-done.1.rest_1_
  21.8 1.0 %collective-permute-start.3 = (bf16[6,64,256]{2,1,0:T(8,128)(2,1)S(1)}, bf16[6,64,256]{2,1,0:T(8,128)(2,1)S(1)}, u32[]{:S(2)}, u32[]{:S(2)}) collective-permute-start(bf16[6,64,256]{2,1,0:T(8,128)(2,1)S(1)} %get-tuple-element.89), channel_id=1, source_target_pairs={{0,28},{1,29},{2,30},{3,31},{4,8},{5,9},{6,10},{7,11},{8,4},{9,5},... | collective-permute-start | bytes 589832 | tf_op jit(solution)/shard_map/ppermute | solution.py:36
  22.8 0.0 collective-permute-start.2
  22.8 2.7 %first_part.1 = (f32[288,64,128]{2,1,0:T(8,128)S(1)}, f32[288,64,128]{2,1,0:T(8,128)S(1)}, f32[72,32,128]{2,1,0:T(8,128)S(1)}, f32[72,32,128]{2,1,0:T(8,128)S(1)...) custom-call(s32[3672]{0:T(1024)S(4)} %get-tuple-element.53.info_ref, ...), custom_call_target="tpu_custom_call", output_to_operand_aliasing={{0}: (7, {}), {1}: (8, {})} | custom-call | flops 2000000000 | bytes 1000000 | tf_op jit(solution)/shard_map/first_part/pallas_call | solution.py:362
  25.5 0.0 collective-permute-done.4.rest_0_
  25.5 0.0 collective-permute-done.5.rest_1_
  25.5 2.6 %middle_part.1 = (f32[288,64,128]{2,1,0:T(8,128)S(1)}, f32[288,64,128]{2,1,0:T(8,128)S(1)}, f32[72,32,128]{2,1,0:T(8,128)S(1)}, f32[72,32,128]{2,1,0:T(8,128)S(1...) custom-call(s32[3672]{0:T(1024)S(4)} %get-tuple-element.53.info_ref,, ...), custom_call_target="tpu_custom_call", output_to_operand_aliasing={{0}: (7, {}), {1}: (8, {}), {2}: (9, {}), {3}: (10, {}), {4... | custom-call | flops 2000000000 | bytes 1000000 | tf_op jit(solution)/shard_map/middle_part/pallas_call | solution.py:362
  28.1 1.9 %collective-permute-done.3.rest_1_ = bf16[6,64,256]{2,1,0:T(8,128)(2,1)S(1)} collective-permute-done((bf16[6,64,256]{2,1,0:T(8,128)(2,1)S(1)}, bf16[6,64,256]{2,1,0:T(8,128)(2,1)S(1)}, u32[]{:S(2)}, u32[]{:S(2)}) %collective-permute-start.3) | collective-permute-done | bytes 196640 | tf_op jit(solution)/shard_map/ppermute | solution.py:36
  30.0 2.2 %collective-permute-done.2.rest_0_ = bf16[6,64,256]{2,1,0:T(8,128)(2,1)S(1)} collective-permute-done((bf16[6,64,256]{2,1,0:T(8,128)(2,1)S(1)}, bf16[6,64,256]{2,1,0:T(8,128)(2,1)S(1)}, u32[]{:S(2)}, u32[]{:S(2)}) %collective-permute-start.2) | collective-permute-done | bytes 196640 | tf_op jit(solution)/shard_map/ppermute | solution.py:36
  32.2 2.6 %last_part.1 = (f32[288,64,128]{2,1,0:T(8,128)S(1)}, f32[288,64,128]{2,1,0:T(8,128)S(1)}, f32[72,32,128]{2,1,0:T(8,128)S(1)}, f32[72,32,128]{2,1,0:T(8,128)S(1)}...) custom-call(s32[3672]{0:T(1024)S(4)} %get-tuple-element.53.info_ref,, ...), custom_call_target="tpu_custom_call", output_to_operand_aliasing={{0}: (7, {}), {1}: (8, {}), {2}: (9, {}), {3}: (10, {}), {4... | custom-call | flops 2000000000 | bytes 1000000 | tf_op jit(solution)/shard_map/last_part/pallas_call | solution.py:362
  34.8 1.1 %collective-permute-start.9 = (bf16[16,32,128]{2,1,0:T(8,128)(2,1)S(1)}, bf16[16,32,128]{2,1,0:T(8,128)(2,1)S(1)}, u32[]{:S(2)}, u32[]{:S(2)}) collective-permute-start(bf16[16,32,128]{2,1,0:T(8,128)(2,1)S(1)} %get-tuple-element.80), channel_id=1, source_target_pairs={{0,4},{1,5},{2,6},{3,7},{4,0},{5,1},{6,2},{7,3},{8,12},{9,13},{10,... | collective-permute-start | bytes 393224 | tf_op jit(solution)/shard_map/ppermute | solution.py:36
  35.9 3.6 %collective-permute-start.10 = (bf16[16,32,128]{2,1,0:T(8,128)(2,1)S(1)}, bf16[16,32,128]{2,1,0:T(8,128)(2,1)S(1)}, u32[]{:S(2)}, u32[]{:S(2)}) collective-permute-start(bf16[16,32,128]{2,1,0:T(8,128)(2,1)S(1)} %get-tuple-element.81), channel_id=1, source_target_pairs={{0,28},{1,29},{2,30},{3,31},{4,8},{5,9},{6,10},{7,11},{8,4},{9,5},... | collective-permute-start | bytes 393224 | tf_op jit(solution)/shard_map/ppermute | solution.py:36
  39.5 2.5 %collective-permute-start.6 = (bf16[8,32,128]{2,1,0:T(8,128)(2,1)S(1)}, bf16[8,32,128]{2,1,0:T(8,128)(2,1)S(1)}, u32[]{:S(2)}, u32[]{:S(2)}) collective-permute-start(bf16[8,32,128]{2,1,0:T(8,128)(2,1)S(1)} %get-tuple-element.76), channel_id=1, source_target_pairs={{0,3},{1,2},{2,1},{3,0},{4,7},{5,6},{6,5},{7,4},{8,11},{9,10},{10,... | collective-permute-start | bytes 196616 | tf_op jit(solution)/shard_map/ppermute | solution.py:36
  42.0 0.0 collective-permute-start.7
  42.0 2.5 %collective-permute-start.8 = (bf16[8,32,128]{2,1,0:T(8,128)(2,1)S(1)}, bf16[8,32,128]{2,1,0:T(8,128)(2,1)S(1)}, u32[]{:S(2)}, u32[]{:S(2)}) collective-permute-start(bf16[8,32,128]{2,1,0:T(8,128)(2,1)S(1)} %get-tuple-element.78), channel_id=1, source_target_pairs={{0,31},{1,30},{2,29},{3,28},{4,11},{5,10},{6,9},{7,8},{8,7},{9,6},... | collective-permute-start | bytes 196616 | tf_op jit(solution)/shard_map/ppermute | solution.py:36
  44.6 0.7 %first_sums.1 = (f32[128,32,128]{2,1,0:T(8,128)S(1)}, f32[8,128]{1,0:T(8,128)S(1)}) custom-call(s32[1,72]{1,0:T(1,128)S(1)} %copy-done.1, f32[8,32,128]{2,1,0:T(8,128)S(1)} %get-tuple-element.82.own), custom_call_target="tpu_custom_call" | custom-call | flops 1000000000 | bytes 1000000 | tf_op jit(solution)/shard_map/first_sums/pallas_call | solution.py:401
  45.3 0.0 collective-permute-done.9.rest_0_
  45.3 0.0 collective-permute-done.10.rest_1_
  45.4 0.1 collective-permute-start.11
  45.4 0.6 %more_sums.1.rest_4_ = f32[128,32,128]{2,1,0:T(8,128)S(1)} custom-call(s32[1,72]{1,0:T(1,128)S(1)} %copy-done.1, bf16[16,32,128]{2,1,0:T(8,128)(2,1)S(1)} %collective-permute-done.9.rest_0_, bf16[16,32,128]{2,1,0:T(8,128)(2,1)S(1)} %collective-permute-done.10.rest_1_, f32[128,32,128]{2,1,0:T(8,128)S(1)} %get-tuple-element.86.rest_2_), custom_call_target="tpu_custom_call", output_to_operand_aliasing={{}: (3, {})} | custom-call | flops 20000000000 | bytes 1000000 | tf_op jit(solution)/shard_map/more_sums/pallas_call | solution.py:423
  46.1 0.6 %collective-permute-done.7.rest_1_ = bf16[8,32,128]{2,1,0:T(8,128)(2,1)S(1)} collective-permute-done((bf16[8,32,128]{2,1,0:T(8,128)(2,1)S(1)}, bf16[8,32,128]{2,1,0:T(8,128)(2,1)S(1)}, u32[]{:S(2)}, u32[]{:S(2)}) %collective-permute-start.7) | collective-permute-done | bytes 65568 | tf_op jit(solution)/shard_map/ppermute | solution.py:36
  46.6 2.7 %collective-permute-done.8.rest_2_ = bf16[8,32,128]{2,1,0:T(8,128)(2,1)S(1)} collective-permute-done((bf16[8,32,128]{2,1,0:T(8,128)(2,1)S(1)}, bf16[8,32,128]{2,1,0:T(8,128)(2,1)S(1)}, u32[]{:S(2)}, u32[]{:S(2)}) %collective-permute-start.8) | collective-permute-done | bytes 65568 | tf_op jit(solution)/shard_map/ppermute | solution.py:36
  49.3 2.3 %owner_sums.1 = (f32[128,32,128]{2,1,0:T(8,128)S(1)}, f32[64,8192]{1,0:T(8,128)}) custom-call(s32[1,72]{1,0:T(1,128)S(1)} %copy-done.1, bf16[8,32,128]{2,1,0:T(8,128)(2,1)S(1)} %collective-permute-done.6.rest_0_, bf16[8,32,128]{2,1,0:T(8,128)(2,1)S(1)} %collective-permute-done.7.rest_1_, ...), custom_call_target="tpu_custom_call", output_to_operand_aliasing={{0}: (5, {})} | custom-call | tf_op jit(solution)/shard_map/owner_sums/pallas_call | solution.py:468
  (17 shorter events, 0.1 us)
Async XLA Ops:
  0.0 9.3 %copy-start.2 = (bf16[32,64,448]{2,1,0:T(8,128)(2,1)S(1)}, bf16[32,64,448]{2,1,0:T(8,128)(2,1)}, u32[]{:S(2)}) copy-start(bf16[32,64,448]{2,1,0:T(8,128)(2,1)} %a_ref.1) | copy-start | bytes 5505028
  0.0 9.3 %copy-start.3 = (s32[32,7,4]{0,2,1:T(4,128)S(1)}, s32[32,7,4]{0,2,1:T(4,128)}, u32[]{:S(2)}) copy-start(s32[32,7,4]{0,2,1:T(4,128)} %param.10) | copy-start | bytes 10756
  0.0 9.3 %copy-start.4 = (s32[32,7]{0,1:T(8,128)S(1)}, s32[32,7]{0,1:T(8,128)}, u32[]{:S(2)}) copy-start(s32[32,7]{0,1:T(8,128)} %param.9) | copy-start | bytes 2692
  1.4 2.8 %collective-permute-start = (bf16[18,64,256]{2,1,0:T(8,128)(2,1)S(1)}, bf16[18,64,256]{2,1,0:T(8,128)(2,1)S(1)}, u32[]{:S(2)}, u32[]{:S(2)}) collective-permute-start(bf16[18,64,256]{2,1,0:T(8,128)(2,1)S(1)} %get-tuple-element.50), channel_id=1, source_target_pairs={{0,1},{1,0},{2,3},{3,2},{4,5},{5,4},{6,7},{7,6},{8,9},{9,8},{10,11... | collective-permute-start | bytes 1769480 | tf_op jit(solution)/shard_map/ppermute | solution.py:36
  1.6 20.1 %collective-permute-start.1 = (bf16[18,64,256]{2,1,0:T(8,128)(2,1)S(1)}, bf16[18,64,256]{2,1,0:T(8,128)(2,1)S(1)}, u32[]{:S(2)}, u32[]{:S(2)}) collective-permute-start(bf16[18,64,256]{2,1,0:T(8,128)(2,1)S(1)} %get-tuple-element.54), channel_id=1, source_target_pairs={{0,3},{1,2},{2,1},{3,0},{4,7},{5,6},{6,5},{7,4},{8,11},{9,10},{10,... | collective-permute-start | bytes 1769480 | tf_op jit(solution)/shard_map/ppermute | solution.py:36
  4.4 21.1 %collective-permute-start.4 = (bf16[12,64,256]{2,1,0:T(8,128)(2,1)S(1)}, bf16[12,64,256]{2,1,0:T(8,128)(2,1)S(1)}, u32[]{:S(2)}, u32[]{:S(2)}) collective-permute-start(bf16[12,64,256]{2,1,0:T(8,128)(2,1)S(1)} %get-tuple-element.60), channel_id=1, source_target_pairs={{0,4},{1,5},{2,6},{3,7},{4,0},{5,1},{6,2},{7,3},{8,12},{9,13},{10,... | collective-permute-start | bytes 1179656 | tf_op jit(solution)/shard_map/ppermute | solution.py:36
  6.1 19.4 %collective-permute-start.5 = (bf16[12,64,256]{2,1,0:T(8,128)(2,1)S(1)}, bf16[12,64,256]{2,1,0:T(8,128)(2,1)S(1)}, u32[]{:S(2)}, u32[]{:S(2)}) collective-permute-start(bf16[12,64,256]{2,1,0:T(8,128)(2,1)S(1)} %get-tuple-element.61), channel_id=1, source_target_pairs={{0,28},{1,29},{2,30},{3,31},{4,8},{5,9},{6,10},{7,11},{8,4},{9,5},... | collective-permute-start | bytes 1179656 | tf_op jit(solution)/shard_map/ppermute | solution.py:36
  9.3 13.5 %copy-start = (s32[32,4,8]{0,2,1:T(8,128)S(1)}, s32[32,4,8]{0,2,1:T(8,128)}, u32[]{:S(2)}) copy-start(s32[32,4,8]{0,2,1:T(8,128)} %param.11) | copy-start | bytes 12292
  21.8 8.2 %collective-permute-start.3 = (bf16[6,64,256]{2,1,0:T(8,128)(2,1)S(1)}, bf16[6,64,256]{2,1,0:T(8,128)(2,1)S(1)}, u32[]{:S(2)}, u32[]{:S(2)}) collective-permute-start(bf16[6,64,256]{2,1,0:T(8,128)(2,1)S(1)} %get-tuple-element.89), channel_id=1, source_target_pairs={{0,28},{1,29},{2,30},{3,31},{4,8},{5,9},{6,10},{7,11},{8,4},{9,5},... | collective-permute-start | bytes 589832 | tf_op jit(solution)/shard_map/ppermute | solution.py:36
  22.8 9.4 %collective-permute-start.2 = (bf16[6,64,256]{2,1,0:T(8,128)(2,1)S(1)}, bf16[6,64,256]{2,1,0:T(8,128)(2,1)S(1)}, u32[]{:S(2)}, u32[]{:S(2)}) collective-permute-start(bf16[6,64,256]{2,1,0:T(8,128)(2,1)S(1)} %get-tuple-element.90), channel_id=1, source_target_pairs={{0,4},{1,5},{2,6},{3,7},{4,0},{5,1},{6,2},{7,3},{8,12},{9,13},{10,... | collective-permute-start | bytes 589832 | tf_op jit(solution)/shard_map/ppermute | solution.py:36
  32.2 12.3 %copy-start.1 = (s32[1,72]{1,0:T(1,128)S(1)}, s32[1,72]{1,0:T(1,128)}, u32[]{:S(2)}) copy-start(s32[1,72]{1,0:T(1,128)} %owner_ref.5) | copy-start | bytes 868
  34.8 10.4 %collective-permute-start.9 = (bf16[16,32,128]{2,1,0:T(8,128)(2,1)S(1)}, bf16[16,32,128]{2,1,0:T(8,128)(2,1)S(1)}, u32[]{:S(2)}, u32[]{:S(2)}) collective-permute-start(bf16[16,32,128]{2,1,0:T(8,128)(2,1)S(1)} %get-tuple-element.80), channel_id=1, source_target_pairs={{0,4},{1,5},{2,6},{3,7},{4,0},{5,1},{6,2},{7,3},{8,12},{9,13},{10,... | collective-permute-start | bytes 393224 | tf_op jit(solution)/shard_map/ppermute | solution.py:36
  35.9 9.4 %collective-permute-start.10 = (bf16[16,32,128]{2,1,0:T(8,128)(2,1)S(1)}, bf16[16,32,128]{2,1,0:T(8,128)(2,1)S(1)}, u32[]{:S(2)}, u32[]{:S(2)}) collective-permute-start(bf16[16,32,128]{2,1,0:T(8,128)(2,1)S(1)} %get-tuple-element.81), channel_id=1, source_target_pairs={{0,28},{1,29},{2,30},{3,31},{4,8},{5,9},{6,10},{7,11},{8,4},{9,5},... | collective-permute-start | bytes 393224 | tf_op jit(solution)/shard_map/ppermute | solution.py:36
  39.5 6.5 %collective-permute-start.6 = (bf16[8,32,128]{2,1,0:T(8,128)(2,1)S(1)}, bf16[8,32,128]{2,1,0:T(8,128)(2,1)S(1)}, u32[]{:S(2)}, u32[]{:S(2)}) collective-permute-start(bf16[8,32,128]{2,1,0:T(8,128)(2,1)S(1)} %get-tuple-element.76), channel_id=1, source_target_pairs={{0,3},{1,2},{2,1},{3,0},{4,7},{5,6},{6,5},{7,4},{8,11},{9,10},{10,... | collective-permute-start | bytes 196616 | tf_op jit(solution)/shard_map/ppermute | solution.py:36
  42.0 4.6 %collective-permute-start.7 = (bf16[8,32,128]{2,1,0:T(8,128)(2,1)S(1)}, bf16[8,32,128]{2,1,0:T(8,128)(2,1)S(1)}, u32[]{:S(2)}, u32[]{:S(2)}) collective-permute-start(bf16[8,32,128]{2,1,0:T(8,128)(2,1)S(1)} %get-tuple-element.77), channel_id=1, source_target_pairs={{0,7},{1,6},{2,5},{3,4},{4,3},{5,2},{6,1},{7,0},{8,15},{9,14},{10,... | collective-permute-start | bytes 196616 | tf_op jit(solution)/shard_map/ppermute | solution.py:36
  42.0 7.3 %collective-permute-start.8 = (bf16[8,32,128]{2,1,0:T(8,128)(2,1)S(1)}, bf16[8,32,128]{2,1,0:T(8,128)(2,1)S(1)}, u32[]{:S(2)}, u32[]{:S(2)}) collective-permute-start(bf16[8,32,128]{2,1,0:T(8,128)(2,1)S(1)} %get-tuple-element.78), channel_id=1, source_target_pairs={{0,31},{1,30},{2,29},{3,28},{4,11},{5,10},{6,9},{7,8},{8,7},{9,6},... | collective-permute-start | bytes 196616 | tf_op jit(solution)/shard_map/ppermute | solution.py:36
  45.4 4.0 %collective-permute-start.11 = (bf16[24,32,128]{2,1,0:T(8,128)(2,1)S(1)}, bf16[24,32,128]{2,1,0:T(8,128)(2,1)S(1)}, u32[]{:S(2)}, u32[]{:S(2)}) collective-permute-start(bf16[24,32,128]{2,1,0:T(8,128)(2,1)S(1)} %pad_maximum_fusion.2), channel_id=1, source_target_pairs={{0,1},{1,0},{2,3},{3,2},{4,5},{5,4},{6,7},{7,6},{8,9},{9,8},{10,11... | collective-permute-start | bytes 589832 | tf_op jit(solution)/shard_map/ppermute | solution.py:36
